TPU v7x, 32 devices: a whole 2x2x4 slice. The times are simulated.
32 devices in a mesh: group: 2 (over y), row: 4 (over z), src: 4 (over x, core).
Axes of the slice: x: 2, y: 2, z: 4, core: 2. Of those that a mesh axis runs over, the one named last changes fastest.
Arguments:
- right_side: bfloat16 [5120, 1536], P(('group', 'row'), 'src'), parts along dimension 0, may hold values from -6 to 6
- factor: bfloat16 [5120, 2048], P(('group', 'row')), parts along dimension 0, may hold values from -0.1875 to 0.1875
- pattern: int32 [40, 16], P(('group', 'row')), parts along dimension 0, may hold values 0 or 1
- inverses: bfloat16 [8, 512, 512], P('group', 'src'), parts along dimension 0, may hold values from -4 to 4
- owners: int32 [8], P('group'), parts along dimension 0, may hold values from 0 to 3, as said below
- offsets: int32 [8], P('group'), parts along dimension 0, may hold values from 0 to 1
Outputs:
- solved: bfloat16 [4096, 1536], P(('group', 'row'), 'src'), parts along dimension 0
- updated: bfloat16 [5120, 1536], P(('group', 'row'), 'src'), parts along dimension 0
There are 2 independent parts, one for each index of `group`. A program takes and returns all parts, laid end to end along the dimension named above; each array names one. Nothing has to cross between parts.
Inputs may be any that keep to these rules, and one draw needn't show every extreme that they name: The 4 owners are different row indices, and the first and the last row index are always among them.
All inputs are finite; a program needn't handle non-finite values. No bound on the sum of `pattern` on one device may be relied on, other than what follows from the above.
Results may differ from a plain program's by a relative error of at most 0.0057.
Values may be sent and summed in bfloat16 or wider, within the bound.
No kernel may reach another device: no remote copies, remote signals or barrier semaphores. Data moves between devices by JAX's collectives and lax.ppermute only.
A program may use at most 64 MiB of HBM per device.

v0:
```python
import jax
import jax.numpy as jnp
from jax import lax
from jax.sharding import PartitionSpec as P

SN = 4
SNR = 512
BLK = 128


def spread(value, axis, source):
    kept = jnp.where(lax.axis_index(axis) == source, value, 0).astype(value.dtype)
    return lax.psum(kept, axis)


def build_masked(factor, pattern, ranking):
    row_blocks, col_blocks = pattern.shape
    tile_mask = jnp.broadcast_to(
        (pattern > 0)[:, None, :, None], (row_blocks, BLK, col_blocks, BLK)
    )
    tile_mask = tile_mask.reshape(row_blocks * BLK, col_blocks * BLK)
    column_node = jnp.arange(factor.shape[1], dtype=jnp.int32) // SNR
    retained = tile_mask & (ranking[:, None] > column_node[None, :])
    return jnp.where(retained, factor, jnp.zeros((), factor.dtype))


def share_solution(segment, whole_inverse, owners, supernode):
    solution = jnp.dot(
        whole_inverse[supernode], segment.astype(jnp.bfloat16), preferred_element_type=jnp.float32
    ).astype(jnp.bfloat16)
    return spread(solution, "row", owners[supernode])


def on_device(right_side, factor, pattern, inverses, owners, offsets):
    local_rows = right_side.shape[0]
    position = lax.axis_index("row")
    row_index = position * local_rows + jnp.arange(local_rows, dtype=jnp.int32)
    starts = owners * local_rows + offsets * BLK
    ranking = jnp.full((local_rows,), SN, jnp.int32)
    for supernode in range(SN):
        inside = (row_index >= starts[supernode]) & (row_index < starts[supernode] + SNR)
        ranking = jnp.where(inside, jnp.int32(supernode), ranking)
    masked = build_masked(factor, pattern, ranking)
    whole_inverse = lax.all_gather(inverses, "src", axis=1, tiled=True)
    local_starts = [
        jnp.clip(starts[supernode] - position * local_rows, 0, local_rows - SNR)
        for supernode in range(SN)
    ]
    running = right_side.astype(jnp.float32)
    pieces = []
    pending = None
    for supernode in range(SN):
        segment = lax.dynamic_slice_in_dim(running, local_starts[supernode], SNR, 0)
        if pending is not None:
            previous_cols = masked[:, (supernode - 1) * SNR : supernode * SNR]
            next_rows = lax.dynamic_slice_in_dim(previous_cols, local_starts[supernode], SNR, 0)
            segment = segment - jnp.dot(next_rows, pending, preferred_element_type=jnp.float32)
        solution = share_solution(segment, whole_inverse, owners, supernode)
        if pending is not None:
            running = running - jnp.dot(previous_cols, pending, preferred_element_type=jnp.float32)
        pieces.append(solution)
        pending = solution
    last_cols = masked[:, (SN - 1) * SNR : SN * SNR]
    running = running - jnp.dot(last_cols, pending, preferred_element_type=jnp.float32)
    solved_all = jnp.concatenate(pieces, 0)
    out_rows = solved_all.shape[0] // lax.axis_size("row")
    own_solved = lax.dynamic_slice_in_dim(solved_all, position * out_rows, out_rows, 0)
    return (own_solved, running.astype(jnp.bfloat16))


def solution(mesh):
    placed = (
        P(("group", "row"), "src"),
        P(("group", "row"), None),
        P(("group", "row"), None),
        P("group", "src", None),
        P("group"),
        P("group"),
    )
    return jax.shard_map(
        on_device,
        mesh=mesh,
        in_specs=placed,
        out_specs=(P(("group", "row"), "src"), P(("group", "row"), "src")),
        check_vma=False,
    )
```

profile of v0, /device:TPU:1, one launch (start us, length us, event | category | flops | bytes accessed | tf_op | source)
XLA Modules:
  0.0 204.8 jit_solution(1691476892449803731)
XLA Ops:
  7.2 0.0 all-gather.2.cloned.1.call-start
  7.2 0.7 all-gather.2.cloned.1.call-update
  7.9 0.0 all-reduce.5.cloned.1.call-start
  7.9 1.1 convert_element_type.39
  9.1 1.5 fusion.52
  11.3 0.7 multiply_add_fusion
  11.9 0.6 fusion.53
  15.7 2.5 %select_select_fusion = s32[640]{0:T(1024)S(1)} fusion(s32[]{:T(128)S(6)} %add.54, s32[]{:T(128)} %bitcast.1, s32[]{:T(128)S(6)} %add.53, s32[]{:T(128)} %bitcast.5, s32[]{:T(128)S(6)} %add.52, s32[]{:T(128)} %bitcast.7, s32[]{:T(128)S(6)} %add.51, s32[]{:T(128)} %bitcast.6, s32[]{:T(128)S(6)} %mul.18), kind=kLoop, calls=%fused_computation.51 | loop fusion | flops 10880 | bytes 2596 | tf_op jit(solution)/shard_map/jit(_where)/select_n | solution.py:42
  18.2 0.7 broadcast_compare_fusion
  18.9 15.8 %all-gather.2.cloned.1.call-done = bf16[4,512,512]{2,1,0:T(8,128)(2,1)} async-done(((bf16[4,128,512]{2,1,0:T(8,128)(2,1)}), bf16[4,512,512]{2,1,0:T(8,128)(2,1)}) %all-gather.2.cloned.1.call-update) | async-done | bytes 2097168 | tf_op jit(solution)/shard_map/all_gather | solution.py:44
  34.7 2.2 %fusion.6 = bf16[512,384]{0,1:T(8,128)(2,1)} fusion(bf16[4,512,512]{2,1,0:T(8,128)(2,1)} %all-gather.2.cloned.1.call-done, f32[640,384]{1,0:T(8,128)S(1)} %convert_element_type.39, s32[]{:T(128)S(6)} %min.13, pred[]{:T(512)S(6)} %eq.12), kind=kOutput, calls=%fused_computation.22 | convolution fusion | flops 201719808 | bytes 1310725 | tf_op jit(solution)/shard_map/dot_general | solution.py:28
  36.9 0.0 all-reduce.5.cloned.1.call-update
  37.0 0.0 all-reduce.7.cloned.1.call-start
  37.0 0.4 broadcast_in_dim.36
  37.4 3.5 %fusion = bf16[640,2048]{1,0:T(8,128)(2,1)S(1)} fusion(bf16[640,2048]{1,0:T(8,128)(2,1)} %param.7, pred[80,8,16,128]{3,2,1,0:T(8,128)(4,1)S(1)} %bitcast.41, s32[2048]{0:T(1024)S(1)} %add_select_fusion, s32[640]{0:T(1024)S(1)} %select_select_fusion), kind=kLoop, calls=%fused_computation.1 | loop fusion | flops 3932160 | bytes 6564352 | tf_op jit(solution)/shard_map/jit(_where)/select_n | solution.py:24
  42.2 1.4 fusion.51
  43.6 29.2 %all-reduce.5.cloned.1.call-done = bf16[512,384]{0,1:T(8,128)(2,1)} async-done(((bf16[512,384]{0,1:T(8,128)(2,1)}), bf16[512,384]{0,1:T(8,128)(2,1)}) %all-reduce.5.cloned.1.call-update) | async-done | bytes 393232 | tf_op jit(solution)/shard_map/psum | solution.py:13
  72.8 3.1 %fusion.8 = bf16[512,384]{0,1:T(8,128)(2,1)} fusion(bf16[512,384]{0,1:T(8,128)(2,1)} %all-reduce.5.cloned.1.call-done, f32[640,384]{1,0:T(8,128)} %copy-done.5, s32[]{:T(128)S(6)} %min.14, bf16[4,512,512]{2,1,0:T(8,128)(2,1)} %all-gather.2.cloned.1.call-done, bf16[640,512]{1,0:T(8,128)(2,1)} %get-tuple-element.6, pred[]{:T(512)S(6)} %eq.13), kind=kOutput, calls=%fused_computation.24 | convolution fusion | flops 403439616 | bytes 2622976 | tf_op jit(solution)/shard_map/dot_general | solution.py:28
  75.9 0.0 all-reduce.7.cloned.1.call-update
  75.9 0.0 all-reduce.9.cloned.1.call-start
  77.3 1.5 convolution_subtract_fusion.3
  78.8 34.0 %all-reduce.7.cloned.1.call-done = bf16[512,384]{0,1:T(8,128)(2,1)} async-done(((bf16[512,384]{0,1:T(8,128)(2,1)}), bf16[512,384]{0,1:T(8,128)(2,1)}) %all-reduce.7.cloned.1.call-update) | async-done | bytes 393232 | tf_op jit(solution)/shard_map/psum | solution.py:13
  112.8 3.1 %fusion.10 = bf16[512,384]{0,1:T(8,128)(2,1)} fusion(bf16[512,384]{0,1:T(8,128)(2,1)} %all-reduce.7.cloned.1.call-done, f32[640,384]{1,0:T(8,128)} %convolution_subtract_fusion.3, s32[]{:T(128)S(6)} %min.15, bf16[4,512,512]{2,1,0:T(8,128)(2,1)} %all-gather.2.cloned.1.call-done, bf16[640,512]{1,0:T(8,128)(2,1)} %get-tuple-element.5, pred[]{:T(512)S(6)} %eq.14), kind=kOutput, calls=%fused_computation.26 | convolution fusion | flops 403439616 | bytes 2622976 | tf_op jit(solution)/shard_map/dot_general | solution.py:28
  116.0 0.0 all-reduce.11.cloned.1.call-start
  117.2 2.7 %convolution_subtract_fusion.2 = f32[640,384]{1,0:T(8,128)} fusion(f32[640,384]{1,0:T(8,128)} %convolution_subtract_fusion.3, bf16[512,384]{0,1:T(8,128)(2,1)S(1)} %copy-done.3, bf16[640,2048]{1,0:T(8,128)(2,1)S(1)} %fusion), kind=kOutput, calls=%fused_computation.8 | convolution fusion | flops 251904000 | bytes 3014656 | tf_op jit(solution)/shard_map/dot_general | solution.py:60
  119.9 32.9 %all-reduce.9.cloned.1.call-done = bf16[512,384]{0,1:T(8,128)(2,1)} async-done(((bf16[512,384]{0,1:T(8,128)(2,1)}), bf16[512,384]{0,1:T(8,128)(2,1)}) %all-reduce.9.cloned.1.call-update) | async-done | bytes 393232 | tf_op jit(solution)/shard_map/psum | solution.py:13
  152.8 3.1 %fusion.12 = bf16[512,384]{0,1:T(8,128)(2,1)} fusion(bf16[512,384]{0,1:T(8,128)(2,1)} %all-reduce.9.cloned.1.call-done, f32[640,384]{1,0:T(8,128)} %convolution_subtract_fusion.2, s32[]{:T(128)S(6)} %min.16, bf16[4,512,512]{2,1,0:T(8,128)(2,1)} %all-gather.2.cloned.1.call-done, bf16[640,512]{1,0:T(8,128)(2,1)} %get-tuple-element.4, pred[]{:T(512)S(6)} %eq.15), kind=kOutput, calls=%fused_computation.28 | convolution fusion | flops 403439616 | bytes 2622976 | tf_op jit(solution)/shard_map/dot_general | solution.py:28
  156.0 2.7 %convolution_subtract_fusion.1 = f32[640,384]{1,0:T(8,128)} fusion(f32[640,384]{1,0:T(8,128)} %convolution_subtract_fusion.2, bf16[512,384]{0,1:T(8,128)(2,1)S(1)} %copy-done.4, bf16[640,2048]{1,0:T(8,128)(2,1)S(1)} %fusion), kind=kOutput, calls=%fused_computation.7 | convolution fusion | flops 251904000 | bytes 3014656 | tf_op jit(solution)/shard_map/dot_general | solution.py:60
  158.7 34.1 %all-reduce.11.cloned.1.call-done = bf16[512,384]{0,1:T(8,128)(2,1)} async-done(((bf16[512,384]{0,1:T(8,128)(2,1)}), bf16[512,384]{0,1:T(8,128)(2,1)}) %all-reduce.11.cloned.1.call-update) | async-done | bytes 393232 | tf_op jit(solution)/shard_map/psum | solution.py:13
  192.8 1.1 fusion.25
  193.9 1.9 copy.8
  195.8 2.5 %fusion.1 = bf16[640,384]{1,0:T(8,128)(2,1)} fusion(f32[640,384]{1,0:T(8,128)} %convolution_subtract_fusion.1, bf16[512,384]{0,1:T(8,128)(2,1)S(1)} %copy-done.2, bf16[640,2048]{1,0:T(8,128)(2,1)S(1)} %fusion), kind=kOutput, calls=%fused_computation.13 | convolution fusion | flops 252149760 | bytes 2523136 | tf_op jit(solution)/shard_map/dot_general | solution.py:64
  (15 shorter events, 0.1 us)
Async XLA Ops:
  7.2 27.6 %all-gather.2.cloned.1.call-start = ((), (), s32[]{:S(2)}) async-start(), calls=%async_computation | async-start | bytes 2621440 | tf_op jit(solution)/shard_map/all_gather | solution.py:44
  7.9 64.9 %all-reduce.5.cloned.1.call-start = ((), (), s32[]{:S(2)}) async-start(), calls=%async_computation.1 | async-start | bytes 786432 | tf_op jit(solution)/shard_map/psum | solution.py:13
  9.0 28.4 %copy-start.5 = (f32[640,384]{1,0:T(8,128)}, f32[640,384]{1,0:T(8,128)S(1)}, u32[]{:S(2)}) copy-start(f32[640,384]{1,0:T(8,128)S(1)} %convert_element_type.39) | copy-start | bytes 2949124
  37.0 75.8 %all-reduce.7.cloned.1.call-start = ((), (), s32[]{:S(2)}) async-start(), calls=%async_computation.2 | async-start | bytes 786432 | tf_op jit(solution)/shard_map/psum | solution.py:13
  43.6 33.7 %copy-start = (bf16[640,384]{1,0:T(8,128)(2,1)S(1)}, bf16[640,384]{1,0:T(8,128)(2,1)}, u32[]{:S(2)}) copy-start(bf16[640,384]{1,0:T(8,128)(2,1)} %param.6) | copy-start | bytes 1474564
  72.8 4.5 %copy-start.1 = (bf16[512,384]{0,1:T(8,128)(2,1)S(1)}, bf16[512,384]{0,1:T(8,128)(2,1)}, u32[]{:S(2)}) copy-start(bf16[512,384]{0,1:T(8,128)(2,1)} %all-reduce.5.cloned.1.call-done) | copy-start | bytes 1179652
  75.9 76.8 %all-reduce.9.cloned.1.call-start = ((), (), s32[]{:S(2)}) async-start(), calls=%async_computation.3 | async-start | bytes 786432 | tf_op jit(solution)/shard_map/psum | solution.py:13
  112.8 4.4 %copy-start.3 = (bf16[512,384]{0,1:T(8,128)(2,1)S(1)}, bf16[512,384]{0,1:T(8,128)(2,1)}, u32[]{:S(2)}) copy-start(bf16[512,384]{0,1:T(8,128)(2,1)} %all-reduce.7.cloned.1.call-done) | copy-start | bytes 1179652
  116.0 76.9 %all-reduce.11.cloned.1.call-start = ((), (), s32[]{:S(2)}) async-start(), calls=%async_computation.4 | async-start | bytes 786432 | tf_op jit(solution)/shard_map/psum | solution.py:13
  152.8 3.2 %copy-start.4 = (bf16[512,384]{0,1:T(8,128)(2,1)S(1)}, bf16[512,384]{0,1:T(8,128)(2,1)}, u32[]{:S(2)}) copy-start(bf16[512,384]{0,1:T(8,128)(2,1)} %all-reduce.9.cloned.1.call-done) | copy-start | bytes 1179652
  192.8 3.0 %copy-start.2 = (bf16[512,384]{0,1:T(8,128)(2,1)S(1)}, bf16[512,384]{0,1:T(8,128)(2,1)}, u32[]{:S(2)}) copy-start(bf16[512,384]{0,1:T(8,128)(2,1)} %all-reduce.11.cloned.1.call-done) | copy-start | bytes 1179652
Sparse Core Ops, SparseCore 0:
  9.6 25.1 all-gather.1
  37.6 35.0 all-reduce.4
  76.1 36.6 all-reduce.6
  116.1 36.6 all-reduce.8
  156.1 36.6 all-reduce.10
where the time goes:
time: 208 us; the launch traced here: 205 us
  waiting for transfers between devices  147 us (71%)
  between operations  21.4 us (10%)
  matrix products  21 us (10%)
  other arithmetic  9.5 us (5%)
  local copies, waits for them, and re-layouts  5.9 us (3%)
    psum x4, waiting for transfers between devices, spread(): return lax.psum(kept, axis)  130 us
    all_gather x1, waiting for transfers between devices, on_device(): whole_inverse = lax.all_gather(inverses, 'src', axis=1, tiled=True)  15.8 us
    dot_general x4, matrix products, share_solution(): jnp.dot(whole_inverse[supernode], segment.astype(jnp.bfloat16), preferred...  11.7 us
    dot_general x3, matrix products, on_device(): jnp.dot(previous_cols, pending, preferred_element_type=jnp.float32)  6.85 us
  transfers between devices with their start and end apart: 5, of which 5 were waited for; matrix products, arithmetic and copies ran while one was open for 9% of the time, Pallas kernels for 0%

commit v1 on v0

v1 whole, which is shorter than its diff:
```python
import functools

import jax
import jax.numpy as jnp
from jax import lax
from jax.experimental import pallas as pl
from jax.experimental.pallas import tpu as pltpu
from jax.sharding import PartitionSpec as P

SN = 4
SNR = 512
BLK = 128
LEFT = (SN - 1) * SNR
ANY = pl.BlockSpec(memory_space=pl.ANY)
SMEM = pl.BlockSpec(memory_space=pltpu.SMEM)
VMEM = pl.BlockSpec(memory_space=pltpu.VMEM)
PARAMS = pltpu.CompilerParams(vmem_limit_bytes=24 << 20)


def line_gather(value, n):
    slots = [value]
    for chain in range(2):
        got = value
        for hop in range(1, n):
            pairs = []
            for i in range(n):
                side = 1 if (i + chain + hop) % 2 else -1
                if 0 <= i + side * hop < n:
                    pairs.append((i + side, i))
            got = lax.ppermute(got, "row", pairs) if pairs else None
            slots.append(got)
    return slots


def slot_of(owner, n):
    position = lax.axis_index("row")
    away = owner - position
    hop = jnp.abs(away)
    side = jnp.where(away > 0, 1, 0)
    chain = lax.rem(position + hop + side, 2)
    return jnp.where(away == 0, 0, hop + chain * (n - 1))


def src_gather(value, n):
    pieces = {0: value}
    bit = n // 2
    while bit:
        for distance in list(pieces):
            pieces[distance ^ bit] = lax.ppermute(
                pieces[distance], "src", [(i, i ^ bit) for i in range(n)]
            )
        bit //= 2
    return [pieces[d] for d in range(n)]


def own_start(owners, offsets):
    position = lax.axis_index("row")
    start = jnp.int32(0)
    for node in range(SN):
        start = jnp.where(owners[node] == position, offsets[node] * BLK, start)
    return start


def start_matching(slots, wanted, place):
    for index, slot in enumerate(slots):
        if slot is not None:

            @pl.when(wanted == index)
            def _(slot=slot):
                place(slot).start()


def fill(held, refs):
    refs = iter(refs)
    return [next(refs) if there else None for there in held]


def stage_kernel(quarter, owners, offsets, pattern, factor, right, piece, segment, rows, sems):
    start = pl.multiple_of(own_start(owners, offsets), BLK)
    first = pl.multiple_of(start + lax.axis_index("src") * quarter, quarter)
    fetch = pltpu.make_async_copy(factor.at[pl.ds(first, quarter), pl.ds(0, LEFT)], rows, sems.at[0])
    move = pltpu.make_async_copy(right.at[pl.ds(start, SNR)], segment, sems.at[1])
    fetch.start()
    move.start()
    fetch.wait()
    tall = min(quarter, BLK)
    for top in range(0, quarter, tall):
        tile_row = (first + top) // BLK
        for col in range(0, LEFT, BLK):
            tile = rows[top : top + tall, col : col + BLK]
            kept = jnp.where(pattern[tile_row, col // BLK] > 0, tile, jnp.zeros_like(tile))
            piece[top : top + tall, col : col + BLK] = kept
    move.wait()


def stage(owners, offsets, pattern, factor, right, n_src):
    quarter = SNR // n_src
    shapes = [(quarter, LEFT), (SNR, right.shape[1])]
    return pl.pallas_call(
        functools.partial(stage_kernel, quarter),
        out_shape=[jax.ShapeDtypeStruct(shape, jnp.bfloat16) for shape in shapes],
        in_specs=[SMEM] * 3 + [ANY] * 2,
        out_specs=[VMEM, VMEM],
        scratch_shapes=[
            pltpu.VMEM((quarter, LEFT), jnp.bfloat16),
            pltpu.SemaphoreType.DMA((2,)),
        ],
        compiler_params=pltpu.CompilerParams(vmem_limit_bytes=56 << 20),
        name="stage",
    )(owners, offsets, pattern, factor, right)


def pick_kernel(n_row, held, owners, *refs):
    slots = fill(held, refs[: sum(held)])
    near, far, sems = refs[sum(held) :]

    def place(node, slot):
        width = node * SNR
        first = 0 if node == SN - 1 else node * (node - 1) // 2 * SNR
        target = (far if node == SN - 1 else near).at[:, pl.ds(first, width)]
        return pltpu.make_async_copy(slot.at[:, pl.ds(0, width)], target, sems.at[node])

    for node in range(1, SN):
        start_matching(slots, slot_of(owners[node], n_row), functools.partial(place, node))
    for node in range(1, SN):
        place(node, slots[0]).wait()


def pick(owners, slots, n_row):
    held = [slot is not None for slot in slots]
    quarter = slots[0].shape[0]
    shapes = [(quarter, (SN - 1) * (SN - 2) // 2 * SNR), (quarter, LEFT)]
    return pl.pallas_call(
        functools.partial(pick_kernel, n_row, held),
        out_shape=[jax.ShapeDtypeStruct(shape, jnp.bfloat16) for shape in shapes],
        in_specs=[SMEM] + [ANY] * sum(held),
        out_specs=[ANY] * 2,
        scratch_shapes=[pltpu.SemaphoreType.DMA((SN,))],
        compiler_params=PARAMS,
        name="pick",
    )(owners, *(slot for slot in slots if slot is not None))


def order_kernel(n_row, held, owners, *refs):
    slots = fill(held, refs[: sum(held)])
    segments, sems = refs[sum(held) :]

    def place(node, slot):
        return pltpu.make_async_copy(slot, segments.at[node], sems.at[node])

    for node in range(SN):
        start_matching(slots, slot_of(owners[node], n_row), functools.partial(place, node))
    for node in range(SN):
        place(node, slots[0]).wait()


def order(owners, slots, n_row):
    held = [slot is not None for slot in slots]
    return pl.pallas_call(
        functools.partial(order_kernel, n_row, held),
        out_shape=jax.ShapeDtypeStruct((SN,) + slots[0].shape, jnp.bfloat16),
        in_specs=[SMEM] + [ANY] * sum(held),
        out_specs=ANY,
        scratch_shapes=[pltpu.SemaphoreType.DMA((SN,))],
        compiler_params=PARAMS,
        cost_estimate=pl.CostEstimate(flops=24 * 10**9, bytes_accessed=0, transcendentals=0),
        name="order",
    )(owners, *(slot for slot in slots if slot is not None))


def join_kernel(*refs):
    *pieces, whole, sems = refs
    me, quarter = lax.axis_index("src"), SNR // len(pieces)
    copies = []
    for d, piece in enumerate(pieces):
        rows = pl.ds(pl.multiple_of(jnp.bitwise_xor(me, d) * quarter, quarter), quarter)
        place = whole.at[rows] if len(whole.shape) == 2 else whole.at[:, rows]
        copies.append(pltpu.make_async_copy(piece, place, sems.at[d]))
    for copy in copies:
        copy.start()
    for copy in copies:
        copy.wait()


def join(pieces):
    shape = pieces[0].shape[:-2] + (SNR, pieces[0].shape[-1])
    return pl.pallas_call(
        join_kernel,
        out_shape=jax.ShapeDtypeStruct(shape, jnp.bfloat16),
        in_specs=[ANY] * len(pieces),
        out_specs=ANY,
        scratch_shapes=[pltpu.SemaphoreType.DMA((len(pieces),))],
        compiler_params=PARAMS,
        name="join",
    )(*pieces)


def mask_kernel(owners, offsets, pattern, factor, masked):
    start = own_start(owners, offsets)
    position = lax.axis_index("row")
    owned = jnp.int32(SN)
    for node in range(SN):
        owned = jnp.where(owners[node] == position, node, owned)
    for top in range(0, factor.shape[0], BLK):
        rank = jnp.where((top >= start) & (top < start + SNR), owned, SN)
        for col in range(0, factor.shape[1], BLK):
            keep = (pattern[top // BLK, col // BLK] > 0) & (rank > col // SNR)
            tile = factor[top : top + BLK, col : col + BLK]
            masked[top : top + BLK, col : col + BLK] = jnp.where(keep, tile, jnp.zeros_like(tile))


def mask(owners, offsets, pattern, factor):
    return pl.pallas_call(
        mask_kernel,
        out_shape=jax.ShapeDtypeStruct(factor.shape, factor.dtype),
        in_specs=[SMEM] * 3 + [pl.BlockSpec(memory_space=pltpu.VMEM)],
        out_specs=pl.BlockSpec(memory_space=pltpu.VMEM),
        compiler_params=PARAMS,
        name="mask",
    )(owners, offsets, pattern, factor)


def solve_kernel(owners, inverse, segments, near, far, masked, right, solved, updated, xs, out, sems):
    position = lax.axis_index("row")
    for node in range(SN):
        segment = segments[node]
        if node:
            first = node * (node - 1) // 2 * SNR
            lower = far[...] if node == SN - 1 else near[:, first : first + node * SNR]
            update = jnp.dot(lower, xs[: node * SNR], preferred_element_type=jnp.float32)
            segment = (segment.astype(jnp.float32) - update).astype(jnp.bfloat16)
        x = jnp.dot(inverse[node], segment, preferred_element_type=jnp.float32)
        xs[node * SNR : (node + 1) * SNR] = x.astype(jnp.bfloat16)
    out_rows = solved.shape[0]
    solved_copy = pltpu.make_async_copy(
        xs.at[pl.ds(pl.multiple_of(position * out_rows, out_rows), out_rows)], solved, sems.at[0]
    )
    solved_copy.start()
    update = jnp.dot(masked[...], xs[...], preferred_element_type=jnp.float32)
    out[...] = (right[...].astype(jnp.float32) - update).astype(jnp.bfloat16)
    updated_copy = pltpu.make_async_copy(out, updated, sems.at[1])
    updated_copy.start()
    solved_copy.wait()
    updated_copy.wait()


def solve(owners, inverse, segments, near, far, masked, right, n_row):
    rows, columns = right.shape
    return pl.pallas_call(
        solve_kernel,
        out_shape=(
            jax.ShapeDtypeStruct((SN * SNR // n_row, columns), jnp.bfloat16),
            jax.ShapeDtypeStruct((rows, columns), jnp.bfloat16),
        ),
        in_specs=[SMEM] + [VMEM] * 6,
        out_specs=(ANY, ANY),
        scratch_shapes=[
            pltpu.VMEM((SN * SNR, columns), jnp.bfloat16),
            pltpu.VMEM((rows, columns), jnp.bfloat16),
            pltpu.SemaphoreType.DMA((2,)),
        ],
        compiler_params=PARAMS,
        name="solve",
    )(owners, inverse, segments, near, far, masked, right)


def on_device(right_side, factor, pattern, inverses, owners, offsets):
    n_row, n_src = lax.axis_size("row"), lax.axis_size("src")
    piece, segment = stage(owners, offsets, pattern, factor, right_side, n_src)
    pieces = line_gather(piece, n_row)
    inverse = join(src_gather(inverses, n_src))
    near, far = pick(owners, pieces, n_row)
    near, far, inverse = lax.optimization_barrier((near, far, inverse))
    near, far = join(src_gather(near, n_src)), join(src_gather(far, n_src))
    segments = order(owners, line_gather(segment, n_row), n_row)
    masked = mask(owners, offsets, pattern, factor)
    return solve(owners, inverse, segments, near, far, masked, right_side, n_row)


def solution(mesh):
    placed = (
        P(("group", "row"), "src"),
        P(("group", "row"), None),
        P(("group", "row"), None),
        P("group", "src", None),
        P("group"),
        P("group"),
    )
    return jax.shard_map(
        on_device,
        mesh=mesh,
        in_specs=placed,
        out_specs=(P(("group", "row"), "src"), P(("group", "row"), "src")),
        check_vma=False,
    )
```

time: 208 us -> 76.1 us (0.37); the launches traced: 205 us -> 75.8 us
  waiting for transfers between devices: 147 us -> 25.6 us
  starting transfers between devices: 0.2 us -> 34.6 us
  matrix products: 21 us -> 0 us
  between operations: 21.4 us -> 0.9 us
  Pallas kernels: 0 us -> 14.4 us
  other arithmetic: 9.5 us -> 0 us
  local copies, waits for them, and re-layouts: 5.9 us -> 0.23 us
    psum x4 -> x0, waiting for transfers between devices: 130 us -> none  [spread(): return lax.psum(kept, axis)]
    ppermute x0 -> x19, starting transfers between devices: none -> 34.6 us  [the longest x9 20.7 us: src_gather(): lax.ppermute(pieces[distance], 'src', [(i, i ^ bit) for i in range(n)])]
    ppermute x0 -> x19, waiting for transfers between devices: none -> 25.6 us  [the longest x10 25.6 us: line_gather(): got = lax.ppermute(got, 'row', pairs) if pairs else None]
    dot_general x8 -> x0, matrix products: 21 us -> none  [the longest x4 11.7 us: share_solution(): jnp.dot(whole_inverse[supernode], segment.astype(jnp.bfloat16), preferred...]
    all_gather x1 -> x0, waiting for transfers between devices: 15.8 us -> none  [on_device(): whole_inverse = lax.all_gather(inverses, 'src', axis=1, tiled=True)]
    pallas_call x0 -> x8, Pallas kernels: none -> 14.4 us  [the longest x1 5.92 us: solve(): pl.pallas_call(solve_kernel, out_shape=(jax.ShapeDtypeStruct((SN * SNR //...]
    select_n x3 -> x0, other arithmetic: 5.98 us -> none  [the longest x1 3.47 us: build_masked(): return jnp.where(retained, factor, jnp.zeros((), factor.dtype))]
    slice x3 -> x0, local copies, waits for them, and re-layouts: 3.56 us -> none  [the longest x1 1.54 us: share_solution(): return spread(solution, 'row', owners[supernode])]
  transfers between devices with their start and end apart: 5 -> 19, of which waited for: 5 -> 4; matrix products, arithmetic and copies ran while one was open for 9% -> 0% of each run, Pallas kernels for 0% -> 6%
where the time goes in v1:
time: 76.1 us; the launch traced here: 75.8 us
  starting transfers between devices  34.6 us (45%)
  waiting for transfers between devices  25.6 us (34%)
  Pallas kernels  14.4 us (19%)
  between operations  0.9 us (1%)
    ppermute x10, waiting for transfers between devices, line_gather(): got = lax.ppermute(got, 'row', pairs) if pairs else None  25.6 us
    ppermute x9, starting transfers between devices, src_gather(): lax.ppermute(pieces[distance], 'src', [(i, i ^ bit) for i in range(n)])  20.7 us
    ppermute x10, starting transfers between devices, line_gather(): got = lax.ppermute(got, 'row', pairs) if pairs else None  13.9 us
    pallas_call x1, Pallas kernels, solve(): pl.pallas_call(solve_kernel, out_shape=(jax.ShapeDtypeStruct((SN * SNR //...  5.92 us
    pallas_call x1, Pallas kernels, stage(): pl.pallas_call(functools.partial(stage_kernel, quarter), out_shape=[jax.S...  2.89 us
    pallas_call x3, Pallas kernels, join(): pl.pallas_call(join_kernel, out_shape=jax.ShapeDtypeStruct(shape, jnp.bfl...  1.81 us
  transfers between devices with their start and end apart: 19, of which 4 were waited for; matrix products, arithmetic and copies ran while one was open for 0% of the time, Pallas kernels for 6%

profile of v1, /device:TPU:1, one launch (start us, length us, event | category | flops | bytes accessed | tf_op | source)
XLA Modules:
  0.0 75.8 jit_solution(199750033139196680)
XLA Ops:
  0.6 2.9 %stage.1 = (bf16[128,1536]{1,0:T(8,128)(2,1)}, bf16[512,384]{1,0:T(8,128)(2,1)}) custom-call(s32[4]{0:T(128)} %owners.9, s32[4]{0:T(128)} %offsets.3, s32[5,16]{1,0:T(8,128)} %pattern.3, bf16[640,2048]{1,0:T(8,128)(2,1)} %factor.3, bf16[640,384]{1,0:T(8,128)(2,1)} %right.3), custom_call_target="tpu_custom_call" | custom-call | tf_op jit(solution)/shard_map/stage/pallas_call | solution.py:99
  3.5 2.2 %collective-permute-start = (bf16[128,1536]{1,0:T(8,128)(2,1)}, bf16[128,1536]{1,0:T(8,128)(2,1)S(1)}, u32[]{:S(2)}, u32[]{:S(2)}) collective-permute-start(bf16[128,1536]{1,0:T(8,128)(2,1)} %get-tuple-element.9.refs_0_), channel_id=1, source_target_pairs={{4,0},{0,4},{12,8},{8,12},{5,1},{1,5},{13,9},{9,13},{6,2},{2,6},{1... | collective-permute-start | bytes 1179656 | tf_op jit(solution)/shard_map/ppermute | solution.py:30
  5.7 1.2 %collective-permute-start.6 = (bf16[4,128,512]{2,1,0:T(8,128)(2,1)S(1)}, bf16[4,128,512]{2,1,0:T(8,128)(2,1)S(1)}, u32[]{:S(2)}, u32[]{:S(2)}) collective-permute-start(bf16[4,128,512]{2,1,0:T(8,128)(2,1)S(1)} %copy-done.2), channel_id=1, source_target_pairs={{0,2},{1,3},{2,0},{3,1},{4,6},{5,7},{6,4},{7,5},{8,10},{9,11},{10,... | collective-permute-start | bytes 1572872 | tf_op jit(solution)/shard_map/ppermute | solution.py:49
  6.9 0.7 collective-permute-start.3
  7.7 0.8 %collective-permute-start.11 = (bf16[512,384]{1,0:T(8,128)(2,1)}, bf16[512,384]{1,0:T(8,128)(2,1)S(1)}, u32[]{:S(2)}, u32[]{:S(2)}) collective-permute-start(bf16[512,384]{1,0:T(8,128)(2,1)} %get-tuple-element.13.refs_0_), channel_id=1, source_target_pairs={{8,4},{4,8},{9,5},{5,9},{10,6},{6,10},{11,7},{7,11},{24,20},{20,24... | collective-permute-start | bytes 1179656 | tf_op jit(solution)/shard_map/ppermute | solution.py:30
  8.5 6.3 %collective-permute-done.refs_1_ = bf16[128,1536]{1,0:T(8,128)(2,1)S(1)} collective-permute-done((bf16[128,1536]{1,0:T(8,128)(2,1)}, bf16[128,1536]{1,0:T(8,128)(2,1)S(1)}, u32[]{:S(2)}, u32[]{:S(2)}) %collective-permute-start) | collective-permute-done | bytes 393248 | tf_op jit(solution)/shard_map/ppermute | solution.py:30
  14.8 0.7 collective-permute-start.1
  15.5 3.7 %collective-permute-start.8 = (bf16[512,384]{1,0:T(8,128)(2,1)}, bf16[512,384]{1,0:T(8,128)(2,1)S(1)}, u32[]{:S(2)}, u32[]{:S(2)}) collective-permute-start(bf16[512,384]{1,0:T(8,128)(2,1)} %get-tuple-element.13.refs_0_), channel_id=1, source_target_pairs={{4,0},{0,4},{12,8},{8,12},{5,1},{1,5},{13,9},{9,13},{6,2},{2,6},{1... | collective-permute-start | bytes 1179656 | tf_op jit(solution)/shard_map/ppermute | solution.py:30
  19.2 2.1 %collective-permute-start.5 = (bf16[4,128,512]{2,1,0:T(8,128)(2,1)S(1)}, bf16[4,128,512]{2,1,0:T(8,128)(2,1)S(1)}, u32[]{:S(2)}, u32[]{:S(2)}) collective-permute-start(bf16[4,128,512]{2,1,0:T(8,128)(2,1)S(1)} %copy-done.2), channel_id=1, source_target_pairs={{0,1},{1,0},{2,3},{3,2},{4,5},{5,4},{6,7},{7,6},{8,9},{9,8},{10,11... | collective-permute-start | bytes 1572872 | tf_op jit(solution)/shard_map/ppermute | solution.py:49
  21.3 0.1 collective-permute-start.7
  21.4 1.3 %collective-permute-start.4 = (bf16[128,1536]{1,0:T(8,128)(2,1)S(1)}, bf16[128,1536]{1,0:T(8,128)(2,1)S(1)}, u32[]{:S(2)}, u32[]{:S(2)}) collective-permute-start(bf16[128,1536]{1,0:T(8,128)(2,1)S(1)} %collective-permute-done.3.refs_4_), channel_id=1, source_target_pairs={{4,0},{8,12},{5,1},{9,13},{6,2},{10,14},{7,3},{11,15},{20,16},{24,... | collective-permute-start | bytes 1179656 | tf_op jit(solution)/shard_map/ppermute | solution.py:30
  22.7 1.3 %collective-permute-start.2 = (bf16[128,1536]{1,0:T(8,128)(2,1)S(1)}, bf16[128,1536]{1,0:T(8,128)(2,1)S(1)}, u32[]{:S(2)}, u32[]{:S(2)}) collective-permute-start(bf16[128,1536]{1,0:T(8,128)(2,1)S(1)} %collective-permute-done.1.refs_2_), channel_id=1, source_target_pairs={{4,0},{8,12},{5,1},{9,13},{6,2},{10,14},{7,3},{11,15},{20,16},{24,... | collective-permute-start | bytes 1179656 | tf_op jit(solution)/shard_map/ppermute | solution.py:30
  24.0 3.0 %collective-permute-done.8.refs_1_ = bf16[512,384]{1,0:T(8,128)(2,1)S(1)} collective-permute-done((bf16[512,384]{1,0:T(8,128)(2,1)}, bf16[512,384]{1,0:T(8,128)(2,1)S(1)}, u32[]{:S(2)}, u32[]{:S(2)}) %collective-permute-start.8) | collective-permute-done | bytes 393248 | tf_op jit(solution)/shard_map/ppermute | solution.py:30
  27.0 0.7 collective-permute-start.9
  27.7 1.3 %collective-permute-start.12 = (bf16[512,384]{1,0:T(8,128)(2,1)S(1)}, bf16[512,384]{1,0:T(8,128)(2,1)S(1)}, u32[]{:S(2)}, u32[]{:S(2)}) collective-permute-start(bf16[512,384]{1,0:T(8,128)(2,1)S(1)} %collective-permute-done.11.refs_4_), channel_id=1, source_target_pairs={{4,0},{8,12},{5,1},{9,13},{6,2},{10,14},{7,3},{11,15},{20,16},{24,... | collective-permute-start | bytes 1179656 | tf_op jit(solution)/shard_map/ppermute | solution.py:30
  29.0 0.2 join.3.inverse
  29.3 6.4 %collective-permute-done.4.refs_5_ = bf16[128,1536]{1,0:T(8,128)(2,1)S(1)} collective-permute-done((bf16[128,1536]{1,0:T(8,128)(2,1)S(1)}, bf16[128,1536]{1,0:T(8,128)(2,1)S(1)}, u32[]{:S(2)}, u32[]{:S(2)}) %collective-permute-start.4) | collective-permute-done | bytes 393248 | tf_op jit(solution)/shard_map/ppermute | solution.py:30
  35.6 9.9 %collective-permute-done.2.refs_3_ = bf16[128,1536]{1,0:T(8,128)(2,1)S(1)} collective-permute-done((bf16[128,1536]{1,0:T(8,128)(2,1)S(1)}, bf16[128,1536]{1,0:T(8,128)(2,1)S(1)}, u32[]{:S(2)}, u32[]{:S(2)}) %collective-permute-start.2) | collective-permute-done | bytes 393248 | tf_op jit(solution)/shard_map/ppermute | solution.py:30
  45.5 0.9 %pick.1 = (bf16[128,1536]{1,0:T(8,128)(2,1)S(1)}, bf16[128,1536]{1,0:T(8,128)(2,1)S(1)}) custom-call(s32[4]{0:T(128)S(1)} %copy-done.5, bf16[128,1536]{1,0:T(8,128)(2,1)S(1)} %copy-done.3, bf16[128,1536]{1,0:T(8,128)(2,1)S(1)} %collective-permute-done.refs_1_, bf16[128,1536]{1,0:T(8,128)(2,1)S(1)} %collective-permute-done.1.refs_2_, ...), custom_call_target="tpu_custom_call" | custom-call | tf_op jit(solution)/shard_map/pick/pallas_call | solution.py:133
  46.5 0.3 collective-permute-start.14
  46.8 1.2 %collective-permute-start.17 = (bf16[128,1536]{1,0:T(8,128)(2,1)S(1)}, bf16[128,1536]{1,0:T(8,128)(2,1)S(1)}, u32[]{:S(2)}, u32[]{:S(2)}) collective-permute-start(bf16[128,1536]{1,0:T(8,128)(2,1)S(1)} %get-tuple-element.15.refs_0_), channel_id=1, source_target_pairs={{0,2},{1,3},{2,0},{3,1},{4,6},{5,7},{6,4},{7,5},{8,10},{9,11},{10,... | collective-permute-start | bytes 1179656 | tf_op jit(solution)/shard_map/ppermute | solution.py:49
  48.0 1.3 %collective-permute-start.10 = (bf16[512,384]{1,0:T(8,128)(2,1)S(1)}, bf16[512,384]{1,0:T(8,128)(2,1)S(1)}, u32[]{:S(2)}, u32[]{:S(2)}) collective-permute-start(bf16[512,384]{1,0:T(8,128)(2,1)S(1)} %collective-permute-done.9.refs_2_), channel_id=1, source_target_pairs={{4,0},{8,12},{5,1},{9,13},{6,2},{10,14},{7,3},{11,15},{20,16},{24,... | collective-permute-start | bytes 1179656 | tf_op jit(solution)/shard_map/ppermute | solution.py:30
  49.3 1.4 %mask.1.masked = bf16[640,2048]{1,0:T(8,128)(2,1)S(1)} custom-call(s32[4]{0:T(128)S(1)} %copy-done.5, s32[4]{0:T(128)S(1)} %copy-done.6, s32[5,16]{1,0:T(8,128)S(1)} %copy-done.4, bf16[640,2048]{1,0:T(8,128)(2,1)S(1)} %copy-done), custom_call_target="tpu_custom_call" | custom-call | tf_op jit(solution)/shard_map/mask/pallas_call | solution.py:213
  50.7 5.2 %collective-permute-start.13 = (bf16[128,1536]{1,0:T(8,128)(2,1)S(1)}, bf16[128,1536]{1,0:T(8,128)(2,1)S(1)}, u32[]{:S(2)}, u32[]{:S(2)}) collective-permute-start(bf16[128,1536]{1,0:T(8,128)(2,1)S(1)} %get-tuple-element.14.refs_0_), channel_id=1, source_target_pairs={{0,1},{1,0},{2,3},{3,2},{4,5},{5,4},{6,7},{7,6},{8,9},{9,8},{10,11... | collective-permute-start | bytes 1179656 | tf_op jit(solution)/shard_map/ppermute | solution.py:49
  55.9 2.6 %collective-permute-start.16 = (bf16[128,1536]{1,0:T(8,128)(2,1)S(1)}, bf16[128,1536]{1,0:T(8,128)(2,1)S(1)}, u32[]{:S(2)}, u32[]{:S(2)}) collective-permute-start(bf16[128,1536]{1,0:T(8,128)(2,1)S(1)} %get-tuple-element.15.refs_0_), channel_id=1, source_target_pairs={{0,1},{1,0},{2,3},{3,2},{4,5},{5,4},{6,7},{7,6},{8,9},{9,8},{10,11... | collective-permute-start | bytes 1179656 | tf_op jit(solution)/shard_map/ppermute | solution.py:49
  58.6 3.7 %collective-permute-start.15 = (bf16[128,1536]{1,0:T(8,128)(2,1)S(1)}, bf16[128,1536]{1,0:T(8,128)(2,1)S(1)}, u32[]{:S(2)}, u32[]{:S(2)}) collective-permute-start(bf16[128,1536]{1,0:T(8,128)(2,1)S(1)} %collective-permute-done.14.refs_2_), channel_id=1, source_target_pairs={{0,1},{1,0},{2,3},{3,2},{4,5},{5,4},{6,7},{7,6},{8,9},{9,8},{10,11... | collective-permute-start | bytes 1179656 | tf_op jit(solution)/shard_map/ppermute | solution.py:49
  62.3 4.2 %collective-permute-start.18 = (bf16[128,1536]{1,0:T(8,128)(2,1)S(1)}, bf16[128,1536]{1,0:T(8,128)(2,1)S(1)}, u32[]{:S(2)}, u32[]{:S(2)}) collective-permute-start(bf16[128,1536]{1,0:T(8,128)(2,1)S(1)} %collective-permute-done.17.refs_2_), channel_id=1, source_target_pairs={{0,1},{1,0},{2,3},{3,2},{4,5},{5,4},{6,7},{7,6},{8,9},{9,8},{10,11... | collective-permute-start | bytes 1179656 | tf_op jit(solution)/shard_map/ppermute | solution.py:49
  66.5 1.5 %order.1.segments = bf16[4,512,384]{2,1,0:T(8,128)(2,1)S(1)} custom-call(s32[4]{0:T(128)S(1)} %copy-done.5, bf16[512,384]{1,0:T(8,128)(2,1)S(1)} %copy-done.7, bf16[512,384]{1,0:T(8,128)(2,1)S(1)} %collective-permute-done.8.refs_1_, bf16[512,384]{1,0:T(8,128)(2,1)S(1)} %collective-permute-done.9.refs_2_, ...), custom_call_target="tpu_custom_call" | custom-call | flops 24000000000 | tf_op jit(solution)/shard_map/order/pallas_call | solution.py:159
  68.0 0.8 %join.4.near = bf16[512,1536]{1,0:T(8,128)(2,1)S(1)} custom-call(bf16[128,1536]{1,0:T(8,128)(2,1)S(1)} %get-tuple-element.14.refs_0_, bf16[128,1536]{1,0:T(8,128)(2,1)S(1)} %collective-permute-done.13.refs_1_, bf16[128,1536]{1,0:T(8,128)(2,1)S(1)} %collective-permute-done.14.refs_2_, bf16[128,1536]{1,0:T(8,128)(2,1)S(1)} %collective-permute-done.15.refs_3_), custom_call_target="tpu_custom_call" | custom-call | tf_op jit(solution)/shard_map/join/pallas_call | solution.py:187
  68.9 0.8 %join.5.far = bf16[512,1536]{1,0:T(8,128)(2,1)S(1)} custom-call(bf16[128,1536]{1,0:T(8,128)(2,1)S(1)} %get-tuple-element.15.refs_0_, bf16[128,1536]{1,0:T(8,128)(2,1)S(1)} %collective-permute-done.16.refs_1_, bf16[128,1536]{1,0:T(8,128)(2,1)S(1)} %collective-permute-done.17.refs_2_, bf16[128,1536]{1,0:T(8,128)(2,1)S(1)} %collective-permute-done.18.refs_3_), custom_call_target="tpu_custom_call" | custom-call | tf_op jit(solution)/shard_map/join/pallas_call | solution.py:187
  69.7 0.2 copy-done.1
  69.9 5.9 %solve.1 = (bf16[512,384]{1,0:T(8,128)(2,1)}, bf16[640,384]{1,0:T(8,128)(2,1)}) custom-call(s32[4]{0:T(128)S(1)} %copy-done.5, bf16[4,512,512]{2,1,0:T(8,128)(2,1)S(1)} %join.3.inverse, bf16[4,512,384]{2,1,0:T(8,128)(2,1)S(1)} %order.1.segments, bf16[512,1536]{1,0:T(8,128)(2,1)S(1)} %join.4.near, bf16[512,1536]{1,0:T(8,128)(2,1)S(1)} %join.5.far, ...), custom_call_target="tpu_custom_call" | custom-call | tf_op jit(solution)/shard_map/solve/pallas_call | solution.py:249
  (30 shorter events, 0.1 us)
Async XLA Ops:
  0.6 5.1 %copy-start.2 = (bf16[4,128,512]{2,1,0:T(8,128)(2,1)S(1)}, bf16[4,128,512]{2,1,0:T(8,128)(2,1)}, u32[]{:S(2)}) copy-start(bf16[4,128,512]{2,1,0:T(8,128)(2,1)} %refs_0_.1) | copy-start | bytes 1572868
  3.5 11.2 %collective-permute-start = (bf16[128,1536]{1,0:T(8,128)(2,1)}, bf16[128,1536]{1,0:T(8,128)(2,1)S(1)}, u32[]{:S(2)}, u32[]{:S(2)}) collective-permute-start(bf16[128,1536]{1,0:T(8,128)(2,1)} %get-tuple-element.9.refs_0_), channel_id=1, source_target_pairs={{4,0},{0,4},{12,8},{8,12},{5,1},{1,5},{13,9},{9,13},{6,2},{2,6},{1... | collective-permute-start | bytes 1179656 | tf_op jit(solution)/shard_map/ppermute | solution.py:30
  5.7 15.6 %collective-permute-start.6 = (bf16[4,128,512]{2,1,0:T(8,128)(2,1)S(1)}, bf16[4,128,512]{2,1,0:T(8,128)(2,1)S(1)}, u32[]{:S(2)}, u32[]{:S(2)}) collective-permute-start(bf16[4,128,512]{2,1,0:T(8,128)(2,1)S(1)} %copy-done.2), channel_id=1, source_target_pairs={{0,2},{1,3},{2,0},{3,1},{4,6},{5,7},{6,4},{7,5},{8,10},{9,11},{10,... | collective-permute-start | bytes 1572872 | tf_op jit(solution)/shard_map/ppermute | solution.py:49
  6.9 12.2 %collective-permute-start.3 = (bf16[128,1536]{1,0:T(8,128)(2,1)}, bf16[128,1536]{1,0:T(8,128)(2,1)S(1)}, u32[]{:S(2)}, u32[]{:S(2)}) collective-permute-start(bf16[128,1536]{1,0:T(8,128)(2,1)} %get-tuple-element.9.refs_0_), channel_id=1, source_target_pairs={{8,4},{4,8},{9,5},{5,9},{10,6},{6,10},{11,7},{7,11},{24,20},{20,24... | collective-permute-start | bytes 1179656 | tf_op jit(solution)/shard_map/ppermute | solution.py:30
  7.6 37.9 %copy-start.3 = (bf16[128,1536]{1,0:T(8,128)(2,1)S(1)}, bf16[128,1536]{1,0:T(8,128)(2,1)}, u32[]{:S(2)}) copy-start(bf16[128,1536]{1,0:T(8,128)(2,1)} %get-tuple-element.9.refs_0_) | copy-start | bytes 1179652
  7.6 37.9 %copy-start.5 = (s32[4]{0:T(128)S(1)}, s32[4]{0:T(128)}, u32[]{:S(2)}) copy-start(s32[4]{0:T(128)} %owners.9) | copy-start | bytes 52
  7.7 13.7 %collective-permute-start.11 = (bf16[512,384]{1,0:T(8,128)(2,1)}, bf16[512,384]{1,0:T(8,128)(2,1)S(1)}, u32[]{:S(2)}, u32[]{:S(2)}) collective-permute-start(bf16[512,384]{1,0:T(8,128)(2,1)} %get-tuple-element.13.refs_0_), channel_id=1, source_target_pairs={{8,4},{4,8},{9,5},{5,9},{10,6},{6,10},{11,7},{7,11},{24,20},{20,24... | collective-permute-start | bytes 1179656 | tf_op jit(solution)/shard_map/ppermute | solution.py:30
  14.8 7.9 %collective-permute-start.1 = (bf16[128,1536]{1,0:T(8,128)(2,1)S(1)}, bf16[128,1536]{1,0:T(8,128)(2,1)S(1)}, u32[]{:S(2)}, u32[]{:S(2)}) collective-permute-start(bf16[128,1536]{1,0:T(8,128)(2,1)S(1)} %collective-permute-done.refs_1_), channel_id=1, source_target_pairs={{8,4},{4,8},{9,5},{5,9},{10,6},{6,10},{11,7},{7,11},{24,20},{20,24... | collective-permute-start | bytes 1179656 | tf_op jit(solution)/shard_map/ppermute | solution.py:30
  15.5 11.5 %collective-permute-start.8 = (bf16[512,384]{1,0:T(8,128)(2,1)}, bf16[512,384]{1,0:T(8,128)(2,1)S(1)}, u32[]{:S(2)}, u32[]{:S(2)}) collective-permute-start(bf16[512,384]{1,0:T(8,128)(2,1)} %get-tuple-element.13.refs_0_), channel_id=1, source_target_pairs={{4,0},{0,4},{12,8},{8,12},{5,1},{1,5},{13,9},{9,13},{6,2},{2,6},{1... | collective-permute-start | bytes 1179656 | tf_op jit(solution)/shard_map/ppermute | solution.py:30
  19.2 8.5 %collective-permute-start.5 = (bf16[4,128,512]{2,1,0:T(8,128)(2,1)S(1)}, bf16[4,128,512]{2,1,0:T(8,128)(2,1)S(1)}, u32[]{:S(2)}, u32[]{:S(2)}) collective-permute-start(bf16[4,128,512]{2,1,0:T(8,128)(2,1)S(1)} %copy-done.2), channel_id=1, source_target_pairs={{0,1},{1,0},{2,3},{3,2},{4,5},{5,4},{6,7},{7,6},{8,9},{9,8},{10,11... | collective-permute-start | bytes 1572872 | tf_op jit(solution)/shard_map/ppermute | solution.py:49
  21.3 7.7 %collective-permute-start.7 = (bf16[4,128,512]{2,1,0:T(8,128)(2,1)S(1)}, bf16[4,128,512]{2,1,0:T(8,128)(2,1)S(1)}, u32[]{:S(2)}, u32[]{:S(2)}) collective-permute-start(bf16[4,128,512]{2,1,0:T(8,128)(2,1)S(1)} %collective-permute-done.6.refs_2_), channel_id=1, source_target_pairs={{0,1},{1,0},{2,3},{3,2},{4,5},{5,4},{6,7},{7,6},{8,9},{9,8},{10,11... | collective-permute-start | bytes 1572872 | tf_op jit(solution)/shard_map/ppermute | solution.py:49
  21.4 14.2 %collective-permute-start.4 = (bf16[128,1536]{1,0:T(8,128)(2,1)S(1)}, bf16[128,1536]{1,0:T(8,128)(2,1)S(1)}, u32[]{:S(2)}, u32[]{:S(2)}) collective-permute-start(bf16[128,1536]{1,0:T(8,128)(2,1)S(1)} %collective-permute-done.3.refs_4_), channel_id=1, source_target_pairs={{4,0},{8,12},{5,1},{9,13},{6,2},{10,14},{7,3},{11,15},{20,16},{24,... | collective-permute-start | bytes 1179656 | tf_op jit(solution)/shard_map/ppermute | solution.py:30
  22.7 22.8 %collective-permute-start.2 = (bf16[128,1536]{1,0:T(8,128)(2,1)S(1)}, bf16[128,1536]{1,0:T(8,128)(2,1)S(1)}, u32[]{:S(2)}, u32[]{:S(2)}) collective-permute-start(bf16[128,1536]{1,0:T(8,128)(2,1)S(1)} %collective-permute-done.1.refs_2_), channel_id=1, source_target_pairs={{4,0},{8,12},{5,1},{9,13},{6,2},{10,14},{7,3},{11,15},{20,16},{24,... | collective-permute-start | bytes 1179656 | tf_op jit(solution)/shard_map/ppermute | solution.py:30
  27.0 21.0 %collective-permute-start.9 = (bf16[512,384]{1,0:T(8,128)(2,1)S(1)}, bf16[512,384]{1,0:T(8,128)(2,1)S(1)}, u32[]{:S(2)}, u32[]{:S(2)}) collective-permute-start(bf16[512,384]{1,0:T(8,128)(2,1)S(1)} %collective-permute-done.8.refs_1_), channel_id=1, source_target_pairs={{8,4},{4,8},{9,5},{5,9},{10,6},{6,10},{11,7},{7,11},{24,20},{20,24... | collective-permute-start | bytes 1179656 | tf_op jit(solution)/shard_map/ppermute | solution.py:30
  27.7 28.2 %collective-permute-start.12 = (bf16[512,384]{1,0:T(8,128)(2,1)S(1)}, bf16[512,384]{1,0:T(8,128)(2,1)S(1)}, u32[]{:S(2)}, u32[]{:S(2)}) collective-permute-start(bf16[512,384]{1,0:T(8,128)(2,1)S(1)} %collective-permute-done.11.refs_4_), channel_id=1, source_target_pairs={{4,0},{8,12},{5,1},{9,13},{6,2},{10,14},{7,3},{11,15},{20,16},{24,... | collective-permute-start | bytes 1179656 | tf_op jit(solution)/shard_map/ppermute | solution.py:30
  29.0 20.3 %copy-start = (bf16[640,2048]{1,0:T(8,128)(2,1)S(1)}, bf16[640,2048]{1,0:T(8,128)(2,1)}, u32[]{:S(2)}) copy-start(bf16[640,2048]{1,0:T(8,128)(2,1)} %factor.3) | copy-start | bytes 7864324
  29.2 20.1 %copy-start.4 = (s32[5,16]{1,0:T(8,128)S(1)}, s32[5,16]{1,0:T(8,128)}, u32[]{:S(2)}) copy-start(s32[5,16]{1,0:T(8,128)} %pattern.3) | copy-start | bytes 964
  29.2 20.1 %copy-start.6 = (s32[4]{0:T(128)S(1)}, s32[4]{0:T(128)}, u32[]{:S(2)}) copy-start(s32[4]{0:T(128)} %offsets.3) | copy-start | bytes 52
  46.5 20.0 %copy-start.7 = (bf16[512,384]{1,0:T(8,128)(2,1)S(1)}, bf16[512,384]{1,0:T(8,128)(2,1)}, u32[]{:S(2)}) copy-start(bf16[512,384]{1,0:T(8,128)(2,1)} %get-tuple-element.13.refs_0_) | copy-start | bytes 1179652
  46.5 12.1 %collective-permute-start.14 = (bf16[128,1536]{1,0:T(8,128)(2,1)S(1)}, bf16[128,1536]{1,0:T(8,128)(2,1)S(1)}, u32[]{:S(2)}, u32[]{:S(2)}) collective-permute-start(bf16[128,1536]{1,0:T(8,128)(2,1)S(1)} %get-tuple-element.14.refs_0_), channel_id=1, source_target_pairs={{0,2},{1,3},{2,0},{3,1},{4,6},{5,7},{6,4},{7,5},{8,10},{9,11},{10,... | collective-permute-start | bytes 1179656 | tf_op jit(solution)/shard_map/ppermute | solution.py:49
  46.8 15.5 %collective-permute-start.17 = (bf16[128,1536]{1,0:T(8,128)(2,1)S(1)}, bf16[128,1536]{1,0:T(8,128)(2,1)S(1)}, u32[]{:S(2)}, u32[]{:S(2)}) collective-permute-start(bf16[128,1536]{1,0:T(8,128)(2,1)S(1)} %get-tuple-element.15.refs_0_), channel_id=1, source_target_pairs={{0,2},{1,3},{2,0},{3,1},{4,6},{5,7},{6,4},{7,5},{8,10},{9,11},{10,... | collective-permute-start | bytes 1179656 | tf_op jit(solution)/shard_map/ppermute | solution.py:49
  48.0 18.5 %collective-permute-start.10 = (bf16[512,384]{1,0:T(8,128)(2,1)S(1)}, bf16[512,384]{1,0:T(8,128)(2,1)S(1)}, u32[]{:S(2)}, u32[]{:S(2)}) collective-permute-start(bf16[512,384]{1,0:T(8,128)(2,1)S(1)} %collective-permute-done.9.refs_2_), channel_id=1, source_target_pairs={{4,0},{8,12},{5,1},{9,13},{6,2},{10,14},{7,3},{11,15},{20,16},{24,... | collective-permute-start | bytes 1179656 | tf_op jit(solution)/shard_map/ppermute | solution.py:30
  50.7 17.3 %collective-permute-start.13 = (bf16[128,1536]{1,0:T(8,128)(2,1)S(1)}, bf16[128,1536]{1,0:T(8,128)(2,1)S(1)}, u32[]{:S(2)}, u32[]{:S(2)}) collective-permute-start(bf16[128,1536]{1,0:T(8,128)(2,1)S(1)} %get-tuple-element.14.refs_0_), channel_id=1, source_target_pairs={{0,1},{1,0},{2,3},{3,2},{4,5},{5,4},{6,7},{7,6},{8,9},{9,8},{10,11... | collective-permute-start | bytes 1179656 | tf_op jit(solution)/shard_map/ppermute | solution.py:49
  55.9 12.9 %collective-permute-start.16 = (bf16[128,1536]{1,0:T(8,128)(2,1)S(1)}, bf16[128,1536]{1,0:T(8,128)(2,1)S(1)}, u32[]{:S(2)}, u32[]{:S(2)}) collective-permute-start(bf16[128,1536]{1,0:T(8,128)(2,1)S(1)} %get-tuple-element.15.refs_0_), channel_id=1, source_target_pairs={{0,1},{1,0},{2,3},{3,2},{4,5},{5,4},{6,7},{7,6},{8,9},{9,8},{10,11... | collective-permute-start | bytes 1179656 | tf_op jit(solution)/shard_map/ppermute | solution.py:49
  58.6 9.5 %collective-permute-start.15 = (bf16[128,1536]{1,0:T(8,128)(2,1)S(1)}, bf16[128,1536]{1,0:T(8,128)(2,1)S(1)}, u32[]{:S(2)}, u32[]{:S(2)}) collective-permute-start(bf16[128,1536]{1,0:T(8,128)(2,1)S(1)} %collective-permute-done.14.refs_2_), channel_id=1, source_target_pairs={{0,1},{1,0},{2,3},{3,2},{4,5},{5,4},{6,7},{7,6},{8,9},{9,8},{10,11... | collective-permute-start | bytes 1179656 | tf_op jit(solution)/shard_map/ppermute | solution.py:49
  62.3 6.6 %collective-permute-start.18 = (bf16[128,1536]{1,0:T(8,128)(2,1)S(1)}, bf16[128,1536]{1,0:T(8,128)(2,1)S(1)}, u32[]{:S(2)}, u32[]{:S(2)}) collective-permute-start(bf16[128,1536]{1,0:T(8,128)(2,1)S(1)} %collective-permute-done.17.refs_2_), channel_id=1, source_target_pairs={{0,1},{1,0},{2,3},{3,2},{4,5},{5,4},{6,7},{7,6},{8,9},{9,8},{10,11... | collective-permute-start | bytes 1179656 | tf_op jit(solution)/shard_map/ppermute | solution.py:49
  68.8 1.0 %copy-start.1 = (bf16[640,384]{1,0:T(8,128)(2,1)S(1)}, bf16[640,384]{1,0:T(8,128)(2,1)}, u32[]{:S(2)}) copy-start(bf16[640,384]{1,0:T(8,128)(2,1)} %right.3) | copy-start | bytes 1474564

commit v2 on v1

--- a/solution.py
+++ b/solution.py
@@ -141,33 +141,6 @@
     )(owners, *(slot for slot in slots if slot is not None))
 
 
-def order_kernel(n_row, held, owners, *refs):
-    slots = fill(held, refs[: sum(held)])
-    segments, sems = refs[sum(held) :]
-
-    def place(node, slot):
-        return pltpu.make_async_copy(slot, segments.at[node], sems.at[node])
-
-    for node in range(SN):
-        start_matching(slots, slot_of(owners[node], n_row), functools.partial(place, node))
-    for node in range(SN):
-        place(node, slots[0]).wait()
-
-
-def order(owners, slots, n_row):
-    held = [slot is not None for slot in slots]
-    return pl.pallas_call(
-        functools.partial(order_kernel, n_row, held),
-        out_shape=jax.ShapeDtypeStruct((SN,) + slots[0].shape, jnp.bfloat16),
-        in_specs=[SMEM] + [ANY] * sum(held),
-        out_specs=ANY,
-        scratch_shapes=[pltpu.SemaphoreType.DMA((SN,))],
-        compiler_params=PARAMS,
-        cost_estimate=pl.CostEstimate(flops=24 * 10**9, bytes_accessed=0, transcendentals=0),
-        name="order",
-    )(owners, *(slot for slot in slots if slot is not None))
-
-
 def join_kernel(*refs):
     *pieces, whole, sems = refs
     me, quarter = lax.axis_index("src"), SNR // len(pieces)
@@ -220,39 +193,119 @@
     )(owners, offsets, pattern, factor)
 
 
-def solve_kernel(owners, inverse, segments, near, far, masked, right, solved, updated, xs, out, sems):
+def first_kernel(n_row, held, owners, inverse, masked, right, *refs):
+    slots = fill(held, refs[: sum(held)])
+    segments, solution, total, segment, sems = refs[sum(held) :]
+
+    def place(node, slot):
+        target = segments.at[node - 1] if node else segment
+        return pltpu.make_async_copy(slot, target, sems.at[node])
+
+    for node in range(SN):
+        start_matching(slots, slot_of(owners[node], n_row), functools.partial(place, node))
+    place(0, slots[0]).wait()
+    x = jnp.dot(inverse[0], segment[...], preferred_element_type=jnp.float32).astype(jnp.bfloat16)
+    solution[...] = x
+    update = jnp.dot(masked[:, :SNR], x, preferred_element_type=jnp.float32)
+    total[...] = right[...].astype(jnp.float32) - update
+    for node in range(1, SN):
+        place(node, slots[0]).wait()
+
+
+def first(owners, inverse, masked, right, slots, n_row):
+    held = [slot is not None for slot in slots]
+    rows, columns = right.shape
+    return pl.pallas_call(
+        functools.partial(first_kernel, n_row, held),
+        out_shape=(
+            jax.ShapeDtypeStruct((SN - 1, SNR, columns), jnp.bfloat16),
+            jax.ShapeDtypeStruct((SNR, columns), jnp.bfloat16),
+            jax.ShapeDtypeStruct((rows, columns), jnp.float32),
+        ),
+        in_specs=[SMEM] + [VMEM] * 3 + [ANY] * sum(held),
+        out_specs=(ANY, VMEM, VMEM),
+        scratch_shapes=[
+            pltpu.VMEM((SNR, columns), jnp.bfloat16),
+            pltpu.SemaphoreType.DMA((SN,)),
+        ],
+        compiler_params=PARAMS,
+        cost_estimate=pl.CostEstimate(flops=60 * 10**9, bytes_accessed=0, transcendentals=0),
+        name="first",
+    )(owners, inverse, masked, right, *(slot for slot in slots if slot is not None))
+
+
+def middle_kernel(inverse, near, masked, segments, start, before, solutions, total):
+    left = before[...]
+    for node in range(1, SN - 1):
+        at = node * (node - 1) // 2 * SNR
+        update = jnp.dot(near[:, at : at + SNR], start[...], preferred_element_type=jnp.float32)
+        if node > 1:
+            update += jnp.dot(
+                near[:, at + SNR : at + node * SNR],
+                solutions[: (node - 1) * SNR],
+                preferred_element_type=jnp.float32,
+            )
+        segment = (segments[node - 1].astype(jnp.float32) - update).astype(jnp.bfloat16)
+        x = jnp.dot(inverse[node], segment, preferred_element_type=jnp.float32).astype(jnp.bfloat16)
+        solutions[(node - 1) * SNR : node * SNR] = x
+    cols = masked[:, SNR : (SN - 1) * SNR]
+    total[...] = left - jnp.dot(cols, solutions[...], preferred_element_type=jnp.float32)
+
+
+def middle(inverse, near, masked, segments, start, total):
+    columns = start.shape[1]
+    return pl.pallas_call(
+        middle_kernel,
+        out_shape=(
+            jax.ShapeDtypeStruct(((SN - 2) * SNR, columns), jnp.bfloat16),
+            jax.ShapeDtypeStruct(total.shape, jnp.float32),
+        ),
+        in_specs=[VMEM] * 6,
+        out_specs=(VMEM, VMEM),
+        compiler_params=PARAMS,
+        cost_estimate=pl.CostEstimate(flops=24 * 10**9, bytes_accessed=0, transcendentals=0),
+        name="middle",
+    )(inverse, near, masked, segments, start, total)
+
+
+def last_kernel(inverse, far, masked, segments, start, solutions, total, solved, updated, xs, out, sems):
     position = lax.axis_index("row")
-    for node in range(SN):
-        segment = segments[node]
-        if node:
-            first = node * (node - 1) // 2 * SNR
-            lower = far[...] if node == SN - 1 else near[:, first : first + node * SNR]
-            update = jnp.dot(lower, xs[: node * SNR], preferred_element_type=jnp.float32)
-            segment = (segment.astype(jnp.float32) - update).astype(jnp.bfloat16)
-        x = jnp.dot(inverse[node], segment, preferred_element_type=jnp.float32)
-        xs[node * SNR : (node + 1) * SNR] = x.astype(jnp.bfloat16)
+    last = (SN - 1) * SNR
+    moves = [
+        pltpu.make_async_copy(start, xs.at[pl.ds(0, SNR)], sems.at[0]),
+        pltpu.make_async_copy(solutions, xs.at[pl.ds(SNR, last - SNR)], sems.at[1]),
+    ]
+    for move in moves:
+        move.start()
+    update = jnp.dot(far[:, :SNR], start[...], preferred_element_type=jnp.float32)
+    update += jnp.dot(far[:, SNR:], solutions[...], preferred_element_type=jnp.float32)
+    segment = (segments[SN - 2].astype(jnp.float32) - update).astype(jnp.bfloat16)
+    x = jnp.dot(inverse[SN - 1], segment, preferred_element_type=jnp.float32).astype(jnp.bfloat16)
+    xs[last:] = x
+    for move in moves:
+        move.wait()
     out_rows = solved.shape[0]
     solved_copy = pltpu.make_async_copy(
         xs.at[pl.ds(pl.multiple_of(position * out_rows, out_rows), out_rows)], solved, sems.at[0]
     )
     solved_copy.start()
-    update = jnp.dot(masked[...], xs[...], preferred_element_type=jnp.float32)
-    out[...] = (right[...].astype(jnp.float32) - update).astype(jnp.bfloat16)
+    update = jnp.dot(masked[:, last:], x, preferred_element_type=jnp.float32)
+    out[...] = (total[...] - update).astype(jnp.bfloat16)
     updated_copy = pltpu.make_async_copy(out, updated, sems.at[1])
     updated_copy.start()
     solved_copy.wait()
     updated_copy.wait()
 
 
-def solve(owners, inverse, segments, near, far, masked, right, n_row):
-    rows, columns = right.shape
-    return pl.pallas_call(
-        solve_kernel,
+def last(inverse, far, masked, segments, start, solutions, total, n_row):
+    rows, columns = total.shape
+    return pl.pallas_call(
+        last_kernel,
         out_shape=(
             jax.ShapeDtypeStruct((SN * SNR // n_row, columns), jnp.bfloat16),
             jax.ShapeDtypeStruct((rows, columns), jnp.bfloat16),
         ),
-        in_specs=[SMEM] + [VMEM] * 6,
+        in_specs=[VMEM] * 7,
         out_specs=(ANY, ANY),
         scratch_shapes=[
             pltpu.VMEM((SN * SNR, columns), jnp.bfloat16),
@@ -260,8 +313,8 @@
             pltpu.SemaphoreType.DMA((2,)),
         ],
         compiler_params=PARAMS,
-        name="solve",
-    )(owners, inverse, segments, near, far, masked, right)
+        name="last",
+    )(inverse, far, masked, segments, start, solutions, total)
 
 
 def on_device(right_side, factor, pattern, inverses, owners, offsets):
@@ -272,9 +325,11 @@
     near, far = pick(owners, pieces, n_row)
     near, far, inverse = lax.optimization_barrier((near, far, inverse))
     near, far = join(src_gather(near, n_src)), join(src_gather(far, n_src))
-    segments = order(owners, line_gather(segment, n_row), n_row)
     masked = mask(owners, offsets, pattern, factor)
-    return solve(owners, inverse, segments, near, far, masked, right_side, n_row)
+    slots = line_gather(segment, n_row)
+    segments, start, total = first(owners, inverse, masked, right_side, slots, n_row)
+    solutions, total = middle(inverse, near, masked, segments, start, total)
+    return last(inverse, far, masked, segments, start, solutions, total, n_row)
 
 
 def solution(mesh):

time: 76.1 us -> 72.5 us (0.953); the launches traced: 75.8 us -> 71.3 us
  starting transfers between devices: 34.6 us -> 29.7 us
    ppermute x9, starting transfers between devices: 20.7 us -> 15.7 us  [src_gather(): lax.ppermute(pieces[distance], 'src', [(i, i ^ bit) for i in range(n)])]
    ppermute x9, waiting for transfers between devices: 0.02 us -> 1.23 us  [src_gather(): lax.ppermute(pieces[distance], 'src', [(i, i ^ bit) for i in range(n)])]
    ppermute x10, waiting for transfers between devices: 25.6 us -> 24.8 us  [line_gather(): got = lax.ppermute(got, 'row', pairs) if pairs else None]
    pallas_call x2 -> x3, Pallas kernels: 7.42 us -> 7.67 us  [the longest x1 2.87 us: last(): pl.pallas_call(last_kernel, out_shape=(jax.ShapeDtypeStruct((SN * SNR //...]
  transfers between devices with their start and end apart: 19 -> 19, of which waited for: 4 -> 6; matrix products, arithmetic and copies ran while one was open for 0% -> 0% of each run, Pallas kernels for 6% -> 11%
where the time goes in v2:
time: 72.5 us; the launch traced here: 71.3 us
  starting transfers between devices  29.7 us (41%)
  waiting for transfers between devices  26 us (36%)
  Pallas kernels  14.7 us (20%)
  between operations  0.91 us (1%)
    ppermute x10, waiting for transfers between devices, line_gather(): got = lax.ppermute(got, 'row', pairs) if pairs else None  24.8 us
    ppermute x9, starting transfers between devices, src_gather(): lax.ppermute(pieces[distance], 'src', [(i, i ^ bit) for i in range(n)])  15.7 us
    ppermute x10, starting transfers between devices, line_gather(): got = lax.ppermute(got, 'row', pairs) if pairs else None  13.9 us
    pallas_call x1, Pallas kernels, stage(): pl.pallas_call(functools.partial(stage_kernel, quarter), out_shape=[jax.S...  2.89 us
    pallas_call x1, Pallas kernels, last(): pl.pallas_call(last_kernel, out_shape=(jax.ShapeDtypeStruct((SN * SNR //...  2.87 us
    pallas_call x1, Pallas kernels, middle(): pl.pallas_call(middle_kernel, out_shape=(jax.ShapeDtypeStruct(((SN - 2) *...  2.45 us
    pallas_call x1, Pallas kernels, first(): pl.pallas_call(functools.partial(first_kernel, n_row, held), out_shape=(j...  2.35 us
    pallas_call x3, Pallas kernels, join(): pl.pallas_call(join_kernel, out_shape=jax.ShapeDtypeStruct(shape, jnp.bfl...  1.79 us
  transfers between devices with their start and end apart: 19, of which 6 were waited for; matrix products, arithmetic and copies ran while one was open for 0% of the time, Pallas kernels for 11%

profile of v2, /device:TPU:1, one launch (start us, length us, event | category | flops | bytes accessed | tf_op | source)
XLA Modules:
  0.0 71.3 jit_solution(14097422236894748673)
XLA Ops:
  0.6 2.9 %stage.1 = (bf16[128,1536]{1,0:T(8,128)(2,1)}, bf16[512,384]{1,0:T(8,128)(2,1)}) custom-call(s32[4]{0:T(128)} %owners.7, s32[4]{0:T(128)} %offsets.3, s32[5,16]{1,0:T(8,128)} %pattern.3, bf16[640,2048]{1,0:T(8,128)(2,1)} %factor.3, bf16[640,384]{1,0:T(8,128)(2,1)} %right.3), custom_call_target="tpu_custom_call" | custom-call | tf_op jit(solution)/shard_map/stage/pallas_call | solution.py:99
  3.5 2.2 %collective-permute-start = (bf16[128,1536]{1,0:T(8,128)(2,1)}, bf16[128,1536]{1,0:T(8,128)(2,1)S(1)}, u32[]{:S(2)}, u32[]{:S(2)}) collective-permute-start(bf16[128,1536]{1,0:T(8,128)(2,1)} %get-tuple-element.14.refs_0_), channel_id=1, source_target_pairs={{4,0},{0,4},{12,8},{8,12},{5,1},{1,5},{13,9},{9,13},{6,2},{2,6},{1... | collective-permute-start | bytes 1179656 | tf_op jit(solution)/shard_map/ppermute | solution.py:30
  5.7 1.2 %collective-permute-start.6 = (bf16[4,128,512]{2,1,0:T(8,128)(2,1)S(1)}, bf16[4,128,512]{2,1,0:T(8,128)(2,1)S(1)}, u32[]{:S(2)}, u32[]{:S(2)}) collective-permute-start(bf16[4,128,512]{2,1,0:T(8,128)(2,1)S(1)} %copy-done.1), channel_id=1, source_target_pairs={{0,2},{1,3},{2,0},{3,1},{4,6},{5,7},{6,4},{7,5},{8,10},{9,11},{10,... | collective-permute-start | bytes 1572872 | tf_op jit(solution)/shard_map/ppermute | solution.py:49
  6.9 0.7 collective-permute-start.3
  7.7 3.9 %collective-permute-start.11 = (bf16[512,384]{1,0:T(8,128)(2,1)}, bf16[512,384]{1,0:T(8,128)(2,1)S(1)}, u32[]{:S(2)}, u32[]{:S(2)}) collective-permute-start(bf16[512,384]{1,0:T(8,128)(2,1)} %get-tuple-element.19.refs_0_), channel_id=1, source_target_pairs={{4,0},{0,4},{12,8},{8,12},{5,1},{1,5},{13,9},{9,13},{6,2},{2,6},{1... | collective-permute-start | bytes 1179656 | tf_op jit(solution)/shard_map/ppermute | solution.py:30
  11.5 3.3 %collective-permute-done.refs_1_ = bf16[128,1536]{1,0:T(8,128)(2,1)S(1)} collective-permute-done((bf16[128,1536]{1,0:T(8,128)(2,1)}, bf16[128,1536]{1,0:T(8,128)(2,1)S(1)}, u32[]{:S(2)}, u32[]{:S(2)}) %collective-permute-start) | collective-permute-done | bytes 393248 | tf_op jit(solution)/shard_map/ppermute | solution.py:30
  14.8 0.7 collective-permute-start.1
  15.5 0.7 collective-permute-start.14
  16.2 2.1 %collective-permute-start.5 = (bf16[4,128,512]{2,1,0:T(8,128)(2,1)S(1)}, bf16[4,128,512]{2,1,0:T(8,128)(2,1)S(1)}, u32[]{:S(2)}, u32[]{:S(2)}) collective-permute-start(bf16[4,128,512]{2,1,0:T(8,128)(2,1)S(1)} %copy-done.1), channel_id=1, source_target_pairs={{0,1},{1,0},{2,3},{3,2},{4,5},{5,4},{6,7},{7,6},{8,9},{9,8},{10,11... | collective-permute-start | bytes 1572872 | tf_op jit(solution)/shard_map/ppermute | solution.py:49
  18.3 1.8 %collective-permute-start.7 = (bf16[4,128,512]{2,1,0:T(8,128)(2,1)S(1)}, bf16[4,128,512]{2,1,0:T(8,128)(2,1)S(1)}, u32[]{:S(2)}, u32[]{:S(2)}) collective-permute-start(bf16[4,128,512]{2,1,0:T(8,128)(2,1)S(1)} %collective-permute-done.6.refs_2_), channel_id=1, source_target_pairs={{0,1},{1,0},{2,3},{3,2},{4,5},{5,4},{6,7},{7,6},{8,9},{9,8},{10,11... | collective-permute-start | bytes 1572872 | tf_op jit(solution)/shard_map/ppermute | solution.py:49
  20.1 3.1 %collective-permute-done.11.refs_1_ = bf16[512,384]{1,0:T(8,128)(2,1)S(1)} collective-permute-done((bf16[512,384]{1,0:T(8,128)(2,1)}, bf16[512,384]{1,0:T(8,128)(2,1)S(1)}, u32[]{:S(2)}, u32[]{:S(2)}) %collective-permute-start.11) | collective-permute-done | bytes 393248 | tf_op jit(solution)/shard_map/ppermute | solution.py:30
  23.2 1.3 %collective-permute-start.4 = (bf16[128,1536]{1,0:T(8,128)(2,1)S(1)}, bf16[128,1536]{1,0:T(8,128)(2,1)S(1)}, u32[]{:S(2)}, u32[]{:S(2)}) collective-permute-start(bf16[128,1536]{1,0:T(8,128)(2,1)S(1)} %collective-permute-done.3.refs_4_), channel_id=1, source_target_pairs={{4,0},{8,12},{5,1},{9,13},{6,2},{10,14},{7,3},{11,15},{20,16},{24,... | collective-permute-start | bytes 1179656 | tf_op jit(solution)/shard_map/ppermute | solution.py:30
  24.5 1.3 %collective-permute-start.2 = (bf16[128,1536]{1,0:T(8,128)(2,1)S(1)}, bf16[128,1536]{1,0:T(8,128)(2,1)S(1)}, u32[]{:S(2)}, u32[]{:S(2)}) collective-permute-start(bf16[128,1536]{1,0:T(8,128)(2,1)S(1)} %collective-permute-done.1.refs_2_), channel_id=1, source_target_pairs={{4,0},{8,12},{5,1},{9,13},{6,2},{10,14},{7,3},{11,15},{20,16},{24,... | collective-permute-start | bytes 1179656 | tf_op jit(solution)/shard_map/ppermute | solution.py:30
  25.8 0.7 collective-permute-start.12
  26.5 1.3 %collective-permute-start.15 = (bf16[512,384]{1,0:T(8,128)(2,1)S(1)}, bf16[512,384]{1,0:T(8,128)(2,1)S(1)}, u32[]{:S(2)}, u32[]{:S(2)}) collective-permute-start(bf16[512,384]{1,0:T(8,128)(2,1)S(1)} %collective-permute-done.14.refs_4_), channel_id=1, source_target_pairs={{4,0},{8,12},{5,1},{9,13},{6,2},{10,14},{7,3},{11,15},{20,16},{24,... | collective-permute-start | bytes 1179656 | tf_op jit(solution)/shard_map/ppermute | solution.py:30
  28.1 6.4 %collective-permute-done.4.refs_5_ = bf16[128,1536]{1,0:T(8,128)(2,1)S(1)} collective-permute-done((bf16[128,1536]{1,0:T(8,128)(2,1)S(1)}, bf16[128,1536]{1,0:T(8,128)(2,1)S(1)}, u32[]{:S(2)}, u32[]{:S(2)}) %collective-permute-start.4) | collective-permute-done | bytes 393248 | tf_op jit(solution)/shard_map/ppermute | solution.py:30
  34.5 8.4 %collective-permute-done.2.refs_3_ = bf16[128,1536]{1,0:T(8,128)(2,1)S(1)} collective-permute-done((bf16[128,1536]{1,0:T(8,128)(2,1)S(1)}, bf16[128,1536]{1,0:T(8,128)(2,1)S(1)}, u32[]{:S(2)}, u32[]{:S(2)}) %collective-permute-start.2) | collective-permute-done | bytes 393248 | tf_op jit(solution)/shard_map/ppermute | solution.py:30
  42.9 0.9 %pick.1 = (bf16[128,1536]{1,0:T(8,128)(2,1)S(1)}, bf16[128,1536]{1,0:T(8,128)(2,1)S(1)}) custom-call(s32[4]{0:T(128)S(1)} %copy-done.5, bf16[128,1536]{1,0:T(8,128)(2,1)S(1)} %copy-done.3, bf16[128,1536]{1,0:T(8,128)(2,1)S(1)} %collective-permute-done.refs_1_, bf16[128,1536]{1,0:T(8,128)(2,1)S(1)} %collective-permute-done.1.refs_2_, ...), custom_call_target="tpu_custom_call" | custom-call | tf_op jit(solution)/shard_map/pick/pallas_call | solution.py:133
  43.9 0.8 %collective-permute-start.17 = (bf16[128,1536]{1,0:T(8,128)(2,1)S(1)}, bf16[128,1536]{1,0:T(8,128)(2,1)S(1)}, u32[]{:S(2)}, u32[]{:S(2)}) collective-permute-start(bf16[128,1536]{1,0:T(8,128)(2,1)S(1)} %get-tuple-element.22.refs_0_), channel_id=1, source_target_pairs={{0,2},{1,3},{2,0},{3,1},{4,6},{5,7},{6,4},{7,5},{8,10},{9,11},{10,... | collective-permute-start | bytes 1179656 | tf_op jit(solution)/shard_map/ppermute | solution.py:49
  44.7 1.3 %collective-permute-start.13 = (bf16[512,384]{1,0:T(8,128)(2,1)S(1)}, bf16[512,384]{1,0:T(8,128)(2,1)S(1)}, u32[]{:S(2)}, u32[]{:S(2)}) collective-permute-start(bf16[512,384]{1,0:T(8,128)(2,1)S(1)} %collective-permute-done.12.refs_2_), channel_id=1, source_target_pairs={{4,0},{8,12},{5,1},{9,13},{6,2},{10,14},{7,3},{11,15},{20,16},{24,... | collective-permute-start | bytes 1179656 | tf_op jit(solution)/shard_map/ppermute | solution.py:30
  46.0 1.4 %mask.1.masked = bf16[640,2048]{1,0:T(8,128)(2,1)S(1)} custom-call(s32[4]{0:T(128)S(1)} %copy-done.5, s32[4]{0:T(128)S(1)} %copy-done.6, s32[5,16]{1,0:T(8,128)S(1)} %copy-done.4, bf16[640,2048]{1,0:T(8,128)(2,1)S(1)} %copy-done), custom_call_target="tpu_custom_call" | custom-call | tf_op jit(solution)/shard_map/mask/pallas_call | solution.py:186
  47.4 4.9 %collective-permute-start.16 = (bf16[128,1536]{1,0:T(8,128)(2,1)S(1)}, bf16[128,1536]{1,0:T(8,128)(2,1)S(1)}, u32[]{:S(2)}, u32[]{:S(2)}) collective-permute-start(bf16[128,1536]{1,0:T(8,128)(2,1)S(1)} %get-tuple-element.22.refs_0_), channel_id=1, source_target_pairs={{0,1},{1,0},{2,3},{3,2},{4,5},{5,4},{6,7},{7,6},{8,9},{9,8},{10,11... | collective-permute-start | bytes 1179656 | tf_op jit(solution)/shard_map/ppermute | solution.py:49
  52.4 2.8 %collective-permute-start.8 = (bf16[128,1536]{1,0:T(8,128)(2,1)S(1)}, bf16[128,1536]{1,0:T(8,128)(2,1)S(1)}, u32[]{:S(2)}, u32[]{:S(2)}) collective-permute-start(bf16[128,1536]{1,0:T(8,128)(2,1)S(1)} %get-tuple-element.18.refs_0_), channel_id=1, source_target_pairs={{0,1},{1,0},{2,3},{3,2},{4,5},{5,4},{6,7},{7,6},{8,9},{9,8},{10,11... | collective-permute-start | bytes 1179656 | tf_op jit(solution)/shard_map/ppermute | solution.py:49
  55.2 1.0 %collective-permute-start.18 = (bf16[128,1536]{1,0:T(8,128)(2,1)S(1)}, bf16[128,1536]{1,0:T(8,128)(2,1)S(1)}, u32[]{:S(2)}, u32[]{:S(2)}) collective-permute-start(bf16[128,1536]{1,0:T(8,128)(2,1)S(1)} %collective-permute-done.17.refs_2_), channel_id=1, source_target_pairs={{0,1},{1,0},{2,3},{3,2},{4,5},{5,4},{6,7},{7,6},{8,9},{9,8},{10,11... | collective-permute-start | bytes 1179656 | tf_op jit(solution)/shard_map/ppermute | solution.py:49
  56.2 3.5 %collective-permute-done.13.refs_3_ = bf16[512,384]{1,0:T(8,128)(2,1)S(1)} collective-permute-done((bf16[512,384]{1,0:T(8,128)(2,1)S(1)}, bf16[512,384]{1,0:T(8,128)(2,1)S(1)}, u32[]{:S(2)}, u32[]{:S(2)}) %collective-permute-start.13) | collective-permute-done | bytes 393248 | tf_op jit(solution)/shard_map/ppermute | solution.py:30
  59.8 2.3 %first.1 = (bf16[3,512,384]{2,1,0:T(8,128)(2,1)S(1)}, bf16[512,384]{1,0:T(8,128)(2,1)S(1)}, f32[640,384]{1,0:T(8,128)S(1)}) custom-call(s32[4]{0:T(128)S(1)} %copy-done.5, bf16[4,512,512]{2,1,0:T(8,128)(2,1)S(1)} %join.3.inverse, bf16[640,2048]{1,0:T(8,128)(2,1)S(1)} %mask.1.masked, bf16[640,384]{1,0:T(8,128)(2,1)S(1)} %copy-done.2, ...), custom_call_target="tpu_custom_call" | custom-call | flops 60000002048 | tf_op jit(solution)/shard_map/first/pallas_call | solution.py:218
  62.1 1.2 %collective-permute-done.9.refs_2_ = bf16[128,1536]{1,0:T(8,128)(2,1)S(1)} collective-permute-done((bf16[128,1536]{1,0:T(8,128)(2,1)S(1)}, bf16[128,1536]{1,0:T(8,128)(2,1)S(1)}, u32[]{:S(2)}, u32[]{:S(2)}) %collective-permute-start.9) | collective-permute-done | bytes 393248 | tf_op jit(solution)/shard_map/ppermute | solution.py:49
  63.3 1.0 %collective-permute-start.10 = (bf16[128,1536]{1,0:T(8,128)(2,1)S(1)}, bf16[128,1536]{1,0:T(8,128)(2,1)S(1)}, u32[]{:S(2)}, u32[]{:S(2)}) collective-permute-start(bf16[128,1536]{1,0:T(8,128)(2,1)S(1)} %collective-permute-done.9.refs_2_), channel_id=1, source_target_pairs={{0,1},{1,0},{2,3},{3,2},{4,5},{5,4},{6,7},{7,6},{8,9},{9,8},{10,11... | collective-permute-start | bytes 1179656 | tf_op jit(solution)/shard_map/ppermute | solution.py:49
  64.3 0.8 %join.5.near = bf16[512,1536]{1,0:T(8,128)(2,1)S(1)} custom-call(bf16[128,1536]{1,0:T(8,128)(2,1)S(1)} %get-tuple-element.22.refs_0_, bf16[128,1536]{1,0:T(8,128)(2,1)S(1)} %collective-permute-done.16.refs_1_, bf16[128,1536]{1,0:T(8,128)(2,1)S(1)} %collective-permute-done.17.refs_2_, bf16[128,1536]{1,0:T(8,128)(2,1)S(1)} %collective-permute-done.18.refs_3_), custom_call_target="tpu_custom_call" | custom-call | tf_op jit(solution)/shard_map/join/pallas_call | solution.py:160
  65.1 2.4 %middle.1 = (bf16[1024,384]{1,0:T(8,128)(2,1)S(1)}, f32[640,384]{1,0:T(8,128)S(1)}) custom-call(bf16[4,512,512]{2,1,0:T(8,128)(2,1)S(1)} %join.3.inverse, bf16[512,1536]{1,0:T(8,128)(2,1)S(1)} %join.5.near, bf16[640,2048]{1,0:T(8,128)(2,1)S(1)} %mask.1.masked, bf16[3,512,384]{2,1,0:T(8,128)(2,1)S(1)} %get-tuple-element.20.segments, ...), custom_call_target="tpu_custom_call" | custom-call | flops 24000000000 | tf_op jit(solution)/shard_map/middle/pallas_call | solution.py:257
  67.6 0.8 %join.4.far = bf16[512,1536]{1,0:T(8,128)(2,1)S(1)} custom-call(bf16[128,1536]{1,0:T(8,128)(2,1)S(1)} %get-tuple-element.18.refs_0_, bf16[128,1536]{1,0:T(8,128)(2,1)S(1)} %collective-permute-done.8.refs_1_, bf16[128,1536]{1,0:T(8,128)(2,1)S(1)} %collective-permute-done.9.refs_2_, bf16[128,1536]{1,0:T(8,128)(2,1)S(1)} %collective-permute-done.10.refs_3_), custom_call_target="tpu_custom_call" | custom-call | tf_op jit(solution)/shard_map/join/pallas_call | solution.py:160
  68.4 2.9 %last.1 = (bf16[512,384]{1,0:T(8,128)(2,1)}, bf16[640,384]{1,0:T(8,128)(2,1)}) custom-call(bf16[4,512,512]{2,1,0:T(8,128)(2,1)S(1)} %join.3.inverse, bf16[512,1536]{1,0:T(8,128)(2,1)S(1)} %join.4.far, bf16[640,2048]{1,0:T(8,128)(2,1)S(1)} %mask.1.masked, bf16[3,512,384]{2,1,0:T(8,128)(2,1)S(1)} %get-tuple-element.20.segments, ...), custom_call_target="tpu_custom_call" | custom-call | tf_op jit(solution)/shard_map/last/pallas_call | solution.py:302
  (31 shorter events, 0.4 us)
Async XLA Ops:
  0.6 5.1 %copy-start.1 = (bf16[4,128,512]{2,1,0:T(8,128)(2,1)S(1)}, bf16[4,128,512]{2,1,0:T(8,128)(2,1)}, u32[]{:S(2)}) copy-start(bf16[4,128,512]{2,1,0:T(8,128)(2,1)} %refs_0_.1) | copy-start | bytes 1572868
  3.5 11.2 %collective-permute-start = (bf16[128,1536]{1,0:T(8,128)(2,1)}, bf16[128,1536]{1,0:T(8,128)(2,1)S(1)}, u32[]{:S(2)}, u32[]{:S(2)}) collective-permute-start(bf16[128,1536]{1,0:T(8,128)(2,1)} %get-tuple-element.14.refs_0_), channel_id=1, source_target_pairs={{4,0},{0,4},{12,8},{8,12},{5,1},{1,5},{13,9},{9,13},{6,2},{2,6},{1... | collective-permute-start | bytes 1179656 | tf_op jit(solution)/shard_map/ppermute | solution.py:30
  5.7 12.6 %collective-permute-start.6 = (bf16[4,128,512]{2,1,0:T(8,128)(2,1)S(1)}, bf16[4,128,512]{2,1,0:T(8,128)(2,1)S(1)}, u32[]{:S(2)}, u32[]{:S(2)}) collective-permute-start(bf16[4,128,512]{2,1,0:T(8,128)(2,1)S(1)} %copy-done.1), channel_id=1, source_target_pairs={{0,2},{1,3},{2,0},{3,1},{4,6},{5,7},{6,4},{7,5},{8,10},{9,11},{10,... | collective-permute-start | bytes 1572872 | tf_op jit(solution)/shard_map/ppermute | solution.py:49
  6.9 9.2 %collective-permute-start.3 = (bf16[128,1536]{1,0:T(8,128)(2,1)}, bf16[128,1536]{1,0:T(8,128)(2,1)S(1)}, u32[]{:S(2)}, u32[]{:S(2)}) collective-permute-start(bf16[128,1536]{1,0:T(8,128)(2,1)} %get-tuple-element.14.refs_0_), channel_id=1, source_target_pairs={{8,4},{4,8},{9,5},{5,9},{10,6},{6,10},{11,7},{7,11},{24,20},{20,24... | collective-permute-start | bytes 1179656 | tf_op jit(solution)/shard_map/ppermute | solution.py:30
  7.6 35.3 %copy-start.3 = (bf16[128,1536]{1,0:T(8,128)(2,1)S(1)}, bf16[128,1536]{1,0:T(8,128)(2,1)}, u32[]{:S(2)}) copy-start(bf16[128,1536]{1,0:T(8,128)(2,1)} %get-tuple-element.14.refs_0_) | copy-start | bytes 1179652
  7.6 35.3 %copy-start.5 = (s32[4]{0:T(128)S(1)}, s32[4]{0:T(128)}, u32[]{:S(2)}) copy-start(s32[4]{0:T(128)} %owners.7) | copy-start | bytes 52
  7.7 15.6 %collective-permute-start.11 = (bf16[512,384]{1,0:T(8,128)(2,1)}, bf16[512,384]{1,0:T(8,128)(2,1)S(1)}, u32[]{:S(2)}, u32[]{:S(2)}) collective-permute-start(bf16[512,384]{1,0:T(8,128)(2,1)} %get-tuple-element.19.refs_0_), channel_id=1, source_target_pairs={{4,0},{0,4},{12,8},{8,12},{5,1},{1,5},{13,9},{9,13},{6,2},{2,6},{1... | collective-permute-start | bytes 1179656 | tf_op jit(solution)/shard_map/ppermute | solution.py:30
  14.8 9.7 %collective-permute-start.1 = (bf16[128,1536]{1,0:T(8,128)(2,1)S(1)}, bf16[128,1536]{1,0:T(8,128)(2,1)S(1)}, u32[]{:S(2)}, u32[]{:S(2)}) collective-permute-start(bf16[128,1536]{1,0:T(8,128)(2,1)S(1)} %collective-permute-done.refs_1_), channel_id=1, source_target_pairs={{8,4},{4,8},{9,5},{5,9},{10,6},{6,10},{11,7},{7,11},{24,20},{20,24... | collective-permute-start | bytes 1179656 | tf_op jit(solution)/shard_map/ppermute | solution.py:30
  15.5 10.3 %collective-permute-start.14 = (bf16[512,384]{1,0:T(8,128)(2,1)}, bf16[512,384]{1,0:T(8,128)(2,1)S(1)}, u32[]{:S(2)}, u32[]{:S(2)}) collective-permute-start(bf16[512,384]{1,0:T(8,128)(2,1)} %get-tuple-element.19.refs_0_), channel_id=1, source_target_pairs={{8,4},{4,8},{9,5},{5,9},{10,6},{6,10},{11,7},{7,11},{24,20},{20,24... | collective-permute-start | bytes 1179656 | tf_op jit(solution)/shard_map/ppermute | solution.py:30
  16.2 10.3 %collective-permute-start.5 = (bf16[4,128,512]{2,1,0:T(8,128)(2,1)S(1)}, bf16[4,128,512]{2,1,0:T(8,128)(2,1)S(1)}, u32[]{:S(2)}, u32[]{:S(2)}) collective-permute-start(bf16[4,128,512]{2,1,0:T(8,128)(2,1)S(1)} %copy-done.1), channel_id=1, source_target_pairs={{0,1},{1,0},{2,3},{3,2},{4,5},{5,4},{6,7},{7,6},{8,9},{9,8},{10,11... | collective-permute-start | bytes 1572872 | tf_op jit(solution)/shard_map/ppermute | solution.py:49
  18.3 9.5 %collective-permute-start.7 = (bf16[4,128,512]{2,1,0:T(8,128)(2,1)S(1)}, bf16[4,128,512]{2,1,0:T(8,128)(2,1)S(1)}, u32[]{:S(2)}, u32[]{:S(2)}) collective-permute-start(bf16[4,128,512]{2,1,0:T(8,128)(2,1)S(1)} %collective-permute-done.6.refs_2_), channel_id=1, source_target_pairs={{0,1},{1,0},{2,3},{3,2},{4,5},{5,4},{6,7},{7,6},{8,9},{9,8},{10,11... | collective-permute-start | bytes 1572872 | tf_op jit(solution)/shard_map/ppermute | solution.py:49
  23.2 11.3 %collective-permute-start.4 = (bf16[128,1536]{1,0:T(8,128)(2,1)S(1)}, bf16[128,1536]{1,0:T(8,128)(2,1)S(1)}, u32[]{:S(2)}, u32[]{:S(2)}) collective-permute-start(bf16[128,1536]{1,0:T(8,128)(2,1)S(1)} %collective-permute-done.3.refs_4_), channel_id=1, source_target_pairs={{4,0},{8,12},{5,1},{9,13},{6,2},{10,14},{7,3},{11,15},{20,16},{24,... | collective-permute-start | bytes 1179656 | tf_op jit(solution)/shard_map/ppermute | solution.py:30
  24.5 18.4 %collective-permute-start.2 = (bf16[128,1536]{1,0:T(8,128)(2,1)S(1)}, bf16[128,1536]{1,0:T(8,128)(2,1)S(1)}, u32[]{:S(2)}, u32[]{:S(2)}) collective-permute-start(bf16[128,1536]{1,0:T(8,128)(2,1)S(1)} %collective-permute-done.1.refs_2_), channel_id=1, source_target_pairs={{4,0},{8,12},{5,1},{9,13},{6,2},{10,14},{7,3},{11,15},{20,16},{24,... | collective-permute-start | bytes 1179656 | tf_op jit(solution)/shard_map/ppermute | solution.py:30
  25.8 18.8 %collective-permute-start.12 = (bf16[512,384]{1,0:T(8,128)(2,1)S(1)}, bf16[512,384]{1,0:T(8,128)(2,1)S(1)}, u32[]{:S(2)}, u32[]{:S(2)}) collective-permute-start(bf16[512,384]{1,0:T(8,128)(2,1)S(1)} %collective-permute-done.11.refs_1_), channel_id=1, source_target_pairs={{8,4},{4,8},{9,5},{5,9},{10,6},{6,10},{11,7},{7,11},{24,20},{20,24... | collective-permute-start | bytes 1179656 | tf_op jit(solution)/shard_map/ppermute | solution.py:30
  26.5 25.9 %collective-permute-start.15 = (bf16[512,384]{1,0:T(8,128)(2,1)S(1)}, bf16[512,384]{1,0:T(8,128)(2,1)S(1)}, u32[]{:S(2)}, u32[]{:S(2)}) collective-permute-start(bf16[512,384]{1,0:T(8,128)(2,1)S(1)} %collective-permute-done.14.refs_4_), channel_id=1, source_target_pairs={{4,0},{8,12},{5,1},{9,13},{6,2},{10,14},{7,3},{11,15},{20,16},{24,... | collective-permute-start | bytes 1179656 | tf_op jit(solution)/shard_map/ppermute | solution.py:30
  27.8 18.1 %copy-start = (bf16[640,2048]{1,0:T(8,128)(2,1)S(1)}, bf16[640,2048]{1,0:T(8,128)(2,1)}, u32[]{:S(2)}) copy-start(bf16[640,2048]{1,0:T(8,128)(2,1)} %factor.3) | copy-start | bytes 7864324
  28.1 17.9 %copy-start.4 = (s32[5,16]{1,0:T(8,128)S(1)}, s32[5,16]{1,0:T(8,128)}, u32[]{:S(2)}) copy-start(s32[5,16]{1,0:T(8,128)} %pattern.3) | copy-start | bytes 964
  28.1 17.9 %copy-start.6 = (s32[4]{0:T(128)S(1)}, s32[4]{0:T(128)}, u32[]{:S(2)}) copy-start(s32[4]{0:T(128)} %offsets.3) | copy-start | bytes 52
  43.8 15.9 %copy-start.2 = (bf16[640,384]{1,0:T(8,128)(2,1)S(1)}, bf16[640,384]{1,0:T(8,128)(2,1)}, u32[]{:S(2)}) copy-start(bf16[640,384]{1,0:T(8,128)(2,1)} %right.3) | copy-start | bytes 1474564
  43.8 15.9 %copy-start.7 = (bf16[512,384]{1,0:T(8,128)(2,1)S(1)}, bf16[512,384]{1,0:T(8,128)(2,1)}, u32[]{:S(2)}) copy-start(bf16[512,384]{1,0:T(8,128)(2,1)} %get-tuple-element.19.refs_0_) | copy-start | bytes 1179652
  43.9 11.4 %collective-permute-start.17 = (bf16[128,1536]{1,0:T(8,128)(2,1)S(1)}, bf16[128,1536]{1,0:T(8,128)(2,1)S(1)}, u32[]{:S(2)}, u32[]{:S(2)}) collective-permute-start(bf16[128,1536]{1,0:T(8,128)(2,1)S(1)} %get-tuple-element.22.refs_0_), channel_id=1, source_target_pairs={{0,2},{1,3},{2,0},{3,1},{4,6},{5,7},{6,4},{7,5},{8,10},{9,11},{10,... | collective-permute-start | bytes 1179656 | tf_op jit(solution)/shard_map/ppermute | solution.py:49
  44.7 15.1 %collective-permute-start.13 = (bf16[512,384]{1,0:T(8,128)(2,1)S(1)}, bf16[512,384]{1,0:T(8,128)(2,1)S(1)}, u32[]{:S(2)}, u32[]{:S(2)}) collective-permute-start(bf16[512,384]{1,0:T(8,128)(2,1)S(1)} %collective-permute-done.12.refs_2_), channel_id=1, source_target_pairs={{4,0},{8,12},{5,1},{9,13},{6,2},{10,14},{7,3},{11,15},{20,16},{24,... | collective-permute-start | bytes 1179656 | tf_op jit(solution)/shard_map/ppermute | solution.py:30
  47.4 17.0 %collective-permute-start.16 = (bf16[128,1536]{1,0:T(8,128)(2,1)S(1)}, bf16[128,1536]{1,0:T(8,128)(2,1)S(1)}, u32[]{:S(2)}, u32[]{:S(2)}) collective-permute-start(bf16[128,1536]{1,0:T(8,128)(2,1)S(1)} %get-tuple-element.22.refs_0_), channel_id=1, source_target_pairs={{0,1},{1,0},{2,3},{3,2},{4,5},{5,4},{6,7},{7,6},{8,9},{9,8},{10,11... | collective-permute-start | bytes 1179656 | tf_op jit(solution)/shard_map/ppermute | solution.py:49
  52.3 11.1 %collective-permute-start.9 = (bf16[128,1536]{1,0:T(8,128)(2,1)S(1)}, bf16[128,1536]{1,0:T(8,128)(2,1)S(1)}, u32[]{:S(2)}, u32[]{:S(2)}) collective-permute-start(bf16[128,1536]{1,0:T(8,128)(2,1)S(1)} %get-tuple-element.18.refs_0_), channel_id=1, source_target_pairs={{0,2},{1,3},{2,0},{3,1},{4,6},{5,7},{6,4},{7,5},{8,10},{9,11},{10,... | collective-permute-start | bytes 1179656 | tf_op jit(solution)/shard_map/ppermute | solution.py:49
  52.4 15.2 %collective-permute-start.8 = (bf16[128,1536]{1,0:T(8,128)(2,1)S(1)}, bf16[128,1536]{1,0:T(8,128)(2,1)S(1)}, u32[]{:S(2)}, u32[]{:S(2)}) collective-permute-start(bf16[128,1536]{1,0:T(8,128)(2,1)S(1)} %get-tuple-element.18.refs_0_), channel_id=1, source_target_pairs={{0,1},{1,0},{2,3},{3,2},{4,5},{5,4},{6,7},{7,6},{8,9},{9,8},{10,11... | collective-permute-start | bytes 1179656 | tf_op jit(solution)/shard_map/ppermute | solution.py:49
  55.2 9.1 %collective-permute-start.18 = (bf16[128,1536]{1,0:T(8,128)(2,1)S(1)}, bf16[128,1536]{1,0:T(8,128)(2,1)S(1)}, u32[]{:S(2)}, u32[]{:S(2)}) collective-permute-start(bf16[128,1536]{1,0:T(8,128)(2,1)S(1)} %collective-permute-done.17.refs_2_), channel_id=1, source_target_pairs={{0,1},{1,0},{2,3},{3,2},{4,5},{5,4},{6,7},{7,6},{8,9},{9,8},{10,11... | collective-permute-start | bytes 1179656 | tf_op jit(solution)/shard_map/ppermute | solution.py:49
  63.3 4.3 %collective-permute-start.10 = (bf16[128,1536]{1,0:T(8,128)(2,1)S(1)}, bf16[128,1536]{1,0:T(8,128)(2,1)S(1)}, u32[]{:S(2)}, u32[]{:S(2)}) collective-permute-start(bf16[128,1536]{1,0:T(8,128)(2,1)S(1)} %collective-permute-done.9.refs_2_), channel_id=1, source_target_pairs={{0,1},{1,0},{2,3},{3,2},{4,5},{5,4},{6,7},{7,6},{8,9},{9,8},{10,11... | collective-permute-start | bytes 1179656 | tf_op jit(solution)/shard_map/ppermute | solution.py:49

commit v3 on v2

--- a/solution.py
+++ b/solution.py
@@ -25,7 +25,8 @@
             pairs = []
             for i in range(n):
                 side = 1 if (i + chain + hop) % 2 else -1
-                if 0 <= i + side * hop < n:
+                there, back = i + side * hop, i - side * (hop - 1)
+                if 0 <= i + side < n and (0 <= there < n or 0 <= back < n):
                     pairs.append((i + side, i))
             got = lax.ppermute(got, "row", pairs) if pairs else None
             slots.append(got)

time: 72.5 us -> 69.8 us (0.963); the launches traced: 71.3 us -> 69.6 us
  waiting for transfers between devices: 26 us -> 13.5 us
  starting transfers between devices: 29.7 us -> 40.5 us
    ppermute x10, starting transfers between devices: 13.9 us -> 26.9 us  [line_gather(): got = lax.ppermute(got, 'row', pairs) if pairs else None]
    ppermute x10, waiting for transfers between devices: 24.8 us -> 12 us  [line_gather(): got = lax.ppermute(got, 'row', pairs) if pairs else None]
    ppermute x9, starting transfers between devices: 15.7 us -> 13.6 us  [src_gather(): lax.ppermute(pieces[distance], 'src', [(i, i ^ bit) for i in range(n)])]
  transfers between devices with their start and end apart: 19 -> 19, of which waited for: 6 -> 5; matrix products, arithmetic and copies ran while one was open for 0% -> 0% of each run, Pallas kernels for 11% -> 12%
where the time goes in v3:
time: 69.8 us; the launch traced here: 69.6 us
  starting transfers between devices  40.5 us (58%)
  Pallas kernels  14.7 us (21%)
  waiting for transfers between devices  13.5 us (19%)
  between operations  0.84 us (1%)
    ppermute x10, starting transfers between devices, line_gather(): got = lax.ppermute(got, 'row', pairs) if pairs else None  26.9 us
    ppermute x9, starting transfers between devices, src_gather(): lax.ppermute(pieces[distance], 'src', [(i, i ^ bit) for i in range(n)])  13.6 us
    ppermute x10, waiting for transfers between devices, line_gather(): got = lax.ppermute(got, 'row', pairs) if pairs else None  12 us
    pallas_call x1, Pallas kernels, stage(): pl.pallas_call(functools.partial(stage_kernel, quarter), out_shape=[jax.S...  2.89 us
    pallas_call x1, Pallas kernels, last(): pl.pallas_call(last_kernel, out_shape=(jax.ShapeDtypeStruct((SN * SNR //...  2.87 us
    pallas_call x1, Pallas kernels, middle(): pl.pallas_call(middle_kernel, out_shape=(jax.ShapeDtypeStruct(((SN - 2) *...  2.45 us
    pallas_call x1, Pallas kernels, first(): pl.pallas_call(functools.partial(first_kernel, n_row, held), out_shape=(j...  2.34 us
    pallas_call x3, Pallas kernels, join(): pl.pallas_call(join_kernel, out_shape=jax.ShapeDtypeStruct(shape, jnp.bfl...  1.78 us
  transfers between devices with their start and end apart: 19, of which 5 were waited for; matrix products, arithmetic and copies ran while one was open for 0% of the time, Pallas kernels for 12%

profile of v3, /device:TPU:1, one launch (start us, length us, event | category | flops | bytes accessed | tf_op | source)
XLA Modules:
  0.0 69.6 jit_solution(5761025561889527843)
XLA Ops:
  0.6 2.9 %stage.1 = (bf16[128,1536]{1,0:T(8,128)(2,1)}, bf16[512,384]{1,0:T(8,128)(2,1)}) custom-call(s32[4]{0:T(128)} %owners.7, s32[4]{0:T(128)} %offsets.3, s32[5,16]{1,0:T(8,128)} %pattern.3, bf16[640,2048]{1,0:T(8,128)(2,1)} %factor.3, bf16[640,384]{1,0:T(8,128)(2,1)} %right.3), custom_call_target="tpu_custom_call" | custom-call | tf_op jit(solution)/shard_map/stage/pallas_call | solution.py:100
  3.5 2.2 %collective-permute-start = (bf16[128,1536]{1,0:T(8,128)(2,1)}, bf16[128,1536]{1,0:T(8,128)(2,1)S(1)}, u32[]{:S(2)}, u32[]{:S(2)}) collective-permute-start(bf16[128,1536]{1,0:T(8,128)(2,1)} %get-tuple-element.14.refs_0_), channel_id=1, source_target_pairs={{4,0},{0,4},{12,8},{8,12},{5,1},{1,5},{13,9},{9,13},{6,2},{2,6},{1... | collective-permute-start | bytes 1179656 | tf_op jit(solution)/shard_map/ppermute | solution.py:31
  5.7 1.2 %collective-permute-start.6 = (bf16[4,128,512]{2,1,0:T(8,128)(2,1)S(1)}, bf16[4,128,512]{2,1,0:T(8,128)(2,1)S(1)}, u32[]{:S(2)}, u32[]{:S(2)}) collective-permute-start(bf16[4,128,512]{2,1,0:T(8,128)(2,1)S(1)} %copy-done.1), channel_id=1, source_target_pairs={{0,2},{1,3},{2,0},{3,1},{4,6},{5,7},{6,4},{7,5},{8,10},{9,11},{10,... | collective-permute-start | bytes 1572872 | tf_op jit(solution)/shard_map/ppermute | solution.py:50
  6.9 0.7 collective-permute-start.3
  7.7 3.9 %collective-permute-start.11 = (bf16[512,384]{1,0:T(8,128)(2,1)}, bf16[512,384]{1,0:T(8,128)(2,1)S(1)}, u32[]{:S(2)}, u32[]{:S(2)}) collective-permute-start(bf16[512,384]{1,0:T(8,128)(2,1)} %get-tuple-element.19.refs_0_), channel_id=1, source_target_pairs={{4,0},{0,4},{12,8},{8,12},{5,1},{1,5},{13,9},{9,13},{6,2},{2,6},{1... | collective-permute-start | bytes 1179656 | tf_op jit(solution)/shard_map/ppermute | solution.py:31
  11.5 3.3 %collective-permute-done.refs_1_ = bf16[128,1536]{1,0:T(8,128)(2,1)S(1)} collective-permute-done((bf16[128,1536]{1,0:T(8,128)(2,1)}, bf16[128,1536]{1,0:T(8,128)(2,1)S(1)}, u32[]{:S(2)}, u32[]{:S(2)}) %collective-permute-start) | collective-permute-done | bytes 393248 | tf_op jit(solution)/shard_map/ppermute | solution.py:31
  14.8 0.7 collective-permute-start.1
  15.5 0.7 collective-permute-start.14
  16.2 2.1 %collective-permute-start.5 = (bf16[4,128,512]{2,1,0:T(8,128)(2,1)S(1)}, bf16[4,128,512]{2,1,0:T(8,128)(2,1)S(1)}, u32[]{:S(2)}, u32[]{:S(2)}) collective-permute-start(bf16[4,128,512]{2,1,0:T(8,128)(2,1)S(1)} %copy-done.1), channel_id=1, source_target_pairs={{0,1},{1,0},{2,3},{3,2},{4,5},{5,4},{6,7},{7,6},{8,9},{9,8},{10,11... | collective-permute-start | bytes 1572872 | tf_op jit(solution)/shard_map/ppermute | solution.py:50
  18.3 1.8 %collective-permute-start.7 = (bf16[4,128,512]{2,1,0:T(8,128)(2,1)S(1)}, bf16[4,128,512]{2,1,0:T(8,128)(2,1)S(1)}, u32[]{:S(2)}, u32[]{:S(2)}) collective-permute-start(bf16[4,128,512]{2,1,0:T(8,128)(2,1)S(1)} %collective-permute-done.6.refs_2_), channel_id=1, source_target_pairs={{0,1},{1,0},{2,3},{3,2},{4,5},{5,4},{6,7},{7,6},{8,9},{9,8},{10,11... | collective-permute-start | bytes 1572872 | tf_op jit(solution)/shard_map/ppermute | solution.py:50
  20.1 3.1 %collective-permute-done.11.refs_1_ = bf16[512,384]{1,0:T(8,128)(2,1)S(1)} collective-permute-done((bf16[512,384]{1,0:T(8,128)(2,1)}, bf16[512,384]{1,0:T(8,128)(2,1)S(1)}, u32[]{:S(2)}, u32[]{:S(2)}) %collective-permute-start.11) | collective-permute-done | bytes 393248 | tf_op jit(solution)/shard_map/ppermute | solution.py:31
  23.2 1.4 %collective-permute-start.4 = (bf16[128,1536]{1,0:T(8,128)(2,1)S(1)}, bf16[128,1536]{1,0:T(8,128)(2,1)S(1)}, u32[]{:S(2)}, u32[]{:S(2)}) collective-permute-start(bf16[128,1536]{1,0:T(8,128)(2,1)S(1)} %collective-permute-done.3.refs_4_), channel_id=1, source_target_pairs={{4,0},{0,4},{12,8},{8,12},{5,1},{1,5},{13,9},{9,13},{6,2},{2,6},{1... | collective-permute-start | bytes 1179656 | tf_op jit(solution)/shard_map/ppermute | solution.py:31
  24.6 2.7 %collective-permute-start.2 = (bf16[128,1536]{1,0:T(8,128)(2,1)S(1)}, bf16[128,1536]{1,0:T(8,128)(2,1)S(1)}, u32[]{:S(2)}, u32[]{:S(2)}) collective-permute-start(bf16[128,1536]{1,0:T(8,128)(2,1)S(1)} %collective-permute-done.1.refs_2_), channel_id=1, source_target_pairs={{4,0},{0,4},{12,8},{8,12},{5,1},{1,5},{13,9},{9,13},{6,2},{2,6},{1... | collective-permute-start | bytes 1179656 | tf_op jit(solution)/shard_map/ppermute | solution.py:31
  27.3 0.7 collective-permute-start.12
  28.0 11.3 %collective-permute-start.15 = (bf16[512,384]{1,0:T(8,128)(2,1)S(1)}, bf16[512,384]{1,0:T(8,128)(2,1)S(1)}, u32[]{:S(2)}, u32[]{:S(2)}) collective-permute-start(bf16[512,384]{1,0:T(8,128)(2,1)S(1)} %collective-permute-done.14.refs_4_), channel_id=1, source_target_pairs={{4,0},{0,4},{12,8},{8,12},{5,1},{1,5},{13,9},{9,13},{6,2},{2,6},{1... | collective-permute-start | bytes 1179656 | tf_op jit(solution)/shard_map/ppermute | solution.py:31
  39.3 0.2 join.3.inverse
  39.6 1.5 %collective-permute-done.2.refs_3_ = bf16[128,1536]{1,0:T(8,128)(2,1)S(1)} collective-permute-done((bf16[128,1536]{1,0:T(8,128)(2,1)S(1)}, bf16[128,1536]{1,0:T(8,128)(2,1)S(1)}, u32[]{:S(2)}, u32[]{:S(2)}) %collective-permute-start.2) | collective-permute-done | bytes 393248 | tf_op jit(solution)/shard_map/ppermute | solution.py:31
  41.0 0.9 %pick.1 = (bf16[128,1536]{1,0:T(8,128)(2,1)S(1)}, bf16[128,1536]{1,0:T(8,128)(2,1)S(1)}) custom-call(s32[4]{0:T(128)S(1)} %copy-done.5, bf16[128,1536]{1,0:T(8,128)(2,1)S(1)} %copy-done.3, bf16[128,1536]{1,0:T(8,128)(2,1)S(1)} %collective-permute-done.refs_1_, bf16[128,1536]{1,0:T(8,128)(2,1)S(1)} %collective-permute-done.1.refs_2_, ...), custom_call_target="tpu_custom_call" | custom-call | tf_op jit(solution)/shard_map/pick/pallas_call | solution.py:134
  42.0 1.0 %collective-permute-start.17 = (bf16[128,1536]{1,0:T(8,128)(2,1)S(1)}, bf16[128,1536]{1,0:T(8,128)(2,1)S(1)}, u32[]{:S(2)}, u32[]{:S(2)}) collective-permute-start(bf16[128,1536]{1,0:T(8,128)(2,1)S(1)} %get-tuple-element.22.refs_0_), channel_id=1, source_target_pairs={{0,2},{1,3},{2,0},{3,1},{4,6},{5,7},{6,4},{7,5},{8,10},{9,11},{10,... | collective-permute-start | bytes 1179656 | tf_op jit(solution)/shard_map/ppermute | solution.py:50
  43.0 2.7 %collective-permute-start.13 = (bf16[512,384]{1,0:T(8,128)(2,1)S(1)}, bf16[512,384]{1,0:T(8,128)(2,1)S(1)}, u32[]{:S(2)}, u32[]{:S(2)}) collective-permute-start(bf16[512,384]{1,0:T(8,128)(2,1)S(1)} %collective-permute-done.12.refs_2_), channel_id=1, source_target_pairs={{4,0},{0,4},{12,8},{8,12},{5,1},{1,5},{13,9},{9,13},{6,2},{2,6},{1... | collective-permute-start | bytes 1179656 | tf_op jit(solution)/shard_map/ppermute | solution.py:31
  45.7 1.4 %mask.1.masked = bf16[640,2048]{1,0:T(8,128)(2,1)S(1)} custom-call(s32[4]{0:T(128)S(1)} %copy-done.5, s32[4]{0:T(128)S(1)} %copy-done.6, s32[5,16]{1,0:T(8,128)S(1)} %copy-done.4, bf16[640,2048]{1,0:T(8,128)(2,1)S(1)} %copy-done), custom_call_target="tpu_custom_call" | custom-call | tf_op jit(solution)/shard_map/mask/pallas_call | solution.py:187
  47.1 3.9 %collective-permute-start.16 = (bf16[128,1536]{1,0:T(8,128)(2,1)S(1)}, bf16[128,1536]{1,0:T(8,128)(2,1)S(1)}, u32[]{:S(2)}, u32[]{:S(2)}) collective-permute-start(bf16[128,1536]{1,0:T(8,128)(2,1)S(1)} %get-tuple-element.22.refs_0_), channel_id=1, source_target_pairs={{0,1},{1,0},{2,3},{3,2},{4,5},{5,4},{6,7},{7,6},{8,9},{9,8},{10,11... | collective-permute-start | bytes 1179656 | tf_op jit(solution)/shard_map/ppermute | solution.py:50
  51.1 2.3 %collective-permute-start.8 = (bf16[128,1536]{1,0:T(8,128)(2,1)S(1)}, bf16[128,1536]{1,0:T(8,128)(2,1)S(1)}, u32[]{:S(2)}, u32[]{:S(2)}) collective-permute-start(bf16[128,1536]{1,0:T(8,128)(2,1)S(1)} %get-tuple-element.18.refs_0_), channel_id=1, source_target_pairs={{0,1},{1,0},{2,3},{3,2},{4,5},{5,4},{6,7},{7,6},{8,9},{9,8},{10,11... | collective-permute-start | bytes 1179656 | tf_op jit(solution)/shard_map/ppermute | solution.py:50
  53.3 0.4 collective-permute-start.18
  53.8 4.1 %collective-permute-done.13.refs_3_ = bf16[512,384]{1,0:T(8,128)(2,1)S(1)} collective-permute-done((bf16[512,384]{1,0:T(8,128)(2,1)S(1)}, bf16[512,384]{1,0:T(8,128)(2,1)S(1)}, u32[]{:S(2)}, u32[]{:S(2)}) %collective-permute-start.13) | collective-permute-done | bytes 393248 | tf_op jit(solution)/shard_map/ppermute | solution.py:31
  57.9 2.3 %first.1 = (bf16[3,512,384]{2,1,0:T(8,128)(2,1)S(1)}, bf16[512,384]{1,0:T(8,128)(2,1)S(1)}, f32[640,384]{1,0:T(8,128)S(1)}) custom-call(s32[4]{0:T(128)S(1)} %copy-done.5, bf16[4,512,512]{2,1,0:T(8,128)(2,1)S(1)} %join.3.inverse, bf16[640,2048]{1,0:T(8,128)(2,1)S(1)} %mask.1.masked, bf16[640,384]{1,0:T(8,128)(2,1)S(1)} %copy-done.2, ...), custom_call_target="tpu_custom_call" | custom-call | flops 60000002048 | tf_op jit(solution)/shard_map/first/pallas_call | solution.py:219
  60.2 1.5 %collective-permute-done.9.refs_2_ = bf16[128,1536]{1,0:T(8,128)(2,1)S(1)} collective-permute-done((bf16[128,1536]{1,0:T(8,128)(2,1)S(1)}, bf16[128,1536]{1,0:T(8,128)(2,1)S(1)}, u32[]{:S(2)}, u32[]{:S(2)}) %collective-permute-start.9) | collective-permute-done | bytes 393248 | tf_op jit(solution)/shard_map/ppermute | solution.py:50
  61.8 0.8 %collective-permute-start.10 = (bf16[128,1536]{1,0:T(8,128)(2,1)S(1)}, bf16[128,1536]{1,0:T(8,128)(2,1)S(1)}, u32[]{:S(2)}, u32[]{:S(2)}) collective-permute-start(bf16[128,1536]{1,0:T(8,128)(2,1)S(1)} %collective-permute-done.9.refs_2_), channel_id=1, source_target_pairs={{0,1},{1,0},{2,3},{3,2},{4,5},{5,4},{6,7},{7,6},{8,9},{9,8},{10,11... | collective-permute-start | bytes 1179656 | tf_op jit(solution)/shard_map/ppermute | solution.py:50
  62.6 0.8 %join.5.near = bf16[512,1536]{1,0:T(8,128)(2,1)S(1)} custom-call(bf16[128,1536]{1,0:T(8,128)(2,1)S(1)} %get-tuple-element.22.refs_0_, bf16[128,1536]{1,0:T(8,128)(2,1)S(1)} %collective-permute-done.16.refs_1_, bf16[128,1536]{1,0:T(8,128)(2,1)S(1)} %collective-permute-done.17.refs_2_, bf16[128,1536]{1,0:T(8,128)(2,1)S(1)} %collective-permute-done.18.refs_3_), custom_call_target="tpu_custom_call" | custom-call | tf_op jit(solution)/shard_map/join/pallas_call | solution.py:161
  63.4 2.4 %middle.1 = (bf16[1024,384]{1,0:T(8,128)(2,1)S(1)}, f32[640,384]{1,0:T(8,128)S(1)}) custom-call(bf16[4,512,512]{2,1,0:T(8,128)(2,1)S(1)} %join.3.inverse, bf16[512,1536]{1,0:T(8,128)(2,1)S(1)} %join.5.near, bf16[640,2048]{1,0:T(8,128)(2,1)S(1)} %mask.1.masked, bf16[3,512,384]{2,1,0:T(8,128)(2,1)S(1)} %get-tuple-element.20.segments, ...), custom_call_target="tpu_custom_call" | custom-call | flops 24000000000 | tf_op jit(solution)/shard_map/middle/pallas_call | solution.py:258
  65.9 0.8 %join.4.far = bf16[512,1536]{1,0:T(8,128)(2,1)S(1)} custom-call(bf16[128,1536]{1,0:T(8,128)(2,1)S(1)} %get-tuple-element.18.refs_0_, bf16[128,1536]{1,0:T(8,128)(2,1)S(1)} %collective-permute-done.8.refs_1_, bf16[128,1536]{1,0:T(8,128)(2,1)S(1)} %collective-permute-done.9.refs_2_, bf16[128,1536]{1,0:T(8,128)(2,1)S(1)} %collective-permute-done.10.refs_3_), custom_call_target="tpu_custom_call" | custom-call | tf_op jit(solution)/shard_map/join/pallas_call | solution.py:161
  66.7 2.9 %last.1 = (bf16[512,384]{1,0:T(8,128)(2,1)}, bf16[640,384]{1,0:T(8,128)(2,1)}) custom-call(bf16[4,512,512]{2,1,0:T(8,128)(2,1)S(1)} %join.3.inverse, bf16[512,1536]{1,0:T(8,128)(2,1)S(1)} %join.4.far, bf16[640,2048]{1,0:T(8,128)(2,1)S(1)} %mask.1.masked, bf16[3,512,384]{2,1,0:T(8,128)(2,1)S(1)} %get-tuple-element.20.segments, ...), custom_call_target="tpu_custom_call" | custom-call | tf_op jit(solution)/shard_map/last/pallas_call | solution.py:303
  (31 shorter events, 0.1 us)
Async XLA Ops:
  0.6 5.1 %copy-start.1 = (bf16[4,128,512]{2,1,0:T(8,128)(2,1)S(1)}, bf16[4,128,512]{2,1,0:T(8,128)(2,1)}, u32[]{:S(2)}) copy-start(bf16[4,128,512]{2,1,0:T(8,128)(2,1)} %refs_0_.1) | copy-start | bytes 1572868
  3.5 11.2 %collective-permute-start = (bf16[128,1536]{1,0:T(8,128)(2,1)}, bf16[128,1536]{1,0:T(8,128)(2,1)S(1)}, u32[]{:S(2)}, u32[]{:S(2)}) collective-permute-start(bf16[128,1536]{1,0:T(8,128)(2,1)} %get-tuple-element.14.refs_0_), channel_id=1, source_target_pairs={{4,0},{0,4},{12,8},{8,12},{5,1},{1,5},{13,9},{9,13},{6,2},{2,6},{1... | collective-permute-start | bytes 1179656 | tf_op jit(solution)/shard_map/ppermute | solution.py:31
  5.7 12.6 %collective-permute-start.6 = (bf16[4,128,512]{2,1,0:T(8,128)(2,1)S(1)}, bf16[4,128,512]{2,1,0:T(8,128)(2,1)S(1)}, u32[]{:S(2)}, u32[]{:S(2)}) collective-permute-start(bf16[4,128,512]{2,1,0:T(8,128)(2,1)S(1)} %copy-done.1), channel_id=1, source_target_pairs={{0,2},{1,3},{2,0},{3,1},{4,6},{5,7},{6,4},{7,5},{8,10},{9,11},{10,... | collective-permute-start | bytes 1572872 | tf_op jit(solution)/shard_map/ppermute | solution.py:50
  6.9 9.2 %collective-permute-start.3 = (bf16[128,1536]{1,0:T(8,128)(2,1)}, bf16[128,1536]{1,0:T(8,128)(2,1)S(1)}, u32[]{:S(2)}, u32[]{:S(2)}) collective-permute-start(bf16[128,1536]{1,0:T(8,128)(2,1)} %get-tuple-element.14.refs_0_), channel_id=1, source_target_pairs={{8,4},{4,8},{9,5},{5,9},{10,6},{6,10},{11,7},{7,11},{24,20},{20,24... | collective-permute-start | bytes 1179656 | tf_op jit(solution)/shard_map/ppermute | solution.py:31
  7.6 33.4 %copy-start.3 = (bf16[128,1536]{1,0:T(8,128)(2,1)S(1)}, bf16[128,1536]{1,0:T(8,128)(2,1)}, u32[]{:S(2)}) copy-start(bf16[128,1536]{1,0:T(8,128)(2,1)} %get-tuple-element.14.refs_0_) | copy-start | bytes 1179652
  7.6 33.4 %copy-start.5 = (s32[4]{0:T(128)S(1)}, s32[4]{0:T(128)}, u32[]{:S(2)}) copy-start(s32[4]{0:T(128)} %owners.7) | copy-start | bytes 52
  7.7 15.6 %collective-permute-start.11 = (bf16[512,384]{1,0:T(8,128)(2,1)}, bf16[512,384]{1,0:T(8,128)(2,1)S(1)}, u32[]{:S(2)}, u32[]{:S(2)}) collective-permute-start(bf16[512,384]{1,0:T(8,128)(2,1)} %get-tuple-element.19.refs_0_), channel_id=1, source_target_pairs={{4,0},{0,4},{12,8},{8,12},{5,1},{1,5},{13,9},{9,13},{6,2},{2,6},{1... | collective-permute-start | bytes 1179656 | tf_op jit(solution)/shard_map/ppermute | solution.py:31
  14.8 9.9 %collective-permute-start.1 = (bf16[128,1536]{1,0:T(8,128)(2,1)S(1)}, bf16[128,1536]{1,0:T(8,128)(2,1)S(1)}, u32[]{:S(2)}, u32[]{:S(2)}) collective-permute-start(bf16[128,1536]{1,0:T(8,128)(2,1)S(1)} %collective-permute-done.refs_1_), channel_id=1, source_target_pairs={{8,4},{4,8},{9,5},{5,9},{10,6},{6,10},{11,7},{7,11},{24,20},{20,24... | collective-permute-start | bytes 1179656 | tf_op jit(solution)/shard_map/ppermute | solution.py:31
  15.5 11.9 %collective-permute-start.14 = (bf16[512,384]{1,0:T(8,128)(2,1)}, bf16[512,384]{1,0:T(8,128)(2,1)S(1)}, u32[]{:S(2)}, u32[]{:S(2)}) collective-permute-start(bf16[512,384]{1,0:T(8,128)(2,1)} %get-tuple-element.19.refs_0_), channel_id=1, source_target_pairs={{8,4},{4,8},{9,5},{5,9},{10,6},{6,10},{11,7},{7,11},{24,20},{20,24... | collective-permute-start | bytes 1179656 | tf_op jit(solution)/shard_map/ppermute | solution.py:31
  16.2 11.8 %collective-permute-start.5 = (bf16[4,128,512]{2,1,0:T(8,128)(2,1)S(1)}, bf16[4,128,512]{2,1,0:T(8,128)(2,1)S(1)}, u32[]{:S(2)}, u32[]{:S(2)}) collective-permute-start(bf16[4,128,512]{2,1,0:T(8,128)(2,1)S(1)} %copy-done.1), channel_id=1, source_target_pairs={{0,1},{1,0},{2,3},{3,2},{4,5},{5,4},{6,7},{7,6},{8,9},{9,8},{10,11... | collective-permute-start | bytes 1572872 | tf_op jit(solution)/shard_map/ppermute | solution.py:50
  18.3 21.0 %collective-permute-start.7 = (bf16[4,128,512]{2,1,0:T(8,128)(2,1)S(1)}, bf16[4,128,512]{2,1,0:T(8,128)(2,1)S(1)}, u32[]{:S(2)}, u32[]{:S(2)}) collective-permute-start(bf16[4,128,512]{2,1,0:T(8,128)(2,1)S(1)} %collective-permute-done.6.refs_2_), channel_id=1, source_target_pairs={{0,1},{1,0},{2,3},{3,2},{4,5},{5,4},{6,7},{7,6},{8,9},{9,8},{10,11... | collective-permute-start | bytes 1572872 | tf_op jit(solution)/shard_map/ppermute | solution.py:50
  23.2 16.3 %collective-permute-start.4 = (bf16[128,1536]{1,0:T(8,128)(2,1)S(1)}, bf16[128,1536]{1,0:T(8,128)(2,1)S(1)}, u32[]{:S(2)}, u32[]{:S(2)}) collective-permute-start(bf16[128,1536]{1,0:T(8,128)(2,1)S(1)} %collective-permute-done.3.refs_4_), channel_id=1, source_target_pairs={{4,0},{0,4},{12,8},{8,12},{5,1},{1,5},{13,9},{9,13},{6,2},{2,6},{1... | collective-permute-start | bytes 1179656 | tf_op jit(solution)/shard_map/ppermute | solution.py:31
  24.6 16.4 %collective-permute-start.2 = (bf16[128,1536]{1,0:T(8,128)(2,1)S(1)}, bf16[128,1536]{1,0:T(8,128)(2,1)S(1)}, u32[]{:S(2)}, u32[]{:S(2)}) collective-permute-start(bf16[128,1536]{1,0:T(8,128)(2,1)S(1)} %collective-permute-done.1.refs_2_), channel_id=1, source_target_pairs={{4,0},{0,4},{12,8},{8,12},{5,1},{1,5},{13,9},{9,13},{6,2},{2,6},{1... | collective-permute-start | bytes 1179656 | tf_op jit(solution)/shard_map/ppermute | solution.py:31
  27.3 15.7 %collective-permute-start.12 = (bf16[512,384]{1,0:T(8,128)(2,1)S(1)}, bf16[512,384]{1,0:T(8,128)(2,1)S(1)}, u32[]{:S(2)}, u32[]{:S(2)}) collective-permute-start(bf16[512,384]{1,0:T(8,128)(2,1)S(1)} %collective-permute-done.11.refs_1_), channel_id=1, source_target_pairs={{8,4},{4,8},{9,5},{5,9},{10,6},{6,10},{11,7},{7,11},{24,20},{20,24... | collective-permute-start | bytes 1179656 | tf_op jit(solution)/shard_map/ppermute | solution.py:31
  28.0 23.1 %collective-permute-start.15 = (bf16[512,384]{1,0:T(8,128)(2,1)S(1)}, bf16[512,384]{1,0:T(8,128)(2,1)S(1)}, u32[]{:S(2)}, u32[]{:S(2)}) collective-permute-start(bf16[512,384]{1,0:T(8,128)(2,1)S(1)} %collective-permute-done.14.refs_4_), channel_id=1, source_target_pairs={{4,0},{0,4},{12,8},{8,12},{5,1},{1,5},{13,9},{9,13},{6,2},{2,6},{1... | collective-permute-start | bytes 1179656 | tf_op jit(solution)/shard_map/ppermute | solution.py:31
  39.3 6.4 %copy-start = (bf16[640,2048]{1,0:T(8,128)(2,1)S(1)}, bf16[640,2048]{1,0:T(8,128)(2,1)}, u32[]{:S(2)}) copy-start(bf16[640,2048]{1,0:T(8,128)(2,1)} %factor.3) | copy-start | bytes 7864324
  39.5 6.2 %copy-start.4 = (s32[5,16]{1,0:T(8,128)S(1)}, s32[5,16]{1,0:T(8,128)}, u32[]{:S(2)}) copy-start(s32[5,16]{1,0:T(8,128)} %pattern.3) | copy-start | bytes 964
  39.5 6.2 %copy-start.6 = (s32[4]{0:T(128)S(1)}, s32[4]{0:T(128)}, u32[]{:S(2)}) copy-start(s32[4]{0:T(128)} %offsets.3) | copy-start | bytes 52
  42.0 15.9 %copy-start.2 = (bf16[640,384]{1,0:T(8,128)(2,1)S(1)}, bf16[640,384]{1,0:T(8,128)(2,1)}, u32[]{:S(2)}) copy-start(bf16[640,384]{1,0:T(8,128)(2,1)} %right.3) | copy-start | bytes 1474564
  42.0 15.9 %copy-start.7 = (bf16[512,384]{1,0:T(8,128)(2,1)S(1)}, bf16[512,384]{1,0:T(8,128)(2,1)}, u32[]{:S(2)}) copy-start(bf16[512,384]{1,0:T(8,128)(2,1)} %get-tuple-element.19.refs_0_) | copy-start | bytes 1179652
  42.0 11.4 %collective-permute-start.17 = (bf16[128,1536]{1,0:T(8,128)(2,1)S(1)}, bf16[128,1536]{1,0:T(8,128)(2,1)S(1)}, u32[]{:S(2)}, u32[]{:S(2)}) collective-permute-start(bf16[128,1536]{1,0:T(8,128)(2,1)S(1)} %get-tuple-element.22.refs_0_), channel_id=1, source_target_pairs={{0,2},{1,3},{2,0},{3,1},{4,6},{5,7},{6,4},{7,5},{8,10},{9,11},{10,... | collective-permute-start | bytes 1179656 | tf_op jit(solution)/shard_map/ppermute | solution.py:50
  43.0 14.9 %collective-permute-start.13 = (bf16[512,384]{1,0:T(8,128)(2,1)S(1)}, bf16[512,384]{1,0:T(8,128)(2,1)S(1)}, u32[]{:S(2)}, u32[]{:S(2)}) collective-permute-start(bf16[512,384]{1,0:T(8,128)(2,1)S(1)} %collective-permute-done.12.refs_2_), channel_id=1, source_target_pairs={{4,0},{0,4},{12,8},{8,12},{5,1},{1,5},{13,9},{9,13},{6,2},{2,6},{1... | collective-permute-start | bytes 1179656 | tf_op jit(solution)/shard_map/ppermute | solution.py:31
  47.1 15.5 %collective-permute-start.16 = (bf16[128,1536]{1,0:T(8,128)(2,1)S(1)}, bf16[128,1536]{1,0:T(8,128)(2,1)S(1)}, u32[]{:S(2)}, u32[]{:S(2)}) collective-permute-start(bf16[128,1536]{1,0:T(8,128)(2,1)S(1)} %get-tuple-element.22.refs_0_), channel_id=1, source_target_pairs={{0,1},{1,0},{2,3},{3,2},{4,5},{5,4},{6,7},{7,6},{8,9},{9,8},{10,11... | collective-permute-start | bytes 1179656 | tf_op jit(solution)/shard_map/ppermute | solution.py:50
  51.1 10.7 %collective-permute-start.9 = (bf16[128,1536]{1,0:T(8,128)(2,1)S(1)}, bf16[128,1536]{1,0:T(8,128)(2,1)S(1)}, u32[]{:S(2)}, u32[]{:S(2)}) collective-permute-start(bf16[128,1536]{1,0:T(8,128)(2,1)S(1)} %get-tuple-element.18.refs_0_), channel_id=1, source_target_pairs={{0,2},{1,3},{2,0},{3,1},{4,6},{5,7},{6,4},{7,5},{8,10},{9,11},{10,... | collective-permute-start | bytes 1179656 | tf_op jit(solution)/shard_map/ppermute | solution.py:50
  51.1 14.8 %collective-permute-start.8 = (bf16[128,1536]{1,0:T(8,128)(2,1)S(1)}, bf16[128,1536]{1,0:T(8,128)(2,1)S(1)}, u32[]{:S(2)}, u32[]{:S(2)}) collective-permute-start(bf16[128,1536]{1,0:T(8,128)(2,1)S(1)} %get-tuple-element.18.refs_0_), channel_id=1, source_target_pairs={{0,1},{1,0},{2,3},{3,2},{4,5},{5,4},{6,7},{7,6},{8,9},{9,8},{10,11... | collective-permute-start | bytes 1179656 | tf_op jit(solution)/shard_map/ppermute | solution.py:50
  53.3 9.3 %collective-permute-start.18 = (bf16[128,1536]{1,0:T(8,128)(2,1)S(1)}, bf16[128,1536]{1,0:T(8,128)(2,1)S(1)}, u32[]{:S(2)}, u32[]{:S(2)}) collective-permute-start(bf16[128,1536]{1,0:T(8,128)(2,1)S(1)} %collective-permute-done.17.refs_2_), channel_id=1, source_target_pairs={{0,1},{1,0},{2,3},{3,2},{4,5},{5,4},{6,7},{7,6},{8,9},{9,8},{10,11... | collective-permute-start | bytes 1179656 | tf_op jit(solution)/shard_map/ppermute | solution.py:50
  61.8 4.1 %collective-permute-start.10 = (bf16[128,1536]{1,0:T(8,128)(2,1)S(1)}, bf16[128,1536]{1,0:T(8,128)(2,1)S(1)}, u32[]{:S(2)}, u32[]{:S(2)}) collective-permute-start(bf16[128,1536]{1,0:T(8,128)(2,1)S(1)} %collective-permute-done.9.refs_2_), channel_id=1, source_target_pairs={{0,1},{1,0},{2,3},{3,2},{4,5},{5,4},{6,7},{7,6},{8,9},{9,8},{10,11... | collective-permute-start | bytes 1179656 | tf_op jit(solution)/shard_map/ppermute | solution.py:50

commit v4 on v3

--- a/solution.py
+++ b/solution.py
@@ -142,14 +142,21 @@
     )(owners, *(slot for slot in slots if slot is not None))
 
 
-def join_kernel(*refs):
-    *pieces, whole, sems = refs
+def join_copies(pieces, whole, sems, cols=None):
     me, quarter = lax.axis_index("src"), SNR // len(pieces)
     copies = []
     for d, piece in enumerate(pieces):
         rows = pl.ds(pl.multiple_of(jnp.bitwise_xor(me, d) * quarter, quarter), quarter)
         place = whole.at[rows] if len(whole.shape) == 2 else whole.at[:, rows]
+        if cols is not None:
+            piece, place = piece.at[:, cols], whole.at[rows, cols]
         copies.append(pltpu.make_async_copy(piece, place, sems.at[d]))
+    return copies
+
+
+def join_kernel(*refs):
+    *pieces, whole, sems = refs
+    copies = join_copies(pieces, whole, sems)
     for copy in copies:
         copy.start()
     for copy in copies:
@@ -235,9 +242,21 @@
     )(owners, inverse, masked, right, *(slot for slot in slots if slot is not None))
 
 
-def middle_kernel(inverse, near, masked, segments, start, before, solutions, total):
+def middle_kernel(inverse, masked, segments, start, before, *refs):
+    *pieces, solutions, total, near, sems = refs
+    copies = {
+        node: join_copies(
+            pieces, near, sems.at[node - 1], pl.ds(node * (node - 1) // 2 * SNR, node * SNR)
+        )
+        for node in range(1, SN - 1)
+    }
+    for node in copies:
+        for copy in copies[node]:
+            copy.start()
     left = before[...]
     for node in range(1, SN - 1):
+        for copy in copies[node]:
+            copy.wait()
         at = node * (node - 1) // 2 * SNR
         update = jnp.dot(near[:, at : at + SNR], start[...], preferred_element_type=jnp.float32)
         if node > 1:
@@ -261,15 +280,23 @@
             jax.ShapeDtypeStruct(((SN - 2) * SNR, columns), jnp.bfloat16),
             jax.ShapeDtypeStruct(total.shape, jnp.float32),
         ),
-        in_specs=[VMEM] * 6,
+        in_specs=[VMEM] * 5 + [ANY] * len(near),
         out_specs=(VMEM, VMEM),
+        scratch_shapes=[pltpu.VMEM((SNR, near[0].shape[1]), jnp.bfloat16), pltpu.SemaphoreType.DMA((SN - 2, len(near)))],
         compiler_params=PARAMS,
         cost_estimate=pl.CostEstimate(flops=24 * 10**9, bytes_accessed=0, transcendentals=0),
         name="middle",
-    )(inverse, near, masked, segments, start, total)
-
-
-def last_kernel(inverse, far, masked, segments, start, solutions, total, solved, updated, xs, out, sems):
+    )(inverse, masked, segments, start, total, *near)
+
+
+def last_kernel(inverse, masked, segments, start, solutions, total, *refs):
+    *pieces, solved, updated, far, xs, out, sems, far_sems = refs
+    copies = [
+        join_copies(pieces, far, far_sems.at[i], cols)
+        for i, cols in enumerate((pl.ds(0, SNR), pl.ds(SNR, LEFT - SNR)))
+    ]
+    for copy in copies[0] + copies[1]:
+        copy.start()
     position = lax.axis_index("row")
     last = (SN - 1) * SNR
     moves = [
@@ -278,7 +305,11 @@
     ]
     for move in moves:
         move.start()
+    for copy in copies[0]:
+        copy.wait()
     update = jnp.dot(far[:, :SNR], start[...], preferred_element_type=jnp.float32)
+    for copy in copies[1]:
+        copy.wait()
     update += jnp.dot(far[:, SNR:], solutions[...], preferred_element_type=jnp.float32)
     segment = (segments[SN - 2].astype(jnp.float32) - update).astype(jnp.bfloat16)
     x = jnp.dot(inverse[SN - 1], segment, preferred_element_type=jnp.float32).astype(jnp.bfloat16)
@@ -306,16 +337,18 @@
             jax.ShapeDtypeStruct((SN * SNR // n_row, columns), jnp.bfloat16),
             jax.ShapeDtypeStruct((rows, columns), jnp.bfloat16),
         ),
-        in_specs=[VMEM] * 7,
+        in_specs=[VMEM] * 6 + [ANY] * len(far),
         out_specs=(ANY, ANY),
         scratch_shapes=[
+            pltpu.VMEM((SNR, LEFT), jnp.bfloat16),
             pltpu.VMEM((SN * SNR, columns), jnp.bfloat16),
             pltpu.VMEM((rows, columns), jnp.bfloat16),
             pltpu.SemaphoreType.DMA((2,)),
+            pltpu.SemaphoreType.DMA((2, len(far))),
         ],
         compiler_params=PARAMS,
         name="last",
-    )(inverse, far, masked, segments, start, solutions, total)
+    )(inverse, masked, segments, start, solutions, total, *far)
 
 
 def on_device(right_side, factor, pattern, inverses, owners, offsets):
@@ -325,7 +358,7 @@
     inverse = join(src_gather(inverses, n_src))
     near, far = pick(owners, pieces, n_row)
     near, far, inverse = lax.optimization_barrier((near, far, inverse))
-    near, far = join(src_gather(near, n_src)), join(src_gather(far, n_src))
+    near, far = src_gather(near, n_src), src_gather(far, n_src)
     masked = mask(owners, offsets, pattern, factor)
     slots = line_gather(segment, n_row)
     segments, start, total = first(owners, inverse, masked, right_side, slots, n_row)

time: 69.8 us -> 68.8 us (0.986)
  Pallas kernels: 14.7 us -> 13.7 us
    pallas_call x3 -> x1, Pallas kernels: 1.78 us -> 0.18 us  [join(): pl.pallas_call(join_kernel, out_shape=jax.ShapeDtypeStruct(shape, jnp.bfl...]
  transfers between devices with their start and end apart: 19 -> 19, of which waited for: 5 -> 5; matrix products, arithmetic and copies ran while one was open for 0% -> 0% of each run, Pallas kernels for 12% -> 11%
where the time goes in v4:
time: 68.8 us; the launch traced here: 68.6 us
  starting transfers between devices  40.5 us (59%)
  Pallas kernels  13.7 us (20%)
  waiting for transfers between devices  13.5 us (20%)
  between operations  0.83 us (1%)
    ppermute x10, starting transfers between devices, line_gather(): got = lax.ppermute(got, 'row', pairs) if pairs else None  26.9 us
    ppermute x9, starting transfers between devices, src_gather(): lax.ppermute(pieces[distance], 'src', [(i, i ^ bit) for i in range(n)])  13.6 us
    ppermute x10, waiting for transfers between devices, line_gather(): got = lax.ppermute(got, 'row', pairs) if pairs else None  12 us
    pallas_call x1, Pallas kernels, last(): pl.pallas_call(last_kernel, out_shape=(jax.ShapeDtypeStruct((SN * SNR //...  3.15 us
    pallas_call x1, Pallas kernels, stage(): pl.pallas_call(functools.partial(stage_kernel, quarter), out_shape=[jax.S...  2.89 us
    pallas_call x1, Pallas kernels, middle(): pl.pallas_call(middle_kernel, out_shape=(jax.ShapeDtypeStruct(((SN - 2) *...  2.77 us
    pallas_call x1, Pallas kernels, first(): pl.pallas_call(functools.partial(first_kernel, n_row, held), out_shape=(j...  2.34 us
    ppermute x9, waiting for transfers between devices, src_gather(): lax.ppermute(pieces[distance], 'src', [(i, i ^ bit) for i in range(n)])  1.55 us
  transfers between devices with their start and end apart: 19, of which 5 were waited for; matrix products, arithmetic and copies ran while one was open for 0% of the time, Pallas kernels for 11%

profile of v4, /device:TPU:1, one launch (start us, length us, event | category | flops | bytes accessed | tf_op | source)
XLA Modules:
  0.0 68.6 jit_solution(17340473227258426189)
XLA Ops:
  0.6 2.9 %stage.1 = (bf16[128,1536]{1,0:T(8,128)(2,1)}, bf16[512,384]{1,0:T(8,128)(2,1)}) custom-call(s32[4]{0:T(128)} %owners.7, s32[4]{0:T(128)} %offsets.3, s32[5,16]{1,0:T(8,128)} %pattern.3, bf16[640,2048]{1,0:T(8,128)(2,1)} %factor.3, bf16[640,384]{1,0:T(8,128)(2,1)} %right.3), custom_call_target="tpu_custom_call" | custom-call | tf_op jit(solution)/shard_map/stage/pallas_call | solution.py:100
  3.5 0.0 copy-start.3
  3.6 2.2 %collective-permute-start = (bf16[128,1536]{1,0:T(8,128)(2,1)}, bf16[128,1536]{1,0:T(8,128)(2,1)S(1)}, u32[]{:S(2)}, u32[]{:S(2)}) collective-permute-start(bf16[128,1536]{1,0:T(8,128)(2,1)} %get-tuple-element.14.refs_0_), channel_id=1, source_target_pairs={{4,0},{0,4},{12,8},{8,12},{5,1},{1,5},{13,9},{9,13},{6,2},{2,6},{1... | collective-permute-start | bytes 1179656 | tf_op jit(solution)/shard_map/ppermute | solution.py:31
  5.8 1.2 %collective-permute-start.6 = (bf16[4,128,512]{2,1,0:T(8,128)(2,1)S(1)}, bf16[4,128,512]{2,1,0:T(8,128)(2,1)S(1)}, u32[]{:S(2)}, u32[]{:S(2)}) collective-permute-start(bf16[4,128,512]{2,1,0:T(8,128)(2,1)S(1)} %copy-done.1), channel_id=1, source_target_pairs={{0,2},{1,3},{2,0},{3,1},{4,6},{5,7},{6,4},{7,5},{8,10},{9,11},{10,... | collective-permute-start | bytes 1572872 | tf_op jit(solution)/shard_map/ppermute | solution.py:50
  7.0 0.7 collective-permute-start.3
  7.7 0.0 copy-start
  7.7 3.9 %collective-permute-start.8 = (bf16[512,384]{1,0:T(8,128)(2,1)}, bf16[512,384]{1,0:T(8,128)(2,1)S(1)}, u32[]{:S(2)}, u32[]{:S(2)}) collective-permute-start(bf16[512,384]{1,0:T(8,128)(2,1)} %get-tuple-element.18.refs_0_), channel_id=1, source_target_pairs={{4,0},{0,4},{12,8},{8,12},{5,1},{1,5},{13,9},{9,13},{6,2},{2,6},{1... | collective-permute-start | bytes 1179656 | tf_op jit(solution)/shard_map/ppermute | solution.py:31
  11.6 3.2 %collective-permute-done.refs_1_ = bf16[128,1536]{1,0:T(8,128)(2,1)S(1)} collective-permute-done((bf16[128,1536]{1,0:T(8,128)(2,1)}, bf16[128,1536]{1,0:T(8,128)(2,1)S(1)}, u32[]{:S(2)}, u32[]{:S(2)}) %collective-permute-start) | collective-permute-done | bytes 393248 | tf_op jit(solution)/shard_map/ppermute | solution.py:31
  14.8 0.7 collective-permute-start.1
  15.5 0.7 collective-permute-start.11
  16.2 2.1 %collective-permute-start.5 = (bf16[4,128,512]{2,1,0:T(8,128)(2,1)S(1)}, bf16[4,128,512]{2,1,0:T(8,128)(2,1)S(1)}, u32[]{:S(2)}, u32[]{:S(2)}) collective-permute-start(bf16[4,128,512]{2,1,0:T(8,128)(2,1)S(1)} %copy-done.1), channel_id=1, source_target_pairs={{0,1},{1,0},{2,3},{3,2},{4,5},{5,4},{6,7},{7,6},{8,9},{9,8},{10,11... | collective-permute-start | bytes 1572872 | tf_op jit(solution)/shard_map/ppermute | solution.py:50
  18.3 1.8 %collective-permute-start.7 = (bf16[4,128,512]{2,1,0:T(8,128)(2,1)S(1)}, bf16[4,128,512]{2,1,0:T(8,128)(2,1)S(1)}, u32[]{:S(2)}, u32[]{:S(2)}) collective-permute-start(bf16[4,128,512]{2,1,0:T(8,128)(2,1)S(1)} %collective-permute-done.6.refs_2_), channel_id=1, source_target_pairs={{0,1},{1,0},{2,3},{3,2},{4,5},{5,4},{6,7},{7,6},{8,9},{9,8},{10,11... | collective-permute-start | bytes 1572872 | tf_op jit(solution)/shard_map/ppermute | solution.py:50
  20.1 3.1 %collective-permute-done.8.refs_1_ = bf16[512,384]{1,0:T(8,128)(2,1)S(1)} collective-permute-done((bf16[512,384]{1,0:T(8,128)(2,1)}, bf16[512,384]{1,0:T(8,128)(2,1)S(1)}, u32[]{:S(2)}, u32[]{:S(2)}) %collective-permute-start.8) | collective-permute-done | bytes 393248 | tf_op jit(solution)/shard_map/ppermute | solution.py:31
  23.2 1.4 %collective-permute-start.4 = (bf16[128,1536]{1,0:T(8,128)(2,1)S(1)}, bf16[128,1536]{1,0:T(8,128)(2,1)S(1)}, u32[]{:S(2)}, u32[]{:S(2)}) collective-permute-start(bf16[128,1536]{1,0:T(8,128)(2,1)S(1)} %collective-permute-done.3.refs_4_), channel_id=1, source_target_pairs={{4,0},{0,4},{12,8},{8,12},{5,1},{1,5},{13,9},{9,13},{6,2},{2,6},{1... | collective-permute-start | bytes 1179656 | tf_op jit(solution)/shard_map/ppermute | solution.py:31
  24.7 2.7 %collective-permute-start.2 = (bf16[128,1536]{1,0:T(8,128)(2,1)S(1)}, bf16[128,1536]{1,0:T(8,128)(2,1)S(1)}, u32[]{:S(2)}, u32[]{:S(2)}) collective-permute-start(bf16[128,1536]{1,0:T(8,128)(2,1)S(1)} %collective-permute-done.1.refs_2_), channel_id=1, source_target_pairs={{4,0},{0,4},{12,8},{8,12},{5,1},{1,5},{13,9},{9,13},{6,2},{2,6},{1... | collective-permute-start | bytes 1179656 | tf_op jit(solution)/shard_map/ppermute | solution.py:31
  27.3 0.7 collective-permute-start.9
  28.0 11.3 %collective-permute-start.12 = (bf16[512,384]{1,0:T(8,128)(2,1)S(1)}, bf16[512,384]{1,0:T(8,128)(2,1)S(1)}, u32[]{:S(2)}, u32[]{:S(2)}) collective-permute-start(bf16[512,384]{1,0:T(8,128)(2,1)S(1)} %collective-permute-done.11.refs_4_), channel_id=1, source_target_pairs={{4,0},{0,4},{12,8},{8,12},{5,1},{1,5},{13,9},{9,13},{6,2},{2,6},{1... | collective-permute-start | bytes 1179656 | tf_op jit(solution)/shard_map/ppermute | solution.py:31
  39.4 0.2 join.1.inverse
  39.6 1.5 %collective-permute-done.2.refs_3_ = bf16[128,1536]{1,0:T(8,128)(2,1)S(1)} collective-permute-done((bf16[128,1536]{1,0:T(8,128)(2,1)S(1)}, bf16[128,1536]{1,0:T(8,128)(2,1)S(1)}, u32[]{:S(2)}, u32[]{:S(2)}) %collective-permute-start.2) | collective-permute-done | bytes 393248 | tf_op jit(solution)/shard_map/ppermute | solution.py:31
  41.0 0.9 %pick.1 = (bf16[128,1536]{1,0:T(8,128)(2,1)S(1)}, bf16[128,1536]{1,0:T(8,128)(2,1)S(1)}) custom-call(s32[4]{0:T(128)S(1)} %copy-done.5, bf16[128,1536]{1,0:T(8,128)(2,1)S(1)} %copy-done.3, bf16[128,1536]{1,0:T(8,128)(2,1)S(1)} %collective-permute-done.refs_1_, bf16[128,1536]{1,0:T(8,128)(2,1)S(1)} %collective-permute-done.1.refs_2_, ...), custom_call_target="tpu_custom_call" | custom-call | tf_op jit(solution)/shard_map/pick/pallas_call | solution.py:134
  42.0 1.0 %collective-permute-start.14 = (bf16[128,1536]{1,0:T(8,128)(2,1)S(1)}, bf16[128,1536]{1,0:T(8,128)(2,1)S(1)}, u32[]{:S(2)}, u32[]{:S(2)}) collective-permute-start(bf16[128,1536]{1,0:T(8,128)(2,1)S(1)} %get-tuple-element.22.refs_0_), channel_id=1, source_target_pairs={{0,2},{1,3},{2,0},{3,1},{4,6},{5,7},{6,4},{7,5},{8,10},{9,11},{10,... | collective-permute-start | bytes 1179656 | tf_op jit(solution)/shard_map/ppermute | solution.py:50
  43.0 2.7 %collective-permute-start.10 = (bf16[512,384]{1,0:T(8,128)(2,1)S(1)}, bf16[512,384]{1,0:T(8,128)(2,1)S(1)}, u32[]{:S(2)}, u32[]{:S(2)}) collective-permute-start(bf16[512,384]{1,0:T(8,128)(2,1)S(1)} %collective-permute-done.9.refs_2_), channel_id=1, source_target_pairs={{4,0},{0,4},{12,8},{8,12},{5,1},{1,5},{13,9},{9,13},{6,2},{2,6},{1... | collective-permute-start | bytes 1179656 | tf_op jit(solution)/shard_map/ppermute | solution.py:31
  45.8 1.4 %mask.1.masked = bf16[640,2048]{1,0:T(8,128)(2,1)S(1)} custom-call(s32[4]{0:T(128)S(1)} %copy-done.5, s32[4]{0:T(128)S(1)} %copy-done.6, s32[5,16]{1,0:T(8,128)S(1)} %copy-done.4, bf16[640,2048]{1,0:T(8,128)(2,1)S(1)} %copy-done), custom_call_target="tpu_custom_call" | custom-call | tf_op jit(solution)/shard_map/mask/pallas_call | solution.py:194
  47.1 3.9 %collective-permute-start.13 = (bf16[128,1536]{1,0:T(8,128)(2,1)S(1)}, bf16[128,1536]{1,0:T(8,128)(2,1)S(1)}, u32[]{:S(2)}, u32[]{:S(2)}) collective-permute-start(bf16[128,1536]{1,0:T(8,128)(2,1)S(1)} %get-tuple-element.22.refs_0_), channel_id=1, source_target_pairs={{0,1},{1,0},{2,3},{3,2},{4,5},{5,4},{6,7},{7,6},{8,9},{9,8},{10,11... | collective-permute-start | bytes 1179656 | tf_op jit(solution)/shard_map/ppermute | solution.py:50
  51.1 2.3 %collective-permute-start.16 = (bf16[128,1536]{1,0:T(8,128)(2,1)S(1)}, bf16[128,1536]{1,0:T(8,128)(2,1)S(1)}, u32[]{:S(2)}, u32[]{:S(2)}) collective-permute-start(bf16[128,1536]{1,0:T(8,128)(2,1)S(1)} %get-tuple-element.25.refs_0_), channel_id=1, source_target_pairs={{0,1},{1,0},{2,3},{3,2},{4,5},{5,4},{6,7},{7,6},{8,9},{9,8},{10,11... | collective-permute-start | bytes 1179656 | tf_op jit(solution)/shard_map/ppermute | solution.py:50
  53.4 0.4 collective-permute-start.15
  53.8 4.1 %collective-permute-done.10.refs_3_ = bf16[512,384]{1,0:T(8,128)(2,1)S(1)} collective-permute-done((bf16[512,384]{1,0:T(8,128)(2,1)S(1)}, bf16[512,384]{1,0:T(8,128)(2,1)S(1)}, u32[]{:S(2)}, u32[]{:S(2)}) %collective-permute-start.10) | collective-permute-done | bytes 393248 | tf_op jit(solution)/shard_map/ppermute | solution.py:31
  57.9 2.3 %first.1 = (bf16[3,512,384]{2,1,0:T(8,128)(2,1)S(1)}, bf16[512,384]{1,0:T(8,128)(2,1)S(1)}, f32[640,384]{1,0:T(8,128)S(1)}) custom-call(s32[4]{0:T(128)S(1)} %copy-done.5, bf16[4,512,512]{2,1,0:T(8,128)(2,1)S(1)} %join.1.inverse, bf16[640,2048]{1,0:T(8,128)(2,1)S(1)} %mask.1.masked, bf16[640,384]{1,0:T(8,128)(2,1)S(1)} %copy-done.2, ...), custom_call_target="tpu_custom_call" | custom-call | flops 60000002048 | tf_op jit(solution)/shard_map/first/pallas_call | solution.py:226
  60.2 1.5 %collective-permute-done.17.refs_2_ = bf16[128,1536]{1,0:T(8,128)(2,1)S(1)} collective-permute-done((bf16[128,1536]{1,0:T(8,128)(2,1)S(1)}, bf16[128,1536]{1,0:T(8,128)(2,1)S(1)}, u32[]{:S(2)}, u32[]{:S(2)}) %collective-permute-start.17) | collective-permute-done | bytes 393248 | tf_op jit(solution)/shard_map/ppermute | solution.py:50
  61.8 0.8 %collective-permute-start.18 = (bf16[128,1536]{1,0:T(8,128)(2,1)S(1)}, bf16[128,1536]{1,0:T(8,128)(2,1)S(1)}, u32[]{:S(2)}, u32[]{:S(2)}) collective-permute-start(bf16[128,1536]{1,0:T(8,128)(2,1)S(1)} %collective-permute-done.17.refs_2_), channel_id=1, source_target_pairs={{0,1},{1,0},{2,3},{3,2},{4,5},{5,4},{6,7},{7,6},{8,9},{9,8},{10,11... | collective-permute-start | bytes 1179656 | tf_op jit(solution)/shard_map/ppermute | solution.py:50
  62.6 2.8 %middle.1 = (bf16[1024,384]{1,0:T(8,128)(2,1)S(1)}, f32[640,384]{1,0:T(8,128)S(1)}) custom-call(bf16[4,512,512]{2,1,0:T(8,128)(2,1)S(1)} %join.1.inverse, bf16[640,2048]{1,0:T(8,128)(2,1)S(1)} %mask.1.masked, bf16[3,512,384]{2,1,0:T(8,128)(2,1)S(1)} %get-tuple-element.19.segments, bf16[512,384]{1,0:T(8,128)(2,1)S(1)} %get-tuple-element.20.start, ...), custom_call_target="tpu_custom_call" | custom-call | flops 24000000000 | tf_op jit(solution)/shard_map/middle/pallas_call | solution.py:277
  65.4 3.1 %last.1 = (bf16[512,384]{1,0:T(8,128)(2,1)}, bf16[640,384]{1,0:T(8,128)(2,1)}) custom-call(bf16[4,512,512]{2,1,0:T(8,128)(2,1)S(1)} %join.1.inverse, bf16[640,2048]{1,0:T(8,128)(2,1)S(1)} %mask.1.masked, bf16[3,512,384]{2,1,0:T(8,128)(2,1)S(1)} %get-tuple-element.19.segments, bf16[512,384]{1,0:T(8,128)(2,1)S(1)} %get-tuple-element.20.start, ...), custom_call_target="tpu_custom_call" | custom-call | tf_op jit(solution)/shard_map/last/pallas_call | solution.py:334
  (29 shorter events, 0.1 us)
Async XLA Ops:
  0.6 5.1 %copy-start.1 = (bf16[4,128,512]{2,1,0:T(8,128)(2,1)S(1)}, bf16[4,128,512]{2,1,0:T(8,128)(2,1)}, u32[]{:S(2)}) copy-start(bf16[4,128,512]{2,1,0:T(8,128)(2,1)} %refs_0_.1) | copy-start | bytes 1572868
  3.5 37.5 %copy-start.3 = (bf16[128,1536]{1,0:T(8,128)(2,1)S(1)}, bf16[128,1536]{1,0:T(8,128)(2,1)}, u32[]{:S(2)}) copy-start(bf16[128,1536]{1,0:T(8,128)(2,1)} %get-tuple-element.14.refs_0_) | copy-start | bytes 1179652
  3.6 37.5 %copy-start.5 = (s32[4]{0:T(128)S(1)}, s32[4]{0:T(128)}, u32[]{:S(2)}) copy-start(s32[4]{0:T(128)} %owners.7) | copy-start | bytes 52
  3.6 11.2 %collective-permute-start = (bf16[128,1536]{1,0:T(8,128)(2,1)}, bf16[128,1536]{1,0:T(8,128)(2,1)S(1)}, u32[]{:S(2)}, u32[]{:S(2)}) collective-permute-start(bf16[128,1536]{1,0:T(8,128)(2,1)} %get-tuple-element.14.refs_0_), channel_id=1, source_target_pairs={{4,0},{0,4},{12,8},{8,12},{5,1},{1,5},{13,9},{9,13},{6,2},{2,6},{1... | collective-permute-start | bytes 1179656 | tf_op jit(solution)/shard_map/ppermute | solution.py:31
  5.8 12.6 %collective-permute-start.6 = (bf16[4,128,512]{2,1,0:T(8,128)(2,1)S(1)}, bf16[4,128,512]{2,1,0:T(8,128)(2,1)S(1)}, u32[]{:S(2)}, u32[]{:S(2)}) collective-permute-start(bf16[4,128,512]{2,1,0:T(8,128)(2,1)S(1)} %copy-done.1), channel_id=1, source_target_pairs={{0,2},{1,3},{2,0},{3,1},{4,6},{5,7},{6,4},{7,5},{8,10},{9,11},{10,... | collective-permute-start | bytes 1572872 | tf_op jit(solution)/shard_map/ppermute | solution.py:50
  7.0 9.2 %collective-permute-start.3 = (bf16[128,1536]{1,0:T(8,128)(2,1)}, bf16[128,1536]{1,0:T(8,128)(2,1)S(1)}, u32[]{:S(2)}, u32[]{:S(2)}) collective-permute-start(bf16[128,1536]{1,0:T(8,128)(2,1)} %get-tuple-element.14.refs_0_), channel_id=1, source_target_pairs={{8,4},{4,8},{9,5},{5,9},{10,6},{6,10},{11,7},{7,11},{24,20},{20,24... | collective-permute-start | bytes 1179656 | tf_op jit(solution)/shard_map/ppermute | solution.py:31
  7.7 38.1 %copy-start = (bf16[640,2048]{1,0:T(8,128)(2,1)S(1)}, bf16[640,2048]{1,0:T(8,128)(2,1)}, u32[]{:S(2)}) copy-start(bf16[640,2048]{1,0:T(8,128)(2,1)} %factor.3) | copy-start | bytes 7864324
  7.7 38.1 %copy-start.4 = (s32[5,16]{1,0:T(8,128)S(1)}, s32[5,16]{1,0:T(8,128)}, u32[]{:S(2)}) copy-start(s32[5,16]{1,0:T(8,128)} %pattern.3) | copy-start | bytes 964
  7.7 38.1 %copy-start.6 = (s32[4]{0:T(128)S(1)}, s32[4]{0:T(128)}, u32[]{:S(2)}) copy-start(s32[4]{0:T(128)} %offsets.3) | copy-start | bytes 52
  7.7 15.5 %collective-permute-start.8 = (bf16[512,384]{1,0:T(8,128)(2,1)}, bf16[512,384]{1,0:T(8,128)(2,1)S(1)}, u32[]{:S(2)}, u32[]{:S(2)}) collective-permute-start(bf16[512,384]{1,0:T(8,128)(2,1)} %get-tuple-element.18.refs_0_), channel_id=1, source_target_pairs={{4,0},{0,4},{12,8},{8,12},{5,1},{1,5},{13,9},{9,13},{6,2},{2,6},{1... | collective-permute-start | bytes 1179656 | tf_op jit(solution)/shard_map/ppermute | solution.py:31
  14.8 9.9 %collective-permute-start.1 = (bf16[128,1536]{1,0:T(8,128)(2,1)S(1)}, bf16[128,1536]{1,0:T(8,128)(2,1)S(1)}, u32[]{:S(2)}, u32[]{:S(2)}) collective-permute-start(bf16[128,1536]{1,0:T(8,128)(2,1)S(1)} %collective-permute-done.refs_1_), channel_id=1, source_target_pairs={{8,4},{4,8},{9,5},{5,9},{10,6},{6,10},{11,7},{7,11},{24,20},{20,24... | collective-permute-start | bytes 1179656 | tf_op jit(solution)/shard_map/ppermute | solution.py:31
  15.5 11.9 %collective-permute-start.11 = (bf16[512,384]{1,0:T(8,128)(2,1)}, bf16[512,384]{1,0:T(8,128)(2,1)S(1)}, u32[]{:S(2)}, u32[]{:S(2)}) collective-permute-start(bf16[512,384]{1,0:T(8,128)(2,1)} %get-tuple-element.18.refs_0_), channel_id=1, source_target_pairs={{8,4},{4,8},{9,5},{5,9},{10,6},{6,10},{11,7},{7,11},{24,20},{20,24... | collective-permute-start | bytes 1179656 | tf_op jit(solution)/shard_map/ppermute | solution.py:31
  16.2 11.8 %collective-permute-start.5 = (bf16[4,128,512]{2,1,0:T(8,128)(2,1)S(1)}, bf16[4,128,512]{2,1,0:T(8,128)(2,1)S(1)}, u32[]{:S(2)}, u32[]{:S(2)}) collective-permute-start(bf16[4,128,512]{2,1,0:T(8,128)(2,1)S(1)} %copy-done.1), channel_id=1, source_target_pairs={{0,1},{1,0},{2,3},{3,2},{4,5},{5,4},{6,7},{7,6},{8,9},{9,8},{10,11... | collective-permute-start | bytes 1572872 | tf_op jit(solution)/shard_map/ppermute | solution.py:50
  18.3 21.0 %collective-permute-start.7 = (bf16[4,128,512]{2,1,0:T(8,128)(2,1)S(1)}, bf16[4,128,512]{2,1,0:T(8,128)(2,1)S(1)}, u32[]{:S(2)}, u32[]{:S(2)}) collective-permute-start(bf16[4,128,512]{2,1,0:T(8,128)(2,1)S(1)} %collective-permute-done.6.refs_2_), channel_id=1, source_target_pairs={{0,1},{1,0},{2,3},{3,2},{4,5},{5,4},{6,7},{7,6},{8,9},{9,8},{10,11... | collective-permute-start | bytes 1572872 | tf_op jit(solution)/shard_map/ppermute | solution.py:50
  23.2 16.3 %collective-permute-start.4 = (bf16[128,1536]{1,0:T(8,128)(2,1)S(1)}, bf16[128,1536]{1,0:T(8,128)(2,1)S(1)}, u32[]{:S(2)}, u32[]{:S(2)}) collective-permute-start(bf16[128,1536]{1,0:T(8,128)(2,1)S(1)} %collective-permute-done.3.refs_4_), channel_id=1, source_target_pairs={{4,0},{0,4},{12,8},{8,12},{5,1},{1,5},{13,9},{9,13},{6,2},{2,6},{1... | collective-permute-start | bytes 1179656 | tf_op jit(solution)/shard_map/ppermute | solution.py:31
  24.7 16.4 %collective-permute-start.2 = (bf16[128,1536]{1,0:T(8,128)(2,1)S(1)}, bf16[128,1536]{1,0:T(8,128)(2,1)S(1)}, u32[]{:S(2)}, u32[]{:S(2)}) collective-permute-start(bf16[128,1536]{1,0:T(8,128)(2,1)S(1)} %collective-permute-done.1.refs_2_), channel_id=1, source_target_pairs={{4,0},{0,4},{12,8},{8,12},{5,1},{1,5},{13,9},{9,13},{6,2},{2,6},{1... | collective-permute-start | bytes 1179656 | tf_op jit(solution)/shard_map/ppermute | solution.py:31
  27.3 15.7 %collective-permute-start.9 = (bf16[512,384]{1,0:T(8,128)(2,1)S(1)}, bf16[512,384]{1,0:T(8,128)(2,1)S(1)}, u32[]{:S(2)}, u32[]{:S(2)}) collective-permute-start(bf16[512,384]{1,0:T(8,128)(2,1)S(1)} %collective-permute-done.8.refs_1_), channel_id=1, source_target_pairs={{8,4},{4,8},{9,5},{5,9},{10,6},{6,10},{11,7},{7,11},{24,20},{20,24... | collective-permute-start | bytes 1179656 | tf_op jit(solution)/shard_map/ppermute | solution.py:31
  28.0 23.1 %collective-permute-start.12 = (bf16[512,384]{1,0:T(8,128)(2,1)S(1)}, bf16[512,384]{1,0:T(8,128)(2,1)S(1)}, u32[]{:S(2)}, u32[]{:S(2)}) collective-permute-start(bf16[512,384]{1,0:T(8,128)(2,1)S(1)} %collective-permute-done.11.refs_4_), channel_id=1, source_target_pairs={{4,0},{0,4},{12,8},{8,12},{5,1},{1,5},{13,9},{9,13},{6,2},{2,6},{1... | collective-permute-start | bytes 1179656 | tf_op jit(solution)/shard_map/ppermute | solution.py:31
  42.0 15.9 %copy-start.2 = (bf16[640,384]{1,0:T(8,128)(2,1)S(1)}, bf16[640,384]{1,0:T(8,128)(2,1)}, u32[]{:S(2)}) copy-start(bf16[640,384]{1,0:T(8,128)(2,1)} %right.3) | copy-start | bytes 1474564
  42.0 15.9 %copy-start.7 = (bf16[512,384]{1,0:T(8,128)(2,1)S(1)}, bf16[512,384]{1,0:T(8,128)(2,1)}, u32[]{:S(2)}) copy-start(bf16[512,384]{1,0:T(8,128)(2,1)} %get-tuple-element.18.refs_0_) | copy-start | bytes 1179652
  42.0 11.4 %collective-permute-start.14 = (bf16[128,1536]{1,0:T(8,128)(2,1)S(1)}, bf16[128,1536]{1,0:T(8,128)(2,1)S(1)}, u32[]{:S(2)}, u32[]{:S(2)}) collective-permute-start(bf16[128,1536]{1,0:T(8,128)(2,1)S(1)} %get-tuple-element.22.refs_0_), channel_id=1, source_target_pairs={{0,2},{1,3},{2,0},{3,1},{4,6},{5,7},{6,4},{7,5},{8,10},{9,11},{10,... | collective-permute-start | bytes 1179656 | tf_op jit(solution)/shard_map/ppermute | solution.py:50
  43.0 14.9 %collective-permute-start.10 = (bf16[512,384]{1,0:T(8,128)(2,1)S(1)}, bf16[512,384]{1,0:T(8,128)(2,1)S(1)}, u32[]{:S(2)}, u32[]{:S(2)}) collective-permute-start(bf16[512,384]{1,0:T(8,128)(2,1)S(1)} %collective-permute-done.9.refs_2_), channel_id=1, source_target_pairs={{4,0},{0,4},{12,8},{8,12},{5,1},{1,5},{13,9},{9,13},{6,2},{2,6},{1... | collective-permute-start | bytes 1179656 | tf_op jit(solution)/shard_map/ppermute | solution.py:31
  47.1 15.5 %collective-permute-start.13 = (bf16[128,1536]{1,0:T(8,128)(2,1)S(1)}, bf16[128,1536]{1,0:T(8,128)(2,1)S(1)}, u32[]{:S(2)}, u32[]{:S(2)}) collective-permute-start(bf16[128,1536]{1,0:T(8,128)(2,1)S(1)} %get-tuple-element.22.refs_0_), channel_id=1, source_target_pairs={{0,1},{1,0},{2,3},{3,2},{4,5},{5,4},{6,7},{7,6},{8,9},{9,8},{10,11... | collective-permute-start | bytes 1179656 | tf_op jit(solution)/shard_map/ppermute | solution.py:50
  51.1 10.7 %collective-permute-start.17 = (bf16[128,1536]{1,0:T(8,128)(2,1)S(1)}, bf16[128,1536]{1,0:T(8,128)(2,1)S(1)}, u32[]{:S(2)}, u32[]{:S(2)}) collective-permute-start(bf16[128,1536]{1,0:T(8,128)(2,1)S(1)} %get-tuple-element.25.refs_0_), channel_id=1, source_target_pairs={{0,2},{1,3},{2,0},{3,1},{4,6},{5,7},{6,4},{7,5},{8,10},{9,11},{10,... | collective-permute-start | bytes 1179656 | tf_op jit(solution)/shard_map/ppermute | solution.py:50
  51.1 14.3 %collective-permute-start.16 = (bf16[128,1536]{1,0:T(8,128)(2,1)S(1)}, bf16[128,1536]{1,0:T(8,128)(2,1)S(1)}, u32[]{:S(2)}, u32[]{:S(2)}) collective-permute-start(bf16[128,1536]{1,0:T(8,128)(2,1)S(1)} %get-tuple-element.25.refs_0_), channel_id=1, source_target_pairs={{0,1},{1,0},{2,3},{3,2},{4,5},{5,4},{6,7},{7,6},{8,9},{9,8},{10,11... | collective-permute-start | bytes 1179656 | tf_op jit(solution)/shard_map/ppermute | solution.py:50
  53.4 9.3 %collective-permute-start.15 = (bf16[128,1536]{1,0:T(8,128)(2,1)S(1)}, bf16[128,1536]{1,0:T(8,128)(2,1)S(1)}, u32[]{:S(2)}, u32[]{:S(2)}) collective-permute-start(bf16[128,1536]{1,0:T(8,128)(2,1)S(1)} %collective-permute-done.14.refs_2_), channel_id=1, source_target_pairs={{0,1},{1,0},{2,3},{3,2},{4,5},{5,4},{6,7},{7,6},{8,9},{9,8},{10,11... | collective-permute-start | bytes 1179656 | tf_op jit(solution)/shard_map/ppermute | solution.py:50
  61.8 3.7 %collective-permute-start.18 = (bf16[128,1536]{1,0:T(8,128)(2,1)S(1)}, bf16[128,1536]{1,0:T(8,128)(2,1)S(1)}, u32[]{:S(2)}, u32[]{:S(2)}) collective-permute-start(bf16[128,1536]{1,0:T(8,128)(2,1)S(1)} %collective-permute-done.17.refs_2_), channel_id=1, source_target_pairs={{0,1},{1,0},{2,3},{3,2},{4,5},{5,4},{6,7},{7,6},{8,9},{9,8},{10,11... | collective-permute-start | bytes 1179656 | tf_op jit(solution)/shard_map/ppermute | solution.py:50

commit v5 on v4

--- a/solution.py
+++ b/solution.py
@@ -76,10 +76,12 @@
     return [next(refs) if there else None for there in held]
 
 
-def stage_kernel(quarter, owners, offsets, pattern, factor, right, piece, segment, rows, sems):
+def stage_kernel(quarter, owners, offsets, pattern, factor, right, piece, segment, sems):
     start = pl.multiple_of(own_start(owners, offsets), BLK)
     first = pl.multiple_of(start + lax.axis_index("src") * quarter, quarter)
-    fetch = pltpu.make_async_copy(factor.at[pl.ds(first, quarter), pl.ds(0, LEFT)], rows, sems.at[0])
+    fetch = pltpu.make_async_copy(
+        factor.at[pl.ds(first, quarter), pl.ds(0, LEFT)], piece, sems.at[0]
+    )
     move = pltpu.make_async_copy(right.at[pl.ds(start, SNR)], segment, sems.at[1])
     fetch.start()
     move.start()
@@ -88,9 +90,11 @@
     for top in range(0, quarter, tall):
         tile_row = (first + top) // BLK
         for col in range(0, LEFT, BLK):
-            tile = rows[top : top + tall, col : col + BLK]
-            kept = jnp.where(pattern[tile_row, col // BLK] > 0, tile, jnp.zeros_like(tile))
-            piece[top : top + tall, col : col + BLK] = kept
+
+            @pl.when(pattern[tile_row, col // BLK] <= 0)
+            def _(top=top, col=col):
+                piece[top : top + tall, col : col + BLK] = jnp.zeros((tall, BLK), piece.dtype)
+
     move.wait()
 
 
@@ -102,10 +106,7 @@
         out_shape=[jax.ShapeDtypeStruct(shape, jnp.bfloat16) for shape in shapes],
         in_specs=[SMEM] * 3 + [ANY] * 2,
         out_specs=[VMEM, VMEM],
-        scratch_shapes=[
-            pltpu.VMEM((quarter, LEFT), jnp.bfloat16),
-            pltpu.SemaphoreType.DMA((2,)),
-        ],
+        scratch_shapes=[pltpu.SemaphoreType.DMA((2,))],
         compiler_params=pltpu.CompilerParams(vmem_limit_bytes=56 << 20),
         name="stage",
     )(owners, offsets, pattern, factor, right)

time: 68.8 us -> 68.8 us (level)
  no operation moved by 1% of the time
where the time goes in v5:
time: 68.8 us; the launch traced here: 68.6 us
  starting transfers between devices  40.5 us (59%)
  Pallas kernels  13.6 us (20%)
  waiting for transfers between devices  13.5 us (20%)
  between operations  0.83 us (1%)
    ppermute x10, starting transfers between devices, line_gather(): got = lax.ppermute(got, 'row', pairs) if pairs else None  26.9 us
    ppermute x9, starting transfers between devices, src_gather(): lax.ppermute(pieces[distance], 'src', [(i, i ^ bit) for i in range(n)])  13.6 us
    ppermute x10, waiting for transfers between devices, line_gather(): got = lax.ppermute(got, 'row', pairs) if pairs else None  12 us
    pallas_call x1, Pallas kernels, last(): pl.pallas_call(last_kernel, out_shape=(jax.ShapeDtypeStruct((SN * SNR //...  3.15 us
    pallas_call x1, Pallas kernels, stage(): pl.pallas_call(functools.partial(stage_kernel, quarter), out_shape=[jax.S...  2.89 us
    pallas_call x1, Pallas kernels, middle(): pl.pallas_call(middle_kernel, out_shape=(jax.ShapeDtypeStruct(((SN - 2) *...  2.77 us
    pallas_call x1, Pallas kernels, first(): pl.pallas_call(functools.partial(first_kernel, n_row, held), out_shape=(j...  2.34 us
    ppermute x9, waiting for transfers between devices, src_gather(): lax.ppermute(pieces[distance], 'src', [(i, i ^ bit) for i in range(n)])  1.55 us
  transfers between devices with their start and end apart: 19, of which 5 were waited for; matrix products, arithmetic and copies ran while one was open for 0% of the time, Pallas kernels for 11%

profile of v5, /device:TPU:1, one launch (start us, length us, event | category | flops | bytes accessed | tf_op | source)
XLA Modules:
  0.0 68.6 jit_solution(17979736808773826204)
XLA Ops:
  0.6 2.9 %stage.1 = (bf16[128,1536]{1,0:T(8,128)(2,1)}, bf16[512,384]{1,0:T(8,128)(2,1)}) custom-call(s32[4]{0:T(128)} %owners.7, s32[4]{0:T(128)} %offsets.3, s32[5,16]{1,0:T(8,128)} %pattern.3, bf16[640,2048]{1,0:T(8,128)(2,1)} %factor.3, bf16[640,384]{1,0:T(8,128)(2,1)} %right.3), custom_call_target="tpu_custom_call" | custom-call | tf_op jit(solution)/shard_map/stage/pallas_call | solution.py:104
  3.5 0.0 copy-start.3
  3.6 0.0 copy-start.5
  3.6 2.2 %collective-permute-start = (bf16[128,1536]{1,0:T(8,128)(2,1)}, bf16[128,1536]{1,0:T(8,128)(2,1)S(1)}, u32[]{:S(2)}, u32[]{:S(2)}) collective-permute-start(bf16[128,1536]{1,0:T(8,128)(2,1)} %get-tuple-element.14.refs_0_), channel_id=1, source_target_pairs={{4,0},{0,4},{12,8},{8,12},{5,1},{1,5},{13,9},{9,13},{6,2},{2,6},{1... | collective-permute-start | bytes 1179656 | tf_op jit(solution)/shard_map/ppermute | solution.py:31
  5.8 1.2 %collective-permute-start.6 = (bf16[4,128,512]{2,1,0:T(8,128)(2,1)S(1)}, bf16[4,128,512]{2,1,0:T(8,128)(2,1)S(1)}, u32[]{:S(2)}, u32[]{:S(2)}) collective-permute-start(bf16[4,128,512]{2,1,0:T(8,128)(2,1)S(1)} %copy-done.1), channel_id=1, source_target_pairs={{0,2},{1,3},{2,0},{3,1},{4,6},{5,7},{6,4},{7,5},{8,10},{9,11},{10,... | collective-permute-start | bytes 1572872 | tf_op jit(solution)/shard_map/ppermute | solution.py:50
  7.0 0.7 collective-permute-start.3
  7.7 3.9 %collective-permute-start.8 = (bf16[512,384]{1,0:T(8,128)(2,1)}, bf16[512,384]{1,0:T(8,128)(2,1)S(1)}, u32[]{:S(2)}, u32[]{:S(2)}) collective-permute-start(bf16[512,384]{1,0:T(8,128)(2,1)} %get-tuple-element.18.refs_0_), channel_id=1, source_target_pairs={{4,0},{0,4},{12,8},{8,12},{5,1},{1,5},{13,9},{9,13},{6,2},{2,6},{1... | collective-permute-start | bytes 1179656 | tf_op jit(solution)/shard_map/ppermute | solution.py:31
  11.6 3.2 %collective-permute-done.refs_1_ = bf16[128,1536]{1,0:T(8,128)(2,1)S(1)} collective-permute-done((bf16[128,1536]{1,0:T(8,128)(2,1)}, bf16[128,1536]{1,0:T(8,128)(2,1)S(1)}, u32[]{:S(2)}, u32[]{:S(2)}) %collective-permute-start) | collective-permute-done | bytes 393248 | tf_op jit(solution)/shard_map/ppermute | solution.py:31
  14.8 0.7 collective-permute-start.1
  15.5 0.7 %collective-permute-start.11 = (bf16[512,384]{1,0:T(8,128)(2,1)}, bf16[512,384]{1,0:T(8,128)(2,1)S(1)}, u32[]{:S(2)}, u32[]{:S(2)}) collective-permute-start(bf16[512,384]{1,0:T(8,128)(2,1)} %get-tuple-element.18.refs_0_), channel_id=1, source_target_pairs={{8,4},{4,8},{9,5},{5,9},{10,6},{6,10},{11,7},{7,11},{24,20},{20,24... | collective-permute-start | bytes 1179656 | tf_op jit(solution)/shard_map/ppermute | solution.py:31
  16.2 2.1 %collective-permute-start.5 = (bf16[4,128,512]{2,1,0:T(8,128)(2,1)S(1)}, bf16[4,128,512]{2,1,0:T(8,128)(2,1)S(1)}, u32[]{:S(2)}, u32[]{:S(2)}) collective-permute-start(bf16[4,128,512]{2,1,0:T(8,128)(2,1)S(1)} %copy-done.1), channel_id=1, source_target_pairs={{0,1},{1,0},{2,3},{3,2},{4,5},{5,4},{6,7},{7,6},{8,9},{9,8},{10,11... | collective-permute-start | bytes 1572872 | tf_op jit(solution)/shard_map/ppermute | solution.py:50
  18.3 1.8 %collective-permute-start.7 = (bf16[4,128,512]{2,1,0:T(8,128)(2,1)S(1)}, bf16[4,128,512]{2,1,0:T(8,128)(2,1)S(1)}, u32[]{:S(2)}, u32[]{:S(2)}) collective-permute-start(bf16[4,128,512]{2,1,0:T(8,128)(2,1)S(1)} %collective-permute-done.6.refs_2_), channel_id=1, source_target_pairs={{0,1},{1,0},{2,3},{3,2},{4,5},{5,4},{6,7},{7,6},{8,9},{9,8},{10,11... | collective-permute-start | bytes 1572872 | tf_op jit(solution)/shard_map/ppermute | solution.py:50
  20.1 3.1 %collective-permute-done.8.refs_1_ = bf16[512,384]{1,0:T(8,128)(2,1)S(1)} collective-permute-done((bf16[512,384]{1,0:T(8,128)(2,1)}, bf16[512,384]{1,0:T(8,128)(2,1)S(1)}, u32[]{:S(2)}, u32[]{:S(2)}) %collective-permute-start.8) | collective-permute-done | bytes 393248 | tf_op jit(solution)/shard_map/ppermute | solution.py:31
  23.2 1.4 %collective-permute-start.4 = (bf16[128,1536]{1,0:T(8,128)(2,1)S(1)}, bf16[128,1536]{1,0:T(8,128)(2,1)S(1)}, u32[]{:S(2)}, u32[]{:S(2)}) collective-permute-start(bf16[128,1536]{1,0:T(8,128)(2,1)S(1)} %collective-permute-done.3.refs_4_), channel_id=1, source_target_pairs={{4,0},{0,4},{12,8},{8,12},{5,1},{1,5},{13,9},{9,13},{6,2},{2,6},{1... | collective-permute-start | bytes 1179656 | tf_op jit(solution)/shard_map/ppermute | solution.py:31
  24.7 2.7 %collective-permute-start.2 = (bf16[128,1536]{1,0:T(8,128)(2,1)S(1)}, bf16[128,1536]{1,0:T(8,128)(2,1)S(1)}, u32[]{:S(2)}, u32[]{:S(2)}) collective-permute-start(bf16[128,1536]{1,0:T(8,128)(2,1)S(1)} %collective-permute-done.1.refs_2_), channel_id=1, source_target_pairs={{4,0},{0,4},{12,8},{8,12},{5,1},{1,5},{13,9},{9,13},{6,2},{2,6},{1... | collective-permute-start | bytes 1179656 | tf_op jit(solution)/shard_map/ppermute | solution.py:31
  27.3 0.7 collective-permute-start.9
  28.0 11.3 %collective-permute-start.12 = (bf16[512,384]{1,0:T(8,128)(2,1)S(1)}, bf16[512,384]{1,0:T(8,128)(2,1)S(1)}, u32[]{:S(2)}, u32[]{:S(2)}) collective-permute-start(bf16[512,384]{1,0:T(8,128)(2,1)S(1)} %collective-permute-done.11.refs_4_), channel_id=1, source_target_pairs={{4,0},{0,4},{12,8},{8,12},{5,1},{1,5},{13,9},{9,13},{6,2},{2,6},{1... | collective-permute-start | bytes 1179656 | tf_op jit(solution)/shard_map/ppermute | solution.py:31
  39.4 0.2 join.1.inverse
  39.6 1.5 %collective-permute-done.2.refs_3_ = bf16[128,1536]{1,0:T(8,128)(2,1)S(1)} collective-permute-done((bf16[128,1536]{1,0:T(8,128)(2,1)S(1)}, bf16[128,1536]{1,0:T(8,128)(2,1)S(1)}, u32[]{:S(2)}, u32[]{:S(2)}) %collective-permute-start.2) | collective-permute-done | bytes 393248 | tf_op jit(solution)/shard_map/ppermute | solution.py:31
  41.0 0.9 %pick.1 = (bf16[128,1536]{1,0:T(8,128)(2,1)S(1)}, bf16[128,1536]{1,0:T(8,128)(2,1)S(1)}) custom-call(s32[4]{0:T(128)S(1)} %copy-done.5, bf16[128,1536]{1,0:T(8,128)(2,1)S(1)} %copy-done.3, bf16[128,1536]{1,0:T(8,128)(2,1)S(1)} %collective-permute-done.refs_1_, bf16[128,1536]{1,0:T(8,128)(2,1)S(1)} %collective-permute-done.1.refs_2_, ...), custom_call_target="tpu_custom_call" | custom-call | tf_op jit(solution)/shard_map/pick/pallas_call | solution.py:135
  42.0 1.0 %collective-permute-start.14 = (bf16[128,1536]{1,0:T(8,128)(2,1)S(1)}, bf16[128,1536]{1,0:T(8,128)(2,1)S(1)}, u32[]{:S(2)}, u32[]{:S(2)}) collective-permute-start(bf16[128,1536]{1,0:T(8,128)(2,1)S(1)} %get-tuple-element.22.refs_0_), channel_id=1, source_target_pairs={{0,2},{1,3},{2,0},{3,1},{4,6},{5,7},{6,4},{7,5},{8,10},{9,11},{10,... | collective-permute-start | bytes 1179656 | tf_op jit(solution)/shard_map/ppermute | solution.py:50
  43.0 2.7 %collective-permute-start.10 = (bf16[512,384]{1,0:T(8,128)(2,1)S(1)}, bf16[512,384]{1,0:T(8,128)(2,1)S(1)}, u32[]{:S(2)}, u32[]{:S(2)}) collective-permute-start(bf16[512,384]{1,0:T(8,128)(2,1)S(1)} %collective-permute-done.9.refs_2_), channel_id=1, source_target_pairs={{4,0},{0,4},{12,8},{8,12},{5,1},{1,5},{13,9},{9,13},{6,2},{2,6},{1... | collective-permute-start | bytes 1179656 | tf_op jit(solution)/shard_map/ppermute | solution.py:31
  45.8 1.4 %mask.1.masked = bf16[640,2048]{1,0:T(8,128)(2,1)S(1)} custom-call(s32[4]{0:T(128)S(1)} %copy-done.5, s32[4]{0:T(128)S(1)} %copy-done.6, s32[5,16]{1,0:T(8,128)S(1)} %copy-done.4, bf16[640,2048]{1,0:T(8,128)(2,1)S(1)} %copy-done), custom_call_target="tpu_custom_call" | custom-call | tf_op jit(solution)/shard_map/mask/pallas_call | solution.py:195
  47.1 3.9 %collective-permute-start.13 = (bf16[128,1536]{1,0:T(8,128)(2,1)S(1)}, bf16[128,1536]{1,0:T(8,128)(2,1)S(1)}, u32[]{:S(2)}, u32[]{:S(2)}) collective-permute-start(bf16[128,1536]{1,0:T(8,128)(2,1)S(1)} %get-tuple-element.22.refs_0_), channel_id=1, source_target_pairs={{0,1},{1,0},{2,3},{3,2},{4,5},{5,4},{6,7},{7,6},{8,9},{9,8},{10,11... | collective-permute-start | bytes 1179656 | tf_op jit(solution)/shard_map/ppermute | solution.py:50
  51.1 2.3 %collective-permute-start.16 = (bf16[128,1536]{1,0:T(8,128)(2,1)S(1)}, bf16[128,1536]{1,0:T(8,128)(2,1)S(1)}, u32[]{:S(2)}, u32[]{:S(2)}) collective-permute-start(bf16[128,1536]{1,0:T(8,128)(2,1)S(1)} %get-tuple-element.25.refs_0_), channel_id=1, source_target_pairs={{0,1},{1,0},{2,3},{3,2},{4,5},{5,4},{6,7},{7,6},{8,9},{9,8},{10,11... | collective-permute-start | bytes 1179656 | tf_op jit(solution)/shard_map/ppermute | solution.py:50
  53.4 0.4 collective-permute-start.15
  53.8 4.1 %collective-permute-done.10.refs_3_ = bf16[512,384]{1,0:T(8,128)(2,1)S(1)} collective-permute-done((bf16[512,384]{1,0:T(8,128)(2,1)S(1)}, bf16[512,384]{1,0:T(8,128)(2,1)S(1)}, u32[]{:S(2)}, u32[]{:S(2)}) %collective-permute-start.10) | collective-permute-done | bytes 393248 | tf_op jit(solution)/shard_map/ppermute | solution.py:31
  57.9 2.3 %first.1 = (bf16[3,512,384]{2,1,0:T(8,128)(2,1)S(1)}, bf16[512,384]{1,0:T(8,128)(2,1)S(1)}, f32[640,384]{1,0:T(8,128)S(1)}) custom-call(s32[4]{0:T(128)S(1)} %copy-done.5, bf16[4,512,512]{2,1,0:T(8,128)(2,1)S(1)} %join.1.inverse, bf16[640,2048]{1,0:T(8,128)(2,1)S(1)} %mask.1.masked, bf16[640,384]{1,0:T(8,128)(2,1)S(1)} %copy-done.2, ...), custom_call_target="tpu_custom_call" | custom-call | flops 60000002048 | tf_op jit(solution)/shard_map/first/pallas_call | solution.py:227
  60.2 1.5 %collective-permute-done.17.refs_2_ = bf16[128,1536]{1,0:T(8,128)(2,1)S(1)} collective-permute-done((bf16[128,1536]{1,0:T(8,128)(2,1)S(1)}, bf16[128,1536]{1,0:T(8,128)(2,1)S(1)}, u32[]{:S(2)}, u32[]{:S(2)}) %collective-permute-start.17) | collective-permute-done | bytes 393248 | tf_op jit(solution)/shard_map/ppermute | solution.py:50
  61.8 0.8 %collective-permute-start.18 = (bf16[128,1536]{1,0:T(8,128)(2,1)S(1)}, bf16[128,1536]{1,0:T(8,128)(2,1)S(1)}, u32[]{:S(2)}, u32[]{:S(2)}) collective-permute-start(bf16[128,1536]{1,0:T(8,128)(2,1)S(1)} %collective-permute-done.17.refs_2_), channel_id=1, source_target_pairs={{0,1},{1,0},{2,3},{3,2},{4,5},{5,4},{6,7},{7,6},{8,9},{9,8},{10,11... | collective-permute-start | bytes 1179656 | tf_op jit(solution)/shard_map/ppermute | solution.py:50
  62.6 2.8 %middle.1 = (bf16[1024,384]{1,0:T(8,128)(2,1)S(1)}, f32[640,384]{1,0:T(8,128)S(1)}) custom-call(bf16[4,512,512]{2,1,0:T(8,128)(2,1)S(1)} %join.1.inverse, bf16[640,2048]{1,0:T(8,128)(2,1)S(1)} %mask.1.masked, bf16[3,512,384]{2,1,0:T(8,128)(2,1)S(1)} %get-tuple-element.19.segments, bf16[512,384]{1,0:T(8,128)(2,1)S(1)} %get-tuple-element.20.start, ...), custom_call_target="tpu_custom_call" | custom-call | flops 24000000000 | tf_op jit(solution)/shard_map/middle/pallas_call | solution.py:278
  65.4 3.1 %last.1 = (bf16[512,384]{1,0:T(8,128)(2,1)}, bf16[640,384]{1,0:T(8,128)(2,1)}) custom-call(bf16[4,512,512]{2,1,0:T(8,128)(2,1)S(1)} %join.1.inverse, bf16[640,2048]{1,0:T(8,128)(2,1)S(1)} %mask.1.masked, bf16[3,512,384]{2,1,0:T(8,128)(2,1)S(1)} %get-tuple-element.19.segments, bf16[512,384]{1,0:T(8,128)(2,1)S(1)} %get-tuple-element.20.start, ...), custom_call_target="tpu_custom_call" | custom-call | tf_op jit(solution)/shard_map/last/pallas_call | solution.py:335
  (29 shorter events, 0.1 us)
Async XLA Ops:
  0.6 5.1 %copy-start.1 = (bf16[4,128,512]{2,1,0:T(8,128)(2,1)S(1)}, bf16[4,128,512]{2,1,0:T(8,128)(2,1)}, u32[]{:S(2)}) copy-start(bf16[4,128,512]{2,1,0:T(8,128)(2,1)} %refs_0_.1) | copy-start | bytes 1572868
  3.5 37.5 %copy-start.3 = (bf16[128,1536]{1,0:T(8,128)(2,1)S(1)}, bf16[128,1536]{1,0:T(8,128)(2,1)}, u32[]{:S(2)}) copy-start(bf16[128,1536]{1,0:T(8,128)(2,1)} %get-tuple-element.14.refs_0_) | copy-start | bytes 1179652
  3.6 37.5 %copy-start.5 = (s32[4]{0:T(128)S(1)}, s32[4]{0:T(128)}, u32[]{:S(2)}) copy-start(s32[4]{0:T(128)} %owners.7) | copy-start | bytes 52
  3.6 11.2 %collective-permute-start = (bf16[128,1536]{1,0:T(8,128)(2,1)}, bf16[128,1536]{1,0:T(8,128)(2,1)S(1)}, u32[]{:S(2)}, u32[]{:S(2)}) collective-permute-start(bf16[128,1536]{1,0:T(8,128)(2,1)} %get-tuple-element.14.refs_0_), channel_id=1, source_target_pairs={{4,0},{0,4},{12,8},{8,12},{5,1},{1,5},{13,9},{9,13},{6,2},{2,6},{1... | collective-permute-start | bytes 1179656 | tf_op jit(solution)/shard_map/ppermute | solution.py:31
  5.8 12.6 %collective-permute-start.6 = (bf16[4,128,512]{2,1,0:T(8,128)(2,1)S(1)}, bf16[4,128,512]{2,1,0:T(8,128)(2,1)S(1)}, u32[]{:S(2)}, u32[]{:S(2)}) collective-permute-start(bf16[4,128,512]{2,1,0:T(8,128)(2,1)S(1)} %copy-done.1), channel_id=1, source_target_pairs={{0,2},{1,3},{2,0},{3,1},{4,6},{5,7},{6,4},{7,5},{8,10},{9,11},{10,... | collective-permute-start | bytes 1572872 | tf_op jit(solution)/shard_map/ppermute | solution.py:50
  7.0 9.2 %collective-permute-start.3 = (bf16[128,1536]{1,0:T(8,128)(2,1)}, bf16[128,1536]{1,0:T(8,128)(2,1)S(1)}, u32[]{:S(2)}, u32[]{:S(2)}) collective-permute-start(bf16[128,1536]{1,0:T(8,128)(2,1)} %get-tuple-element.14.refs_0_), channel_id=1, source_target_pairs={{8,4},{4,8},{9,5},{5,9},{10,6},{6,10},{11,7},{7,11},{24,20},{20,24... | collective-permute-start | bytes 1179656 | tf_op jit(solution)/shard_map/ppermute | solution.py:31
  7.7 38.1 %copy-start = (bf16[640,2048]{1,0:T(8,128)(2,1)S(1)}, bf16[640,2048]{1,0:T(8,128)(2,1)}, u32[]{:S(2)}) copy-start(bf16[640,2048]{1,0:T(8,128)(2,1)} %factor.3) | copy-start | bytes 7864324
  7.7 38.1 %copy-start.4 = (s32[5,16]{1,0:T(8,128)S(1)}, s32[5,16]{1,0:T(8,128)}, u32[]{:S(2)}) copy-start(s32[5,16]{1,0:T(8,128)} %pattern.3) | copy-start | bytes 964
  7.7 38.1 %copy-start.6 = (s32[4]{0:T(128)S(1)}, s32[4]{0:T(128)}, u32[]{:S(2)}) copy-start(s32[4]{0:T(128)} %offsets.3) | copy-start | bytes 52
  7.7 15.5 %collective-permute-start.8 = (bf16[512,384]{1,0:T(8,128)(2,1)}, bf16[512,384]{1,0:T(8,128)(2,1)S(1)}, u32[]{:S(2)}, u32[]{:S(2)}) collective-permute-start(bf16[512,384]{1,0:T(8,128)(2,1)} %get-tuple-element.18.refs_0_), channel_id=1, source_target_pairs={{4,0},{0,4},{12,8},{8,12},{5,1},{1,5},{13,9},{9,13},{6,2},{2,6},{1... | collective-permute-start | bytes 1179656 | tf_op jit(solution)/shard_map/ppermute | solution.py:31
  14.8 9.9 %collective-permute-start.1 = (bf16[128,1536]{1,0:T(8,128)(2,1)S(1)}, bf16[128,1536]{1,0:T(8,128)(2,1)S(1)}, u32[]{:S(2)}, u32[]{:S(2)}) collective-permute-start(bf16[128,1536]{1,0:T(8,128)(2,1)S(1)} %collective-permute-done.refs_1_), channel_id=1, source_target_pairs={{8,4},{4,8},{9,5},{5,9},{10,6},{6,10},{11,7},{7,11},{24,20},{20,24... | collective-permute-start | bytes 1179656 | tf_op jit(solution)/shard_map/ppermute | solution.py:31
  15.5 11.9 %collective-permute-start.11 = (bf16[512,384]{1,0:T(8,128)(2,1)}, bf16[512,384]{1,0:T(8,128)(2,1)S(1)}, u32[]{:S(2)}, u32[]{:S(2)}) collective-permute-start(bf16[512,384]{1,0:T(8,128)(2,1)} %get-tuple-element.18.refs_0_), channel_id=1, source_target_pairs={{8,4},{4,8},{9,5},{5,9},{10,6},{6,10},{11,7},{7,11},{24,20},{20,24... | collective-permute-start | bytes 1179656 | tf_op jit(solution)/shard_map/ppermute | solution.py:31
  16.2 11.8 %collective-permute-start.5 = (bf16[4,128,512]{2,1,0:T(8,128)(2,1)S(1)}, bf16[4,128,512]{2,1,0:T(8,128)(2,1)S(1)}, u32[]{:S(2)}, u32[]{:S(2)}) collective-permute-start(bf16[4,128,512]{2,1,0:T(8,128)(2,1)S(1)} %copy-done.1), channel_id=1, source_target_pairs={{0,1},{1,0},{2,3},{3,2},{4,5},{5,4},{6,7},{7,6},{8,9},{9,8},{10,11... | collective-permute-start | bytes 1572872 | tf_op jit(solution)/shard_map/ppermute | solution.py:50
  18.3 21.0 %collective-permute-start.7 = (bf16[4,128,512]{2,1,0:T(8,128)(2,1)S(1)}, bf16[4,128,512]{2,1,0:T(8,128)(2,1)S(1)}, u32[]{:S(2)}, u32[]{:S(2)}) collective-permute-start(bf16[4,128,512]{2,1,0:T(8,128)(2,1)S(1)} %collective-permute-done.6.refs_2_), channel_id=1, source_target_pairs={{0,1},{1,0},{2,3},{3,2},{4,5},{5,4},{6,7},{7,6},{8,9},{9,8},{10,11... | collective-permute-start | bytes 1572872 | tf_op jit(solution)/shard_map/ppermute | solution.py:50
  23.2 16.3 %collective-permute-start.4 = (bf16[128,1536]{1,0:T(8,128)(2,1)S(1)}, bf16[128,1536]{1,0:T(8,128)(2,1)S(1)}, u32[]{:S(2)}, u32[]{:S(2)}) collective-permute-start(bf16[128,1536]{1,0:T(8,128)(2,1)S(1)} %collective-permute-done.3.refs_4_), channel_id=1, source_target_pairs={{4,0},{0,4},{12,8},{8,12},{5,1},{1,5},{13,9},{9,13},{6,2},{2,6},{1... | collective-permute-start | bytes 1179656 | tf_op jit(solution)/shard_map/ppermute | solution.py:31
  24.7 16.4 %collective-permute-start.2 = (bf16[128,1536]{1,0:T(8,128)(2,1)S(1)}, bf16[128,1536]{1,0:T(8,128)(2,1)S(1)}, u32[]{:S(2)}, u32[]{:S(2)}) collective-permute-start(bf16[128,1536]{1,0:T(8,128)(2,1)S(1)} %collective-permute-done.1.refs_2_), channel_id=1, source_target_pairs={{4,0},{0,4},{12,8},{8,12},{5,1},{1,5},{13,9},{9,13},{6,2},{2,6},{1... | collective-permute-start | bytes 1179656 | tf_op jit(solution)/shard_map/ppermute | solution.py:31
  27.3 15.7 %collective-permute-start.9 = (bf16[512,384]{1,0:T(8,128)(2,1)S(1)}, bf16[512,384]{1,0:T(8,128)(2,1)S(1)}, u32[]{:S(2)}, u32[]{:S(2)}) collective-permute-start(bf16[512,384]{1,0:T(8,128)(2,1)S(1)} %collective-permute-done.8.refs_1_), channel_id=1, source_target_pairs={{8,4},{4,8},{9,5},{5,9},{10,6},{6,10},{11,7},{7,11},{24,20},{20,24... | collective-permute-start | bytes 1179656 | tf_op jit(solution)/shard_map/ppermute | solution.py:31
  28.0 23.1 %collective-permute-start.12 = (bf16[512,384]{1,0:T(8,128)(2,1)S(1)}, bf16[512,384]{1,0:T(8,128)(2,1)S(1)}, u32[]{:S(2)}, u32[]{:S(2)}) collective-permute-start(bf16[512,384]{1,0:T(8,128)(2,1)S(1)} %collective-permute-done.11.refs_4_), channel_id=1, source_target_pairs={{4,0},{0,4},{12,8},{8,12},{5,1},{1,5},{13,9},{9,13},{6,2},{2,6},{1... | collective-permute-start | bytes 1179656 | tf_op jit(solution)/shard_map/ppermute | solution.py:31
  42.0 15.9 %copy-start.2 = (bf16[640,384]{1,0:T(8,128)(2,1)S(1)}, bf16[640,384]{1,0:T(8,128)(2,1)}, u32[]{:S(2)}) copy-start(bf16[640,384]{1,0:T(8,128)(2,1)} %right.3) | copy-start | bytes 1474564
  42.0 15.9 %copy-start.7 = (bf16[512,384]{1,0:T(8,128)(2,1)S(1)}, bf16[512,384]{1,0:T(8,128)(2,1)}, u32[]{:S(2)}) copy-start(bf16[512,384]{1,0:T(8,128)(2,1)} %get-tuple-element.18.refs_0_) | copy-start | bytes 1179652
  42.0 11.4 %collective-permute-start.14 = (bf16[128,1536]{1,0:T(8,128)(2,1)S(1)}, bf16[128,1536]{1,0:T(8,128)(2,1)S(1)}, u32[]{:S(2)}, u32[]{:S(2)}) collective-permute-start(bf16[128,1536]{1,0:T(8,128)(2,1)S(1)} %get-tuple-element.22.refs_0_), channel_id=1, source_target_pairs={{0,2},{1,3},{2,0},{3,1},{4,6},{5,7},{6,4},{7,5},{8,10},{9,11},{10,... | collective-permute-start | bytes 1179656 | tf_op jit(solution)/shard_map/ppermute | solution.py:50
  43.0 14.9 %collective-permute-start.10 = (bf16[512,384]{1,0:T(8,128)(2,1)S(1)}, bf16[512,384]{1,0:T(8,128)(2,1)S(1)}, u32[]{:S(2)}, u32[]{:S(2)}) collective-permute-start(bf16[512,384]{1,0:T(8,128)(2,1)S(1)} %collective-permute-done.9.refs_2_), channel_id=1, source_target_pairs={{4,0},{0,4},{12,8},{8,12},{5,1},{1,5},{13,9},{9,13},{6,2},{2,6},{1... | collective-permute-start | bytes 1179656 | tf_op jit(solution)/shard_map/ppermute | solution.py:31
  47.1 15.5 %collective-permute-start.13 = (bf16[128,1536]{1,0:T(8,128)(2,1)S(1)}, bf16[128,1536]{1,0:T(8,128)(2,1)S(1)}, u32[]{:S(2)}, u32[]{:S(2)}) collective-permute-start(bf16[128,1536]{1,0:T(8,128)(2,1)S(1)} %get-tuple-element.22.refs_0_), channel_id=1, source_target_pairs={{0,1},{1,0},{2,3},{3,2},{4,5},{5,4},{6,7},{7,6},{8,9},{9,8},{10,11... | collective-permute-start | bytes 1179656 | tf_op jit(solution)/shard_map/ppermute | solution.py:50
  51.1 10.7 %collective-permute-start.17 = (bf16[128,1536]{1,0:T(8,128)(2,1)S(1)}, bf16[128,1536]{1,0:T(8,128)(2,1)S(1)}, u32[]{:S(2)}, u32[]{:S(2)}) collective-permute-start(bf16[128,1536]{1,0:T(8,128)(2,1)S(1)} %get-tuple-element.25.refs_0_), channel_id=1, source_target_pairs={{0,2},{1,3},{2,0},{3,1},{4,6},{5,7},{6,4},{7,5},{8,10},{9,11},{10,... | collective-permute-start | bytes 1179656 | tf_op jit(solution)/shard_map/ppermute | solution.py:50
  51.1 14.3 %collective-permute-start.16 = (bf16[128,1536]{1,0:T(8,128)(2,1)S(1)}, bf16[128,1536]{1,0:T(8,128)(2,1)S(1)}, u32[]{:S(2)}, u32[]{:S(2)}) collective-permute-start(bf16[128,1536]{1,0:T(8,128)(2,1)S(1)} %get-tuple-element.25.refs_0_), channel_id=1, source_target_pairs={{0,1},{1,0},{2,3},{3,2},{4,5},{5,4},{6,7},{7,6},{8,9},{9,8},{10,11... | collective-permute-start | bytes 1179656 | tf_op jit(solution)/shard_map/ppermute | solution.py:50
  53.4 9.3 %collective-permute-start.15 = (bf16[128,1536]{1,0:T(8,128)(2,1)S(1)}, bf16[128,1536]{1,0:T(8,128)(2,1)S(1)}, u32[]{:S(2)}, u32[]{:S(2)}) collective-permute-start(bf16[128,1536]{1,0:T(8,128)(2,1)S(1)} %collective-permute-done.14.refs_2_), channel_id=1, source_target_pairs={{0,1},{1,0},{2,3},{3,2},{4,5},{5,4},{6,7},{7,6},{8,9},{9,8},{10,11... | collective-permute-start | bytes 1179656 | tf_op jit(solution)/shard_map/ppermute | solution.py:50
  61.8 3.6 %collective-permute-start.18 = (bf16[128,1536]{1,0:T(8,128)(2,1)S(1)}, bf16[128,1536]{1,0:T(8,128)(2,1)S(1)}, u32[]{:S(2)}, u32[]{:S(2)}) collective-permute-start(bf16[128,1536]{1,0:T(8,128)(2,1)S(1)} %collective-permute-done.17.refs_2_), channel_id=1, source_target_pairs={{0,1},{1,0},{2,3},{3,2},{4,5},{5,4},{6,7},{7,6},{8,9},{9,8},{10,11... | collective-permute-start | bytes 1179656 | tf_op jit(solution)/shard_map/ppermute | solution.py:50

commit v6 on v5

--- a/solution.py
+++ b/solution.py
@@ -322,12 +322,15 @@
         xs.at[pl.ds(pl.multiple_of(position * out_rows, out_rows), out_rows)], solved, sems.at[0]
     )
     solved_copy.start()
-    update = jnp.dot(masked[:, last:], x, preferred_element_type=jnp.float32)
-    out[...] = (total[...] - update).astype(jnp.bfloat16)
-    updated_copy = pltpu.make_async_copy(out, updated, sems.at[1])
-    updated_copy.start()
-    solved_copy.wait()
-    updated_copy.wait()
+    half = pl.cdiv(total.shape[0] // 2, BLK) * BLK
+    copies = [solved_copy]
+    for part, rows in enumerate((pl.ds(0, half), pl.ds(half, total.shape[0] - half))):
+        update = jnp.dot(masked[rows, last:], x, preferred_element_type=jnp.float32)
+        out[rows] = (total[rows] - update).astype(jnp.bfloat16)
+        copies.append(pltpu.make_async_copy(out.at[rows], updated.at[rows], sems.at[1 + part]))
+        copies[-1].start()
+    for copy in copies:
+        copy.wait()
 
 
 def last(inverse, far, masked, segments, start, solutions, total, n_row):
@@ -344,7 +347,7 @@
             pltpu.VMEM((SNR, LEFT), jnp.bfloat16),
             pltpu.VMEM((SN * SNR, columns), jnp.bfloat16),
             pltpu.VMEM((rows, columns), jnp.bfloat16),
-            pltpu.SemaphoreType.DMA((2,)),
+            pltpu.SemaphoreType.DMA((3,)),
             pltpu.SemaphoreType.DMA((2, len(far))),
         ],
         compiler_params=PARAMS,

time: 68.8 us -> 68.7 us (level)
  no operation moved by 1% of the time
where the time goes in v6:
time: 68.7 us; the launch traced here: 68.5 us
  starting transfers between devices  40.5 us (59%)
  Pallas kernels  13.6 us (20%)
  waiting for transfers between devices  13.5 us (20%)
  between operations  0.83 us (1%)
    ppermute x10, starting transfers between devices, line_gather(): got = lax.ppermute(got, 'row', pairs) if pairs else None  26.9 us
    ppermute x9, starting transfers between devices, src_gather(): lax.ppermute(pieces[distance], 'src', [(i, i ^ bit) for i in range(n)])  13.6 us
    ppermute x10, waiting for transfers between devices, line_gather(): got = lax.ppermute(got, 'row', pairs) if pairs else None  12 us
    pallas_call x1, Pallas kernels, last(): pl.pallas_call(last_kernel, out_shape=(jax.ShapeDtypeStruct((SN * SNR //...  3.05 us
    pallas_call x1, Pallas kernels, stage(): pl.pallas_call(functools.partial(stage_kernel, quarter), out_shape=[jax.S...  2.89 us
    pallas_call x1, Pallas kernels, middle(): pl.pallas_call(middle_kernel, out_shape=(jax.ShapeDtypeStruct(((SN - 2) *...  2.77 us
    pallas_call x1, Pallas kernels, first(): pl.pallas_call(functools.partial(first_kernel, n_row, held), out_shape=(j...  2.34 us
    ppermute x9, waiting for transfers between devices, src_gather(): lax.ppermute(pieces[distance], 'src', [(i, i ^ bit) for i in range(n)])  1.55 us
  transfers between devices with their start and end apart: 19, of which 5 were waited for; matrix products, arithmetic and copies ran while one was open for 0% of the time, Pallas kernels for 11%

profile of v6, /device:TPU:1, one launch (start us, length us, event | category | flops | bytes accessed | tf_op | source)
XLA Modules:
  0.0 68.5 jit_solution(17954079460936696859)
XLA Ops:
  0.6 2.9 %stage.1 = (bf16[128,1536]{1,0:T(8,128)(2,1)}, bf16[512,384]{1,0:T(8,128)(2,1)}) custom-call(s32[4]{0:T(128)} %owners.7, s32[4]{0:T(128)} %offsets.3, s32[5,16]{1,0:T(8,128)} %pattern.3, bf16[640,2048]{1,0:T(8,128)(2,1)} %factor.3, bf16[640,384]{1,0:T(8,128)(2,1)} %right.3), custom_call_target="tpu_custom_call" | custom-call | tf_op jit(solution)/shard_map/stage/pallas_call | solution.py:104
  3.5 0.0 copy-start.3
  3.6 2.2 %collective-permute-start = (bf16[128,1536]{1,0:T(8,128)(2,1)}, bf16[128,1536]{1,0:T(8,128)(2,1)S(1)}, u32[]{:S(2)}, u32[]{:S(2)}) collective-permute-start(bf16[128,1536]{1,0:T(8,128)(2,1)} %get-tuple-element.14.refs_0_), channel_id=1, source_target_pairs={{4,0},{0,4},{12,8},{8,12},{5,1},{1,5},{13,9},{9,13},{6,2},{2,6},{1... | collective-permute-start | bytes 1179656 | tf_op jit(solution)/shard_map/ppermute | solution.py:31
  5.8 1.2 %collective-permute-start.6 = (bf16[4,128,512]{2,1,0:T(8,128)(2,1)S(1)}, bf16[4,128,512]{2,1,0:T(8,128)(2,1)S(1)}, u32[]{:S(2)}, u32[]{:S(2)}) collective-permute-start(bf16[4,128,512]{2,1,0:T(8,128)(2,1)S(1)} %copy-done.1), channel_id=1, source_target_pairs={{0,2},{1,3},{2,0},{3,1},{4,6},{5,7},{6,4},{7,5},{8,10},{9,11},{10,... | collective-permute-start | bytes 1572872 | tf_op jit(solution)/shard_map/ppermute | solution.py:50
  7.0 0.7 collective-permute-start.3
  7.7 0.0 copy-start
  7.7 3.9 %collective-permute-start.8 = (bf16[512,384]{1,0:T(8,128)(2,1)}, bf16[512,384]{1,0:T(8,128)(2,1)S(1)}, u32[]{:S(2)}, u32[]{:S(2)}) collective-permute-start(bf16[512,384]{1,0:T(8,128)(2,1)} %get-tuple-element.18.refs_0_), channel_id=1, source_target_pairs={{4,0},{0,4},{12,8},{8,12},{5,1},{1,5},{13,9},{9,13},{6,2},{2,6},{1... | collective-permute-start | bytes 1179656 | tf_op jit(solution)/shard_map/ppermute | solution.py:31
  11.6 3.2 %collective-permute-done.refs_1_ = bf16[128,1536]{1,0:T(8,128)(2,1)S(1)} collective-permute-done((bf16[128,1536]{1,0:T(8,128)(2,1)}, bf16[128,1536]{1,0:T(8,128)(2,1)S(1)}, u32[]{:S(2)}, u32[]{:S(2)}) %collective-permute-start) | collective-permute-done | bytes 393248 | tf_op jit(solution)/shard_map/ppermute | solution.py:31
  14.8 0.7 collective-permute-start.1
  15.5 0.7 %collective-permute-start.11 = (bf16[512,384]{1,0:T(8,128)(2,1)}, bf16[512,384]{1,0:T(8,128)(2,1)S(1)}, u32[]{:S(2)}, u32[]{:S(2)}) collective-permute-start(bf16[512,384]{1,0:T(8,128)(2,1)} %get-tuple-element.18.refs_0_), channel_id=1, source_target_pairs={{8,4},{4,8},{9,5},{5,9},{10,6},{6,10},{11,7},{7,11},{24,20},{20,24... | collective-permute-start | bytes 1179656 | tf_op jit(solution)/shard_map/ppermute | solution.py:31
  16.2 2.1 %collective-permute-start.5 = (bf16[4,128,512]{2,1,0:T(8,128)(2,1)S(1)}, bf16[4,128,512]{2,1,0:T(8,128)(2,1)S(1)}, u32[]{:S(2)}, u32[]{:S(2)}) collective-permute-start(bf16[4,128,512]{2,1,0:T(8,128)(2,1)S(1)} %copy-done.1), channel_id=1, source_target_pairs={{0,1},{1,0},{2,3},{3,2},{4,5},{5,4},{6,7},{7,6},{8,9},{9,8},{10,11... | collective-permute-start | bytes 1572872 | tf_op jit(solution)/shard_map/ppermute | solution.py:50
  18.3 1.8 %collective-permute-start.7 = (bf16[4,128,512]{2,1,0:T(8,128)(2,1)S(1)}, bf16[4,128,512]{2,1,0:T(8,128)(2,1)S(1)}, u32[]{:S(2)}, u32[]{:S(2)}) collective-permute-start(bf16[4,128,512]{2,1,0:T(8,128)(2,1)S(1)} %collective-permute-done.6.refs_2_), channel_id=1, source_target_pairs={{0,1},{1,0},{2,3},{3,2},{4,5},{5,4},{6,7},{7,6},{8,9},{9,8},{10,11... | collective-permute-start | bytes 1572872 | tf_op jit(solution)/shard_map/ppermute | solution.py:50
  20.1 3.1 %collective-permute-done.8.refs_1_ = bf16[512,384]{1,0:T(8,128)(2,1)S(1)} collective-permute-done((bf16[512,384]{1,0:T(8,128)(2,1)}, bf16[512,384]{1,0:T(8,128)(2,1)S(1)}, u32[]{:S(2)}, u32[]{:S(2)}) %collective-permute-start.8) | collective-permute-done | bytes 393248 | tf_op jit(solution)/shard_map/ppermute | solution.py:31
  23.2 1.4 %collective-permute-start.4 = (bf16[128,1536]{1,0:T(8,128)(2,1)S(1)}, bf16[128,1536]{1,0:T(8,128)(2,1)S(1)}, u32[]{:S(2)}, u32[]{:S(2)}) collective-permute-start(bf16[128,1536]{1,0:T(8,128)(2,1)S(1)} %collective-permute-done.3.refs_4_), channel_id=1, source_target_pairs={{4,0},{0,4},{12,8},{8,12},{5,1},{1,5},{13,9},{9,13},{6,2},{2,6},{1... | collective-permute-start | bytes 1179656 | tf_op jit(solution)/shard_map/ppermute | solution.py:31
  24.7 2.7 %collective-permute-start.2 = (bf16[128,1536]{1,0:T(8,128)(2,1)S(1)}, bf16[128,1536]{1,0:T(8,128)(2,1)S(1)}, u32[]{:S(2)}, u32[]{:S(2)}) collective-permute-start(bf16[128,1536]{1,0:T(8,128)(2,1)S(1)} %collective-permute-done.1.refs_2_), channel_id=1, source_target_pairs={{4,0},{0,4},{12,8},{8,12},{5,1},{1,5},{13,9},{9,13},{6,2},{2,6},{1... | collective-permute-start | bytes 1179656 | tf_op jit(solution)/shard_map/ppermute | solution.py:31
  27.3 0.7 collective-permute-start.9
  28.0 11.3 %collective-permute-start.12 = (bf16[512,384]{1,0:T(8,128)(2,1)S(1)}, bf16[512,384]{1,0:T(8,128)(2,1)S(1)}, u32[]{:S(2)}, u32[]{:S(2)}) collective-permute-start(bf16[512,384]{1,0:T(8,128)(2,1)S(1)} %collective-permute-done.11.refs_4_), channel_id=1, source_target_pairs={{4,0},{0,4},{12,8},{8,12},{5,1},{1,5},{13,9},{9,13},{6,2},{2,6},{1... | collective-permute-start | bytes 1179656 | tf_op jit(solution)/shard_map/ppermute | solution.py:31
  39.4 0.2 join.1.inverse
  39.6 1.5 %collective-permute-done.2.refs_3_ = bf16[128,1536]{1,0:T(8,128)(2,1)S(1)} collective-permute-done((bf16[128,1536]{1,0:T(8,128)(2,1)S(1)}, bf16[128,1536]{1,0:T(8,128)(2,1)S(1)}, u32[]{:S(2)}, u32[]{:S(2)}) %collective-permute-start.2) | collective-permute-done | bytes 393248 | tf_op jit(solution)/shard_map/ppermute | solution.py:31
  41.0 0.9 %pick.1 = (bf16[128,1536]{1,0:T(8,128)(2,1)S(1)}, bf16[128,1536]{1,0:T(8,128)(2,1)S(1)}) custom-call(s32[4]{0:T(128)S(1)} %copy-done.5, bf16[128,1536]{1,0:T(8,128)(2,1)S(1)} %copy-done.3, bf16[128,1536]{1,0:T(8,128)(2,1)S(1)} %collective-permute-done.refs_1_, bf16[128,1536]{1,0:T(8,128)(2,1)S(1)} %collective-permute-done.1.refs_2_, ...), custom_call_target="tpu_custom_call" | custom-call | tf_op jit(solution)/shard_map/pick/pallas_call | solution.py:135
  42.0 1.0 %collective-permute-start.14 = (bf16[128,1536]{1,0:T(8,128)(2,1)S(1)}, bf16[128,1536]{1,0:T(8,128)(2,1)S(1)}, u32[]{:S(2)}, u32[]{:S(2)}) collective-permute-start(bf16[128,1536]{1,0:T(8,128)(2,1)S(1)} %get-tuple-element.22.refs_0_), channel_id=1, source_target_pairs={{0,2},{1,3},{2,0},{3,1},{4,6},{5,7},{6,4},{7,5},{8,10},{9,11},{10,... | collective-permute-start | bytes 1179656 | tf_op jit(solution)/shard_map/ppermute | solution.py:50
  43.0 2.7 %collective-permute-start.10 = (bf16[512,384]{1,0:T(8,128)(2,1)S(1)}, bf16[512,384]{1,0:T(8,128)(2,1)S(1)}, u32[]{:S(2)}, u32[]{:S(2)}) collective-permute-start(bf16[512,384]{1,0:T(8,128)(2,1)S(1)} %collective-permute-done.9.refs_2_), channel_id=1, source_target_pairs={{4,0},{0,4},{12,8},{8,12},{5,1},{1,5},{13,9},{9,13},{6,2},{2,6},{1... | collective-permute-start | bytes 1179656 | tf_op jit(solution)/shard_map/ppermute | solution.py:31
  45.8 1.4 %mask.1.masked = bf16[640,2048]{1,0:T(8,128)(2,1)S(1)} custom-call(s32[4]{0:T(128)S(1)} %copy-done.5, s32[4]{0:T(128)S(1)} %copy-done.6, s32[5,16]{1,0:T(8,128)S(1)} %copy-done.4, bf16[640,2048]{1,0:T(8,128)(2,1)S(1)} %copy-done), custom_call_target="tpu_custom_call" | custom-call | tf_op jit(solution)/shard_map/mask/pallas_call | solution.py:195
  47.1 3.9 %collective-permute-start.13 = (bf16[128,1536]{1,0:T(8,128)(2,1)S(1)}, bf16[128,1536]{1,0:T(8,128)(2,1)S(1)}, u32[]{:S(2)}, u32[]{:S(2)}) collective-permute-start(bf16[128,1536]{1,0:T(8,128)(2,1)S(1)} %get-tuple-element.22.refs_0_), channel_id=1, source_target_pairs={{0,1},{1,0},{2,3},{3,2},{4,5},{5,4},{6,7},{7,6},{8,9},{9,8},{10,11... | collective-permute-start | bytes 1179656 | tf_op jit(solution)/shard_map/ppermute | solution.py:50
  51.1 2.3 %collective-permute-start.16 = (bf16[128,1536]{1,0:T(8,128)(2,1)S(1)}, bf16[128,1536]{1,0:T(8,128)(2,1)S(1)}, u32[]{:S(2)}, u32[]{:S(2)}) collective-permute-start(bf16[128,1536]{1,0:T(8,128)(2,1)S(1)} %get-tuple-element.25.refs_0_), channel_id=1, source_target_pairs={{0,1},{1,0},{2,3},{3,2},{4,5},{5,4},{6,7},{7,6},{8,9},{9,8},{10,11... | collective-permute-start | bytes 1179656 | tf_op jit(solution)/shard_map/ppermute | solution.py:50
  53.4 0.4 collective-permute-start.15
  53.8 4.1 %collective-permute-done.10.refs_3_ = bf16[512,384]{1,0:T(8,128)(2,1)S(1)} collective-permute-done((bf16[512,384]{1,0:T(8,128)(2,1)S(1)}, bf16[512,384]{1,0:T(8,128)(2,1)S(1)}, u32[]{:S(2)}, u32[]{:S(2)}) %collective-permute-start.10) | collective-permute-done | bytes 393248 | tf_op jit(solution)/shard_map/ppermute | solution.py:31
  57.9 2.3 %first.1 = (bf16[3,512,384]{2,1,0:T(8,128)(2,1)S(1)}, bf16[512,384]{1,0:T(8,128)(2,1)S(1)}, f32[640,384]{1,0:T(8,128)S(1)}) custom-call(s32[4]{0:T(128)S(1)} %copy-done.5, bf16[4,512,512]{2,1,0:T(8,128)(2,1)S(1)} %join.1.inverse, bf16[640,2048]{1,0:T(8,128)(2,1)S(1)} %mask.1.masked, bf16[640,384]{1,0:T(8,128)(2,1)S(1)} %copy-done.2, ...), custom_call_target="tpu_custom_call" | custom-call | flops 60000002048 | tf_op jit(solution)/shard_map/first/pallas_call | solution.py:227
  60.2 1.5 %collective-permute-done.17.refs_2_ = bf16[128,1536]{1,0:T(8,128)(2,1)S(1)} collective-permute-done((bf16[128,1536]{1,0:T(8,128)(2,1)S(1)}, bf16[128,1536]{1,0:T(8,128)(2,1)S(1)}, u32[]{:S(2)}, u32[]{:S(2)}) %collective-permute-start.17) | collective-permute-done | bytes 393248 | tf_op jit(solution)/shard_map/ppermute | solution.py:50
  61.8 0.8 %collective-permute-start.18 = (bf16[128,1536]{1,0:T(8,128)(2,1)S(1)}, bf16[128,1536]{1,0:T(8,128)(2,1)S(1)}, u32[]{:S(2)}, u32[]{:S(2)}) collective-permute-start(bf16[128,1536]{1,0:T(8,128)(2,1)S(1)} %collective-permute-done.17.refs_2_), channel_id=1, source_target_pairs={{0,1},{1,0},{2,3},{3,2},{4,5},{5,4},{6,7},{7,6},{8,9},{9,8},{10,11... | collective-permute-start | bytes 1179656 | tf_op jit(solution)/shard_map/ppermute | solution.py:50
  62.6 2.8 %middle.1 = (bf16[1024,384]{1,0:T(8,128)(2,1)S(1)}, f32[640,384]{1,0:T(8,128)S(1)}) custom-call(bf16[4,512,512]{2,1,0:T(8,128)(2,1)S(1)} %join.1.inverse, bf16[640,2048]{1,0:T(8,128)(2,1)S(1)} %mask.1.masked, bf16[3,512,384]{2,1,0:T(8,128)(2,1)S(1)} %get-tuple-element.19.segments, bf16[512,384]{1,0:T(8,128)(2,1)S(1)} %get-tuple-element.20.start, ...), custom_call_target="tpu_custom_call" | custom-call | flops 24000000000 | tf_op jit(solution)/shard_map/middle/pallas_call | solution.py:278
  65.4 3.1 %last.1 = (bf16[512,384]{1,0:T(8,128)(2,1)}, bf16[640,384]{1,0:T(8,128)(2,1)}) custom-call(bf16[4,512,512]{2,1,0:T(8,128)(2,1)S(1)} %join.1.inverse, bf16[640,2048]{1,0:T(8,128)(2,1)S(1)} %mask.1.masked, bf16[3,512,384]{2,1,0:T(8,128)(2,1)S(1)} %get-tuple-element.19.segments, bf16[512,384]{1,0:T(8,128)(2,1)S(1)} %get-tuple-element.20.start, ...), custom_call_target="tpu_custom_call" | custom-call | tf_op jit(solution)/shard_map/last/pallas_call | solution.py:338
  (29 shorter events, 0.1 us)
Async XLA Ops:
  0.6 5.1 %copy-start.1 = (bf16[4,128,512]{2,1,0:T(8,128)(2,1)S(1)}, bf16[4,128,512]{2,1,0:T(8,128)(2,1)}, u32[]{:S(2)}) copy-start(bf16[4,128,512]{2,1,0:T(8,128)(2,1)} %refs_0_.1) | copy-start | bytes 1572868
  3.5 37.5 %copy-start.3 = (bf16[128,1536]{1,0:T(8,128)(2,1)S(1)}, bf16[128,1536]{1,0:T(8,128)(2,1)}, u32[]{:S(2)}) copy-start(bf16[128,1536]{1,0:T(8,128)(2,1)} %get-tuple-element.14.refs_0_) | copy-start | bytes 1179652
  3.6 37.5 %copy-start.5 = (s32[4]{0:T(128)S(1)}, s32[4]{0:T(128)}, u32[]{:S(2)}) copy-start(s32[4]{0:T(128)} %owners.7) | copy-start | bytes 52
  3.6 11.2 %collective-permute-start = (bf16[128,1536]{1,0:T(8,128)(2,1)}, bf16[128,1536]{1,0:T(8,128)(2,1)S(1)}, u32[]{:S(2)}, u32[]{:S(2)}) collective-permute-start(bf16[128,1536]{1,0:T(8,128)(2,1)} %get-tuple-element.14.refs_0_), channel_id=1, source_target_pairs={{4,0},{0,4},{12,8},{8,12},{5,1},{1,5},{13,9},{9,13},{6,2},{2,6},{1... | collective-permute-start | bytes 1179656 | tf_op jit(solution)/shard_map/ppermute | solution.py:31
  5.8 12.6 %collective-permute-start.6 = (bf16[4,128,512]{2,1,0:T(8,128)(2,1)S(1)}, bf16[4,128,512]{2,1,0:T(8,128)(2,1)S(1)}, u32[]{:S(2)}, u32[]{:S(2)}) collective-permute-start(bf16[4,128,512]{2,1,0:T(8,128)(2,1)S(1)} %copy-done.1), channel_id=1, source_target_pairs={{0,2},{1,3},{2,0},{3,1},{4,6},{5,7},{6,4},{7,5},{8,10},{9,11},{10,... | collective-permute-start | bytes 1572872 | tf_op jit(solution)/shard_map/ppermute | solution.py:50
  7.0 9.2 %collective-permute-start.3 = (bf16[128,1536]{1,0:T(8,128)(2,1)}, bf16[128,1536]{1,0:T(8,128)(2,1)S(1)}, u32[]{:S(2)}, u32[]{:S(2)}) collective-permute-start(bf16[128,1536]{1,0:T(8,128)(2,1)} %get-tuple-element.14.refs_0_), channel_id=1, source_target_pairs={{8,4},{4,8},{9,5},{5,9},{10,6},{6,10},{11,7},{7,11},{24,20},{20,24... | collective-permute-start | bytes 1179656 | tf_op jit(solution)/shard_map/ppermute | solution.py:31
  7.7 38.1 %copy-start = (bf16[640,2048]{1,0:T(8,128)(2,1)S(1)}, bf16[640,2048]{1,0:T(8,128)(2,1)}, u32[]{:S(2)}) copy-start(bf16[640,2048]{1,0:T(8,128)(2,1)} %factor.3) | copy-start | bytes 7864324
  7.7 38.1 %copy-start.4 = (s32[5,16]{1,0:T(8,128)S(1)}, s32[5,16]{1,0:T(8,128)}, u32[]{:S(2)}) copy-start(s32[5,16]{1,0:T(8,128)} %pattern.3) | copy-start | bytes 964
  7.7 38.1 %copy-start.6 = (s32[4]{0:T(128)S(1)}, s32[4]{0:T(128)}, u32[]{:S(2)}) copy-start(s32[4]{0:T(128)} %offsets.3) | copy-start | bytes 52
  7.7 15.5 %collective-permute-start.8 = (bf16[512,384]{1,0:T(8,128)(2,1)}, bf16[512,384]{1,0:T(8,128)(2,1)S(1)}, u32[]{:S(2)}, u32[]{:S(2)}) collective-permute-start(bf16[512,384]{1,0:T(8,128)(2,1)} %get-tuple-element.18.refs_0_), channel_id=1, source_target_pairs={{4,0},{0,4},{12,8},{8,12},{5,1},{1,5},{13,9},{9,13},{6,2},{2,6},{1... | collective-permute-start | bytes 1179656 | tf_op jit(solution)/shard_map/ppermute | solution.py:31
  14.8 9.9 %collective-permute-start.1 = (bf16[128,1536]{1,0:T(8,128)(2,1)S(1)}, bf16[128,1536]{1,0:T(8,128)(2,1)S(1)}, u32[]{:S(2)}, u32[]{:S(2)}) collective-permute-start(bf16[128,1536]{1,0:T(8,128)(2,1)S(1)} %collective-permute-done.refs_1_), channel_id=1, source_target_pairs={{8,4},{4,8},{9,5},{5,9},{10,6},{6,10},{11,7},{7,11},{24,20},{20,24... | collective-permute-start | bytes 1179656 | tf_op jit(solution)/shard_map/ppermute | solution.py:31
  15.5 11.9 %collective-permute-start.11 = (bf16[512,384]{1,0:T(8,128)(2,1)}, bf16[512,384]{1,0:T(8,128)(2,1)S(1)}, u32[]{:S(2)}, u32[]{:S(2)}) collective-permute-start(bf16[512,384]{1,0:T(8,128)(2,1)} %get-tuple-element.18.refs_0_), channel_id=1, source_target_pairs={{8,4},{4,8},{9,5},{5,9},{10,6},{6,10},{11,7},{7,11},{24,20},{20,24... | collective-permute-start | bytes 1179656 | tf_op jit(solution)/shard_map/ppermute | solution.py:31
  16.2 11.8 %collective-permute-start.5 = (bf16[4,128,512]{2,1,0:T(8,128)(2,1)S(1)}, bf16[4,128,512]{2,1,0:T(8,128)(2,1)S(1)}, u32[]{:S(2)}, u32[]{:S(2)}) collective-permute-start(bf16[4,128,512]{2,1,0:T(8,128)(2,1)S(1)} %copy-done.1), channel_id=1, source_target_pairs={{0,1},{1,0},{2,3},{3,2},{4,5},{5,4},{6,7},{7,6},{8,9},{9,8},{10,11... | collective-permute-start | bytes 1572872 | tf_op jit(solution)/shard_map/ppermute | solution.py:50
  18.3 21.0 %collective-permute-start.7 = (bf16[4,128,512]{2,1,0:T(8,128)(2,1)S(1)}, bf16[4,128,512]{2,1,0:T(8,128)(2,1)S(1)}, u32[]{:S(2)}, u32[]{:S(2)}) collective-permute-start(bf16[4,128,512]{2,1,0:T(8,128)(2,1)S(1)} %collective-permute-done.6.refs_2_), channel_id=1, source_target_pairs={{0,1},{1,0},{2,3},{3,2},{4,5},{5,4},{6,7},{7,6},{8,9},{9,8},{10,11... | collective-permute-start | bytes 1572872 | tf_op jit(solution)/shard_map/ppermute | solution.py:50
  23.2 16.3 %collective-permute-start.4 = (bf16[128,1536]{1,0:T(8,128)(2,1)S(1)}, bf16[128,1536]{1,0:T(8,128)(2,1)S(1)}, u32[]{:S(2)}, u32[]{:S(2)}) collective-permute-start(bf16[128,1536]{1,0:T(8,128)(2,1)S(1)} %collective-permute-done.3.refs_4_), channel_id=1, source_target_pairs={{4,0},{0,4},{12,8},{8,12},{5,1},{1,5},{13,9},{9,13},{6,2},{2,6},{1... | collective-permute-start | bytes 1179656 | tf_op jit(solution)/shard_map/ppermute | solution.py:31
  24.7 16.4 %collective-permute-start.2 = (bf16[128,1536]{1,0:T(8,128)(2,1)S(1)}, bf16[128,1536]{1,0:T(8,128)(2,1)S(1)}, u32[]{:S(2)}, u32[]{:S(2)}) collective-permute-start(bf16[128,1536]{1,0:T(8,128)(2,1)S(1)} %collective-permute-done.1.refs_2_), channel_id=1, source_target_pairs={{4,0},{0,4},{12,8},{8,12},{5,1},{1,5},{13,9},{9,13},{6,2},{2,6},{1... | collective-permute-start | bytes 1179656 | tf_op jit(solution)/shard_map/ppermute | solution.py:31
  27.3 15.7 %collective-permute-start.9 = (bf16[512,384]{1,0:T(8,128)(2,1)S(1)}, bf16[512,384]{1,0:T(8,128)(2,1)S(1)}, u32[]{:S(2)}, u32[]{:S(2)}) collective-permute-start(bf16[512,384]{1,0:T(8,128)(2,1)S(1)} %collective-permute-done.8.refs_1_), channel_id=1, source_target_pairs={{8,4},{4,8},{9,5},{5,9},{10,6},{6,10},{11,7},{7,11},{24,20},{20,24... | collective-permute-start | bytes 1179656 | tf_op jit(solution)/shard_map/ppermute | solution.py:31
  28.0 23.1 %collective-permute-start.12 = (bf16[512,384]{1,0:T(8,128)(2,1)S(1)}, bf16[512,384]{1,0:T(8,128)(2,1)S(1)}, u32[]{:S(2)}, u32[]{:S(2)}) collective-permute-start(bf16[512,384]{1,0:T(8,128)(2,1)S(1)} %collective-permute-done.11.refs_4_), channel_id=1, source_target_pairs={{4,0},{0,4},{12,8},{8,12},{5,1},{1,5},{13,9},{9,13},{6,2},{2,6},{1... | collective-permute-start | bytes 1179656 | tf_op jit(solution)/shard_map/ppermute | solution.py:31
  42.0 15.9 %copy-start.2 = (bf16[640,384]{1,0:T(8,128)(2,1)S(1)}, bf16[640,384]{1,0:T(8,128)(2,1)}, u32[]{:S(2)}) copy-start(bf16[640,384]{1,0:T(8,128)(2,1)} %right.3) | copy-start | bytes 1474564
  42.0 15.9 %copy-start.7 = (bf16[512,384]{1,0:T(8,128)(2,1)S(1)}, bf16[512,384]{1,0:T(8,128)(2,1)}, u32[]{:S(2)}) copy-start(bf16[512,384]{1,0:T(8,128)(2,1)} %get-tuple-element.18.refs_0_) | copy-start | bytes 1179652
  42.0 11.4 %collective-permute-start.14 = (bf16[128,1536]{1,0:T(8,128)(2,1)S(1)}, bf16[128,1536]{1,0:T(8,128)(2,1)S(1)}, u32[]{:S(2)}, u32[]{:S(2)}) collective-permute-start(bf16[128,1536]{1,0:T(8,128)(2,1)S(1)} %get-tuple-element.22.refs_0_), channel_id=1, source_target_pairs={{0,2},{1,3},{2,0},{3,1},{4,6},{5,7},{6,4},{7,5},{8,10},{9,11},{10,... | collective-permute-start | bytes 1179656 | tf_op jit(solution)/shard_map/ppermute | solution.py:50
  43.0 14.9 %collective-permute-start.10 = (bf16[512,384]{1,0:T(8,128)(2,1)S(1)}, bf16[512,384]{1,0:T(8,128)(2,1)S(1)}, u32[]{:S(2)}, u32[]{:S(2)}) collective-permute-start(bf16[512,384]{1,0:T(8,128)(2,1)S(1)} %collective-permute-done.9.refs_2_), channel_id=1, source_target_pairs={{4,0},{0,4},{12,8},{8,12},{5,1},{1,5},{13,9},{9,13},{6,2},{2,6},{1... | collective-permute-start | bytes 1179656 | tf_op jit(solution)/shard_map/ppermute | solution.py:31
  47.1 15.5 %collective-permute-start.13 = (bf16[128,1536]{1,0:T(8,128)(2,1)S(1)}, bf16[128,1536]{1,0:T(8,128)(2,1)S(1)}, u32[]{:S(2)}, u32[]{:S(2)}) collective-permute-start(bf16[128,1536]{1,0:T(8,128)(2,1)S(1)} %get-tuple-element.22.refs_0_), channel_id=1, source_target_pairs={{0,1},{1,0},{2,3},{3,2},{4,5},{5,4},{6,7},{7,6},{8,9},{9,8},{10,11... | collective-permute-start | bytes 1179656 | tf_op jit(solution)/shard_map/ppermute | solution.py:50
  51.1 10.7 %collective-permute-start.17 = (bf16[128,1536]{1,0:T(8,128)(2,1)S(1)}, bf16[128,1536]{1,0:T(8,128)(2,1)S(1)}, u32[]{:S(2)}, u32[]{:S(2)}) collective-permute-start(bf16[128,1536]{1,0:T(8,128)(2,1)S(1)} %get-tuple-element.25.refs_0_), channel_id=1, source_target_pairs={{0,2},{1,3},{2,0},{3,1},{4,6},{5,7},{6,4},{7,5},{8,10},{9,11},{10,... | collective-permute-start | bytes 1179656 | tf_op jit(solution)/shard_map/ppermute | solution.py:50
  51.1 14.3 %collective-permute-start.16 = (bf16[128,1536]{1,0:T(8,128)(2,1)S(1)}, bf16[128,1536]{1,0:T(8,128)(2,1)S(1)}, u32[]{:S(2)}, u32[]{:S(2)}) collective-permute-start(bf16[128,1536]{1,0:T(8,128)(2,1)S(1)} %get-tuple-element.25.refs_0_), channel_id=1, source_target_pairs={{0,1},{1,0},{2,3},{3,2},{4,5},{5,4},{6,7},{7,6},{8,9},{9,8},{10,11... | collective-permute-start | bytes 1179656 | tf_op jit(solution)/shard_map/ppermute | solution.py:50
  53.4 9.3 %collective-permute-start.15 = (bf16[128,1536]{1,0:T(8,128)(2,1)S(1)}, bf16[128,1536]{1,0:T(8,128)(2,1)S(1)}, u32[]{:S(2)}, u32[]{:S(2)}) collective-permute-start(bf16[128,1536]{1,0:T(8,128)(2,1)S(1)} %collective-permute-done.14.refs_2_), channel_id=1, source_target_pairs={{0,1},{1,0},{2,3},{3,2},{4,5},{5,4},{6,7},{7,6},{8,9},{9,8},{10,11... | collective-permute-start | bytes 1179656 | tf_op jit(solution)/shard_map/ppermute | solution.py:50
  61.8 3.6 %collective-permute-start.18 = (bf16[128,1536]{1,0:T(8,128)(2,1)S(1)}, bf16[128,1536]{1,0:T(8,128)(2,1)S(1)}, u32[]{:S(2)}, u32[]{:S(2)}) collective-permute-start(bf16[128,1536]{1,0:T(8,128)(2,1)S(1)} %collective-permute-done.17.refs_2_), channel_id=1, source_target_pairs={{0,1},{1,0},{2,3},{3,2},{4,5},{5,4},{6,7},{7,6},{8,9},{9,8},{10,11... | collective-permute-start | bytes 1179656 | tf_op jit(solution)/shard_map/ppermute | solution.py:50
